TPU v7x, 32 devices: a whole 2x2x4 slice. The times are simulated.
32 devices in a mesh: groups: 2 (over y), tiles: 4 (over z), freq: 2 (over x), field: 2 (over core).
Axes of the slice: x: 2, y: 2, z: 4, core: 2. Of those that a mesh axis runs over, the one named last changes fastest.
Arguments:
- fields: bfloat16 [2, 4, 512, 1024], P('field', 'tiles', ('groups', 'freq')), parts along dimension 2, may hold values from -7.5 to 7.5
- slot_tile_ids: int32 [4], replicated, may hold values from 0 to 3, each once
- neighbour_tile_ids: int32 [4, 4], replicated, may hold values from 0 to 3
- neighbour_rotation_code: int32 [4, 4], replicated, may hold values from 0 to 7
- paired_tile_ids: int32 [4, 2], P('tiles'), may hold values from 0 to 3
Outputs:
- csd: float32 [8, 2, 2, 32, 128, 128], P(('groups', 'tiles'), None, None, ('freq', 'field')), parts along dimension 0
There are 2 independent parts, one for each index of `groups`. A program takes and returns all parts, laid end to end along the dimension named above; an argument that names none is the same for every part. Nothing has to cross between parts.
All inputs are finite; a program needn't handle non-finite values.
Results may differ from a plain program's by a relative error of at most 0.0095.
Values may be sent and summed in bfloat16 or wider, within the bound.
No kernel may reach another device: no remote copies, remote signals or barrier semaphores. Data moves between devices by JAX's collectives and lax.ppermute only.
A program may use at most 64 MiB of HBM per device.

v0:
```python
import math

import jax
import jax.numpy as jnp
from jax import lax
from jax.sharding import PartitionSpec as P

SIDE = 32
SEGLEN = 64


diffusion = 0.25


def slot_lookup(slot_tile_ids, tile_ids):
    matches = (slot_tile_ids[None, :] == tile_ids.reshape(-1)[:, None]).astype(jnp.int32)
    positions = jnp.sum(
        matches * jnp.arange(slot_tile_ids.shape[0], dtype=jnp.int32)[None, :], axis=1
    )
    return positions.reshape(tile_ids.shape)


def tile_edges(field, tile_side):
    cell_count = field.shape[-1]
    north = field[..., :tile_side]
    east = field[..., tile_side - 1 :: tile_side]
    south = field[..., cell_count - tile_side :]
    west = field[..., ::tile_side]
    return jnp.stack([north, east, south, west], axis=-3)


def inner_edges(field, tile_side):
    cell_count = field.shape[-1]
    north = field[..., tile_side : 2 * tile_side]
    east = field[..., tile_side - 2 :: tile_side]
    south = field[..., cell_count - 2 * tile_side : cell_count - tile_side]
    west = field[..., 1::tile_side]
    return jnp.stack([north, east, south, west], axis=-3)


def pick_rims(all_edges, near_slots, codes):
    chosen = all_edges[near_slots, codes % 4]
    flipped = chosen[..., ::-1]
    return jnp.where((codes // 4 == 1)[:, :, None, None], flipped, chosen)


def smooth_step(field, rims, tile_side):
    cell_count = field.shape[-1]
    values = field.astype(jnp.float32)
    edge_vals = rims.astype(jnp.float32)
    above_row = jnp.concatenate([edge_vals[:, 0], values[..., : cell_count - tile_side]], axis=-1)
    below_row = jnp.concatenate([values[..., tile_side:], edge_vals[:, 2]], axis=-1)
    column_pos = jnp.arange(cell_count, dtype=jnp.int32) % tile_side
    west_full = jnp.repeat(edge_vals[:, 3], tile_side, axis=-1)
    east_full = jnp.repeat(edge_vals[:, 1], tile_side, axis=-1)
    leftward = jnp.where(column_pos == 0, west_full, jnp.roll(values, 1, axis=-1))
    rightward = jnp.where(column_pos == tile_side - 1, east_full, jnp.roll(values, -1, axis=-1))
    laplace = above_row + below_row + leftward + rightward - 4.0 * values
    return (values + diffusion * laplace).astype(jnp.bfloat16)


def before_along(values, first):
    return jnp.concatenate([first[..., None], values[..., :-1]], axis=-1)


def after_along(values, last):
    return jnp.concatenate([values[..., 1:], last[..., None]], axis=-1)


def smooth_one(values, above, below, leftward, rightward):
    laplace = above + below + leftward + rightward - 4.0 * values
    return (values + diffusion * laplace).astype(jnp.bfloat16)


def edge_sweep(outer, inner, rims):
    outer_vals = outer.astype(jnp.float32)
    inner_vals = inner.astype(jnp.float32)
    rim_vals = rims.astype(jnp.float32)
    north_rim = rim_vals[:, 0]
    east_rim = rim_vals[:, 1]
    south_rim = rim_vals[:, 2]
    west_rim = rim_vals[:, 3]
    north = outer_vals[:, 0]
    east = outer_vals[:, 1]
    south = outer_vals[:, 2]
    west = outer_vals[:, 3]
    new_north = smooth_one(
        north,
        north_rim,
        inner_vals[:, 0],
        before_along(north, west_rim[..., 0]),
        after_along(north, east_rim[..., 0]),
    )
    new_east = smooth_one(
        east,
        before_along(east, north_rim[..., -1]),
        after_along(east, south_rim[..., -1]),
        inner_vals[:, 1],
        east_rim,
    )
    new_south = smooth_one(
        south,
        inner_vals[:, 2],
        south_rim,
        before_along(south, west_rim[..., -1]),
        after_along(south, east_rim[..., -1]),
    )
    new_west = smooth_one(
        west,
        before_along(west, north_rim[..., 0]),
        after_along(west, south_rim[..., 0]),
        west_rim,
        inner_vals[:, 3],
    )
    return jnp.stack([new_north, new_east, new_south, new_west], axis=1)


def coarse_sums(field, tile_side):
    leading = field.shape[:-1]
    blocks = field.astype(jnp.float32).reshape(leading + (tile_side // 2, 2, tile_side // 4, 4))
    return jnp.sum(blocks, axis=(-3, -1)).reshape(leading + (tile_side // 2 * (tile_side // 4),))


def window_table(seg_length):
    samples = jnp.arange(seg_length, dtype=jnp.int32)
    frequency = jnp.arange(seg_length // 2, dtype=jnp.int32)
    products = frequency[:, None] * samples[None, :] % seg_length
    angles = 2.0 * math.pi / seg_length * products.astype(jnp.float32)
    window = 0.5 - 0.5 * jnp.cos(2.0 * math.pi / seg_length * samples.astype(jnp.float32))
    dft_table = jnp.stack([window[None, :] * jnp.cos(angles), -window[None, :] * jnp.sin(angles)])
    return (dft_table, jnp.sum(window * window))


def segment_spectra(coarse, dft_table):
    leading = coarse.shape[0]
    segments = coarse.reshape(leading, -1, dft_table.shape[-1], coarse.shape[-1])
    spectra = jnp.einsum("cft,nstp->nscfp", dft_table, segments, precision=lax.Precision.HIGHEST)
    return spectra.astype(jnp.bfloat16)


def cross_density(height, partner, window_power):
    rotated = jnp.stack([height[:, :, 1], -height[:, :, 0]], axis=2)
    stacked = jnp.stack([height, rotated], axis=1)
    cross = jnp.einsum(
        "noscfi,nkscfj->nkofij", stacked, partner, preferred_element_type=jnp.float32
    )
    return cross / (partner.shape[2] * window_power)


def shards(fields, slot_tile_ids, neighbour_tile_ids, neighbour_rotation_code, paired_tile_ids):
    field = fields[0]
    local_count = field.shape[0]
    first_local = lax.axis_index("tiles") * local_count
    near_all = slot_lookup(slot_tile_ids, neighbour_tile_ids)
    near_local = lax.dynamic_slice_in_dim(near_all, first_local, local_count, 0)
    code_local = lax.dynamic_slice_in_dim(neighbour_rotation_code, first_local, local_count, 0)
    every_outer = lax.all_gather(tile_edges(field, SIDE), "tiles", axis=0, tiled=True)
    every_inner = lax.all_gather(inner_edges(field, SIDE), "tiles", axis=0, tiled=True)
    every_rim = pick_rims(every_outer, near_all, neighbour_rotation_code)
    local_rim = lax.dynamic_slice_in_dim(every_rim, first_local, local_count, 0)
    field = smooth_step(field, local_rim, SIDE)
    new_edges = edge_sweep(every_outer, every_inner, every_rim)
    field = smooth_step(field, pick_rims(new_edges, near_local, code_local), SIDE)
    dft_table, window_power = window_table(SEGLEN)
    spectra = segment_spectra(coarse_sums(field, SIDE), dft_table)
    banded = lax.all_to_all(
        lax.all_to_all(spectra[None], "freq", split_axis=4, concat_axis=2, tiled=True),
        "field",
        split_axis=4,
        concat_axis=0,
        tiled=True,
    )
    partner_slots = slot_lookup(slot_tile_ids, paired_tile_ids)
    every_band = lax.all_gather(banded, "tiles", axis=1, tiled=True)
    first_slot = lax.axis_index("tiles") * banded.shape[1]
    height = lax.dynamic_slice_in_dim(every_band[0], first_slot, banded.shape[1], 0)
    velocity = every_band[1]
    return cross_density(height, velocity[partner_slots], window_power)


def solution(mesh):
    placed = (P("field", "tiles", ("groups", "freq"), None), P(), P(), P(), P("tiles", None))
    return jax.shard_map(
        shards,
        mesh=mesh,
        in_specs=placed,
        out_specs=P(("groups", "tiles"), None, None, ("freq", "field"), None, None),
        check_vma=False,
    )
```

profile of v0, /device:TPU:0, one launch (start us, length us, event | category | flops | bytes accessed | tf_op | source)
XLA Modules:
  0.0 69.6 jit_solution(6394495090829797569)
XLA Ops:
  0.1 0.8 %eq.65 = s32[16]{0:T(128)S(1)} reshape(s32[4,4]{1,0:T(4,128)} %param.7) | data formatting | bytes 128 | tf_op jit(solution)/shard_map/eq | solution.py:16
  0.9 0.7 %select_reduce_fusion = s32[16]{0:T(128)S(1)} fusion(s32[16]{0:T(128)S(1)} %eq.65, s32[4]{0:T(128)} %param.6), kind=kLoop, calls=%fused_computation.163 | loop fusion | flops 176 | bytes 144 | tf_op jit(solution)/shard_map/reduce_sum | solution.py:17
  1.6 0.1 reshape.896
  1.7 0.1 reshape.895
  1.8 0.1 broadcast_compare_fusion
  1.9 1.1 %copy.181 = bf16[1,1,128,1024]{2,3,1,0:T(8,128)(2,1)S(1)} copy(bf16[1,1,128,1024]{3,2,1,0:T(8,128)(2,1)} %param.5) | data formatting | bytes 524288 | tf_op args[0]
  3.0 0.1 slice.203
  3.0 0.1 slice.187
  3.1 0.1 slice.201
  3.2 0.1 slice.185
  3.3 0.0 copy-start
  3.3 1.0 %fusion.83 = (f32[1,128,992]{1,2,0:T(8,128)}, f32[1,128,992]{1,2,0:T(8,128)}) fusion(f32[1,128,1024]{1,2,0:T(8,128)S(1)} %bitcast_convert_fusion), kind=kLoop, calls=%fused_computation.197 | loop fusion | bytes 2031616 | tf_op jit(solution)/shard_map/slice | solution.py:51
  4.3 0.1 fusion.81
  4.4 0.0 copy-done
  4.5 0.1 reshape.901
  4.6 15.1 %all_gather.9 = bf16[4,4,128,32]{2,3,1,0:T(8,128)(2,1)S(1)} all-gather(bf16[1,4,128,32]{2,3,1,0:T(8,128)(2,1)S(1)} %pad_maximum_fusion.5), channel_id=1, replica_groups=mesh['groups'=2,'tiles'=4,'freq'=2,'field'=2] {'tiles'}, dimensions={0}, use_global_device_ids=true | all-gather | bytes 163840 | tf_op jit(solution)/shard_map/all_gather | solution.py:157
  19.7 0.6 gather_fusion
  20.3 0.1 rev.6
  20.3 0.1 fusion.77
  20.5 2.2 %fusion.14 = (f32[1,128,1024]{1,2,0:T(8,128)S(1)}, f32[1,128,1024]{1,2,0:T(8,128)S(1)}, f32[1,128,1024]{1,2,0:T(8,128)S(1)}, f32[1,128,1024]{1,2,0:T(8,128)S(1)}) fusion(f32[128,32]{0,1:T(8,128)S(1)} %get-tuple-element.45, f32[128,32]{0,1:T(8,128)S(1)} %get-tuple-element.44, pred[1024]{0:T(1024)(128)(4,1)S(1)} %get-tuple-element.75, ...), kind=kLoop, calls=%fused_computation.32 | loop fusion | flops 2097152 | bytes 4491264 | tf_op jit(solution)/shard_map/convert_element_type | solution.py:49
  22.7 1.0 %fusion.80 = (f32[1,128,992]{1,2,0:T(8,128)}, f32[1,128,992]{1,2,0:T(8,128)}) fusion(f32[1,128,1024]{1,2,0:T(8,128)S(1)} %get-tuple-element.9), kind=kLoop, calls=%fused_computation.194 | loop fusion | bytes 2031616 | tf_op jit(solution)/shard_map/slice | solution.py:52
  23.7 0.1 fusion.79
  23.8 13.5 %all_gather.10 = bf16[4,4,128,32]{2,3,1,0:T(8,128)(2,1)S(1)} all-gather(bf16[1,4,128,32]{2,3,1,0:T(8,128)(2,1)S(1)} %pad_maximum_fusion.6), channel_id=1, replica_groups=mesh['groups'=2,'tiles'=4,'freq'=2,'field'=2] {'tiles'}, dimensions={0}, use_global_device_ids=true | all-gather | bytes 163840 | tf_op jit(solution)/shard_map/all_gather | solution.py:158
  37.5 0.1 fusion.41
  37.6 0.1 fusion.33
  37.7 0.6 gather_fusion.1
  38.3 0.1 fusion.50
  38.5 1.2 %maximum_add_fusion.1 = f32[1,128,1024]{1,2,0:T(8,128)S(1)} fusion(f32[1,128,992]{1,2,0:T(8,128)} %get-tuple-element.22, f32[1,128,32]{1,2,0:T(8,128)S(1)} %get-tuple-element.52, f32[1,128,32]{1,2,0:T(8,128)S(1)} %get-tuple-element.51, f32[1,128,992]{1,2,0:T(8,128)} %get-tuple-element.21), kind=kLoop, calls=%fused_computation.20 | loop fusion | flops 393216 | bytes 1572864 | tf_op jit(solution)/shard_map/add | solution.py:58
  39.8 0.0 copy-start.1
  39.8 0.0 copy-start.2
  39.8 1.3 %convert_reduce_fusion = f32[128,16,8]{0,2,1:T(8,128)S(1)} fusion(f32[1,128,16,2,8,4]{1,5,4,3,2,0:T(4,128)S(1)} %bitcast.265, f32[128,16,2]{0,2,1:T(2,128)S(1)} %bitcast.274, f32[1,128,16,2,8,4]{1,5,4,3,2,0:T(4,128)S(1)} %bitcast.263, f32[1,128,16,2,8,4]{1,5,4,3,2,0:T(4,128)S(1)} %bitcast.264, f32[128,16,2]{0,2,1:T(2,128)S(1)} %bitcast.273, ...), kind=kLoop, calls=%fused_computation.31 | loop fusion | flops 2867200 | bytes 3540992 | tf_op jit(solution)/shard_map/reduce_sum | solution.py:121
  41.1 0.1 reshape.897
  41.2 0.1 sine_multiply_fusion
  41.3 0.3 fusion.1
  41.6 0.6 copy.200
  42.2 3.3 %all-to-all-start = ((bf16[1,1,2,2,32,128]{5,3,2,1,0,4:T(2,128)(2,1)}), bf16[1,1,2,2,32,128]{5,3,2,1,0,4:T(2,128)(2,1)S(1)}, u32[]{:S(2)}, u32[]{:S(2)}) async-start(bf16[1,1,2,2,32,128]{5,3,2,1,0,4:T(2,128)(2,1)} %copy.200), calls=%async_computation | async-start | bytes 65536 | tf_op jit(solution)/shard_map/all_to_all | solution.py:167
  45.5 0.0 copy-done.1
  45.5 0.0 copy-done.2
  45.5 0.2 fusion.70
  45.7 0.7 multiply_reduce_fusion
  47.0 2.4 %all-to-all-done = bf16[1,1,2,2,32,128]{5,3,2,1,0,4:T(2,128)(2,1)S(1)} async-done(((bf16[1,1,2,2,32,128]{5,3,2,1,0,4:T(2,128)(2,1)}), bf16[1,1,2,2,32,128]{5,3,2,1,0,4:T(2,128)(2,1)S(1)}, u32[]{:S(2)}, u32[]{:S(2)}) %all-to-all-start) | async-done | bytes 32800 | tf_op jit(solution)/shard_map/all_to_all | solution.py:167
  49.5 3.7 %all_to_all.36 = bf16[1,1,4,2,16,128]{5,3,2,1,0,4:T(2,128)(2,1)S(1)} all-to-all(bf16[1,1,4,2,16,128]{5,3,2,1,0,4:T(2,128)(2,1)S(1)} %copy.203), channel_id=1, replica_groups=mesh['groups'=2,'tiles'=4,'freq'=2,'field'=2] {'field'}, dimensions={4} | all-to-all | bytes 65536 | tf_op jit(solution)/shard_map/all_to_all | solution.py:166
  53.2 13.4 %all-gather = bf16[2,4,1,4,2,8,128]{6,5,4,3,1,2,0:T(8,128)(2,1)S(1)} all-gather(bf16[2,1,1,4,2,8,128]{6,5,4,3,1,2,0:T(8,128)(2,1)S(1)} %bitcast.267), channel_id=2, replica_groups=mesh['groups'=2,'tiles'=4,'freq'=2,'field'=2] {'tiles'}, dimensions={1}, use_global_device_ids=true | all-gather | bytes 163840 | tf_op jit(solution)/shard_map/all_gather | solution.py:174
  66.7 0.6 gather_fusion.2
  67.3 0.5 fusion
  67.8 1.8 %copy.209 = f32[1,2,2,8,128,128]{5,4,3,2,1,0:T(8,128)} copy(f32[1,2,2,8,128,128]{4,5,2,1,3,0:T(8,128)S(1)} %fusion) | data formatting | bytes 4194304 | tf_op jit(solution)/shard_map/div | solution.py:147
  (43 shorter events, 0.6 us)
Async XLA Ops:
  3.3 1.1 %copy-start = (s32[4,4]{1,0:T(4,128)S(1)}, s32[4,4]{1,0:T(4,128)}, u32[]{:S(2)}) copy-start(s32[4,4]{1,0:T(4,128)} %param.8) | copy-start | bytes 196
  39.8 5.7 %copy-start.1 = (s32[4]{0:T(128)S(1)}, s32[4]{0:T(128)}, u32[]{:S(2)}) copy-start(s32[4]{0:T(128)} %param.6) | copy-start | bytes 52
  39.8 5.7 %copy-start.2 = (s32[1,2]{1,0:T(1,128)S(1)}, s32[1,2]{1,0:T(1,128)}, u32[]{:S(2)}) copy-start(s32[1,2]{1,0:T(1,128)} %param.9) | copy-start | bytes 28
  42.2 7.2 %all-to-all-start = ((bf16[1,1,2,2,32,128]{5,3,2,1,0,4:T(2,128)(2,1)}), bf16[1,1,2,2,32,128]{5,3,2,1,0,4:T(2,128)(2,1)S(1)}, u32[]{:S(2)}, u32[]{:S(2)}) async-start(bf16[1,1,2,2,32,128]{5,3,2,1,0,4:T(2,128)(2,1)} %copy.200), calls=%async_computation | async-start | bytes 65536 | tf_op jit(solution)/shard_map/all_to_all | solution.py:167
where the time goes:
time: 70 us; the launch traced here: 69.6 us
  blocking collectives  45.8 us (65%)
  local copies, waits for them, and re-layouts  9.18 us (13%)
  other arithmetic  7.23 us (10%)
  starting transfers between devices  3.26 us (5%)
  waiting for transfers between devices  2.42 us (3%)
  between operations  1.03 us (1%)
  matrix products  0.77 us (1%)
    all_gather x1, blocking collectives, shards(): lax.all_gather(tile_edges(field, SIDE), 'tiles', axis=0, tiled=True)  15.1 us
    all_gather x1, blocking collectives, shards(): lax.all_gather(inner_edges(field, SIDE), 'tiles', axis=0, tiled=True)  13.5 us
    all_gather x1, blocking collectives, shards(): every_band = lax.all_gather(banded, 'tiles', axis=1, tiled=True)  13.4 us
    all_to_all x1, blocking collectives, shards(): lax.all_to_all(lax.all_to_all(spectra[None], 'freq', split_axis=4, concat...  3.75 us
    all_to_all x1, starting transfers between devices, shards(): lax.all_to_all(spectra[None], 'freq', split_axis=4, concat_axis=2, tiled=...  3.26 us
    all_to_all x1, waiting for transfers between devices, shards(): lax.all_to_all(spectra[None], 'freq', split_axis=4, concat_axis=2, tiled=...  2.42 us
    convert_element_type x2, other arithmetic, smooth_step(): values = field.astype(jnp.float32)  2.21 us
    div x1, local copies, waits for them, and re-layouts, cross_density(): return cross / (partner.shape[2] * window_power)  1.81 us
  transfers between devices with their start and end apart: 1, of which 1 were waited for; matrix products, arithmetic and copies ran while one was open for 1% of the time, Pallas kernels for 0%

commit v1 on v0

v1 whole, which is shorter than its diff:
```python
import functools
import math

import jax
import jax.numpy as jnp
import ml_dtypes
import numpy as np
from jax import lax
from jax.experimental import pallas as pl
from jax.experimental.pallas import tpu as pltpu
from jax.sharding import PartitionSpec as P

SIDE = 32
SEGLEN = 64
LANES = 128
BLOCKS = SIDE // 2
CORNER_ROWS = 16
FREQS = SEGLEN // 2

NORTH, EAST, SOUTH, WEST = range(4)
EDGE_CORNERS = ((0, 1), (1, 3), (2, 3), (0, 2))
END_RIMS = (
    ((WEST, 0), (EAST, 0)),
    ((NORTH, 1), (SOUTH, 1)),
    ((WEST, 1), (EAST, 1)),
    ((NORTH, 0), (SOUTH, 0)),
)


def split_bf16(values):
    high = values.astype(ml_dtypes.bfloat16)
    low = (values - high.astype(np.float64)).astype(ml_dtypes.bfloat16)
    return high, low


@functools.lru_cache(maxsize=None)
def cell_tables():
    cells = SIDE * SIDE

    def at(row, column):
        return row * SIDE + column

    near = np.zeros((cells, cells))
    pool = np.zeros((cells, LANES))
    for row in range(SIDE):
        for column in range(SIDE):
            pool[at(row, column), (row // 2) * (SIDE // 4) + column // 4] = 1
            for down, right in ((1, 0), (-1, 0), (0, 1), (0, -1)):
                if 0 <= row + down < SIDE and 0 <= column + right < SIDE:
                    near[at(row + down, column + right), at(row, column)] = 1
    last = SIDE - 1
    outer = [[at(0, i), at(i, last), at(last, i), at(i, 0)] for i in range(SIDE)]
    inner = [[at(1, i), at(i, last - 1), at(last - 1, i), at(i, 1)] for i in range(SIDE)]
    carried = np.zeros((cells, 4 * BLOCKS))
    sums = np.zeros((cells, 4 * BLOCKS))
    for edge in range(4):
        for i in range(SIDE):
            block = edge * BLOCKS + i // 2
            sums[outer[i][edge], block] += 1
            carried[outer[i][edge], block] += 1
            carried[inner[i][edge], block] += 1
            if i > 0:
                carried[outer[i - 1][edge], block] += 2
            if i < last:
                carried[outer[i + 1][edge], block] += 2
    cell_map = np.concatenate([near @ near @ pool, carried, sums], axis=1)
    first_corners = np.zeros((CORNER_ROWS, LANES))
    last_corners = np.zeros((CORNER_ROWS, LANES))
    first_corners[0, 0] = 1
    first_corners[1, last] = 1
    last_corners[2, LANES - SIDE] = 1
    last_corners[3, LANES - 1] = 1
    to_bf16 = lambda table: table.astype(ml_dtypes.bfloat16)
    return to_bf16(cell_map), to_bf16(first_corners), to_bf16(last_corners)


@functools.lru_cache(maxsize=None)
def time_tables(bands, samples):
    per_band = FREQS // bands
    segments = samples // SEGLEN
    time = np.arange(SEGLEN)
    frequency = np.arange(FREQS)
    angles = 2.0 * math.pi / SEGLEN * (frequency[:, None] * time[None, :] % SEGLEN)
    window = 0.5 - 0.5 * np.cos(2.0 * math.pi / SEGLEN * time)
    waves = np.stack([window * np.cos(angles), -window * np.sin(angles)]) / 16.0
    table = np.zeros((bands, segments, 2, per_band, segments, SEGLEN))
    for segment in range(segments):
        table[:, segment, :, :, segment, :] = waves.reshape(2, bands, per_band, SEGLEN).transpose(1, 0, 2, 3)
    table = table.reshape(bands * segments * 2 * per_band, samples)
    high, low = split_bf16(table)
    return high, low, np.ascontiguousarray(high.T), np.ascontiguousarray(low.T)


def dot(left, right):
    return jnp.dot(left, right, preferred_element_type=jnp.float32)


def transform_kernel(
    devices, place_ref, x_ref, cells_ref, first_ref, last_ref, high_ref, low_ref, high_t_ref, low_t_ref, *rest
):
    outs, spectra_ref = rest[:devices], rest[devices]
    place = place_ref[0]
    rows = high_ref.shape[0] // devices
    x = x_ref[...]
    sums = dot(x, cells_ref[...])
    sums_high = sums.astype(jnp.bfloat16)
    sums_low = (sums - sums_high.astype(jnp.float32)).astype(jnp.bfloat16)
    high = high_ref[...]
    spectra_ref[...] = dot(high, sums_high) + (dot(high, sums_low) + dot(low_ref[...], sums_high))
    across = (((1,), (1,)), ((), ()))
    corners = lax.dot_general(first_ref[...], x[:, :LANES], across, preferred_element_type=jnp.float32)
    corners += lax.dot_general(
        last_ref[...], x[:, SIDE * SIDE - LANES :], across, preferred_element_type=jnp.float32
    )
    corners = corners.astype(jnp.bfloat16)
    corner_spectra = dot(corners, high_t_ref[...]) + dot(corners, low_t_ref[...])
    field, half = place % 2, place // 2
    lane_start = field * (LANES // 2) + half * rows
    lane = lax.broadcasted_iota(jnp.int32, (CORNER_ROWS, LANES), 1)
    mine = (lane >= lane_start) & (lane < lane_start + rows)
    for step in range(devices):
        band = jnp.bitwise_xor(place, step)
        start = pl.multiple_of(band * rows, rows)
        block = spectra_ref[pl.ds(start, rows), :].astype(jnp.bfloat16)
        outs[step][0:rows, :] = block[:, :LANES]
        outs[step][rows : 2 * rows, :] = block[:, LANES:]
        turned = pltpu.roll(corner_spectra, lax.rem(lane_start - start + LANES, LANES), 1)
        outs[step][2 * rows : 2 * rows + CORNER_ROWS, :] = jnp.where(mine, turned, 0.0).astype(jnp.bfloat16)


def collect_kernel(devices, place_ref, *rest):
    blocks, (band_ref, height_ref, held_ref) = rest[:devices], rest[devices:]
    place = place_ref[0]
    rows = (blocks[0].shape[0] - CORNER_ROWS) // 2
    total = height_ref.shape[0]
    corners = jnp.zeros((CORNER_ROWS, LANES), jnp.float32)
    for step in range(devices):
        source = jnp.bitwise_xor(place, step)
        field, half = source % 2, source // 2
        start = pl.multiple_of(field * total + half * rows, rows)
        held_ref[pl.ds(start, rows), :] = blocks[step][0:rows, :]
        held_ref[pl.ds(2 * total + start, rows), :] = blocks[step][rows : 2 * rows, :]
        corners += blocks[step][2 * rows :, :].astype(jnp.float32)
    height_ref[...] = held_ref[0:total, :]
    band_ref[0 : 3 * total, :] = held_ref[total : 4 * total, :]
    band_ref[3 * total :, :] = corners.astype(jnp.bfloat16)


def placement_kernel(
    tile_ref, ids_ref, near_ids_ref, codes_ref, paired_ref, map_ref, corner_map_ref, slot_ref, wide_ref, corner_ref
):
    slots = ids_ref.shape[0]
    tile = tile_ref[0]

    def invert(slot, carry):
        slot_ref[ids_ref[slot]] = slot
        return carry

    lax.fori_loop(0, slots, invert, 0, unroll=slots <= 8)
    wide_ref[...] = jnp.zeros_like(wide_ref)
    corner_ref[...] = jnp.zeros_like(corner_ref)
    block = lax.broadcasted_iota(jnp.int32, (BLOCKS, LANES), 0)
    cell = lax.broadcasted_iota(jnp.int32, (BLOCKS, LANES), 1)
    corner_row = lax.broadcasted_iota(jnp.int32, (CORNER_ROWS, LANES), 0)
    corner_cell = lax.broadcasted_iota(jnp.int32, (CORNER_ROWS, LANES), 1)

    def target(edge, position):
        if edge == NORTH:
            return position // 2
        if edge == EAST:
            return position * (SIDE // 4) + SIDE // 4 - 1
        if edge == SOUTH:
            return LANES - SIDE // 4 + position // 2
        return position * (SIDE // 4)

    def turn(position, reverse):
        return position + reverse * (BLOCKS - 1 - 2 * position)

    partners = paired_ref.shape[1]
    wanted = [tile] + [slot_ref[paired_ref[0, partner]] for partner in range(partners)]
    for index, slot in enumerate(wanted):
        columns = slice(index * LANES, (index + 1) * LANES)
        for edge in range(4):
            near = slot_ref[near_ids_ref[slot, edge]]
            code = codes_ref[slot, edge]
            touching, reverse = code % 4, code // 4
            pattern = (cell == target(edge, turn(block, reverse))).astype(jnp.float32)
            start = pl.multiple_of(jnp.bitwise_xor(tile, near) * LANES + touching * BLOCKS, BLOCKS)
            wide_ref[pl.ds(start, BLOCKS), columns] += pattern
            beyond = slot_ref[near_ids_ref[near, touching]]
            beyond_code = codes_ref[near, touching]
            reverse_both = jnp.bitwise_xor(reverse, beyond_code // 4)
            pattern = (cell == target(edge, turn(block, reverse_both))).astype(jnp.float32)
            start = pl.multiple_of(
                jnp.bitwise_xor(tile, beyond) * LANES + 4 * BLOCKS + (beyond_code % 4) * BLOCKS, BLOCKS
            )
            wide_ref[pl.ds(start, BLOCKS), columns] += pattern
            for end in range(2):
                rim_edge = jnp.int32(0)
                rim_end = jnp.int32(0)
                for option in range(4):
                    rim_edge = jnp.where(touching == option, END_RIMS[option][end][0], rim_edge)
                    rim_end = jnp.where(touching == option, END_RIMS[option][end][1], rim_end)
                other = slot_ref[near_ids_ref[near, rim_edge]]
                other_code = codes_ref[near, rim_edge]
                other_end = jnp.bitwise_xor(rim_end, other_code // 4)
                corner = jnp.int32(0)
                for option in range(4):
                    for which in range(2):
                        corner = jnp.where(
                            (other_code % 4 == option) & (other_end == which), EDGE_CORNERS[option][which], corner
                        )
                position = turn((BLOCKS - 1) * end, reverse)
                hit = (corner_row == corner) & (corner_cell == target(edge, position))
                start = pl.multiple_of(jnp.bitwise_xor(tile, other) * CORNER_ROWS, CORNER_ROWS)
                corner_ref[pl.ds(start, CORNER_ROWS), columns] += hit.astype(jnp.float32)
    map_ref[...] = wide_ref[...].astype(jnp.bfloat16)
    corner_map_ref[...] = corner_ref[...].astype(jnp.bfloat16)


def density_kernel(
    tiles, scale, per_band, tile_ref, ids_ref, paired_ref, height_ref, map_ref, corner_map_ref, *rest
):
    bands, (out_ref, turned_ref, partner_ref) = rest[:tiles], rest[tiles:]
    total = height_ref.shape[0]
    partners = paired_ref.shape[1]
    step_freqs = out_ref.shape[3]

    @pl.when(pl.program_id(0) == 0)
    def _():
        tile = tile_ref[0]
        height_rims = jnp.concatenate([band[total : 2 * total, :] for band in bands], axis=1)
        velocity_rims = jnp.concatenate([band[2 * total : 3 * total, :] for band in bands], axis=1)
        corners = jnp.concatenate([band[3 * total :, :] for band in bands], axis=0)
        corner_part = lax.dot_general(
            corners, corner_map_ref[...], (((0,), (0,)), ((), ())), preferred_element_type=jnp.float32
        )
        height = height_ref[...].astype(jnp.float32) + dot(height_rims, map_ref[:, :LANES])
        height = height + corner_part[:total, :LANES]
        velocity = dot(velocity_rims, map_ref[:, LANES:]) + corner_part[total:, LANES:]
        own = []
        for partner in range(partners):
            slot = jnp.int32(0)
            for candidate in range(ids_ref.shape[0]):
                slot = jnp.where(ids_ref[candidate] == paired_ref[0, partner], candidate, slot)
            wanted = jnp.bitwise_xor(tile, slot)
            chosen = bands[0][0:total, :]
            for step in range(1, tiles):
                chosen = jnp.where(wanted == step, bands[step][0:total, :], chosen)
            own.append(chosen.astype(jnp.float32))
        velocity = velocity + jnp.concatenate(own, axis=1)
        partner_ref[...] = velocity.astype(jnp.bfloat16)
        height = height.astype(jnp.bfloat16).astype(jnp.float32)
        row = lax.broadcasted_iota(jnp.int32, height.shape, 0)
        rotated = jnp.where(
            (row // per_band) % 2 == 0,
            pltpu.roll(height, total - per_band, 0),
            -pltpu.roll(height, per_band, 0),
        )
        turned_ref[0:LANES, :] = height.T
        turned_ref[LANES:, :] = rotated.T

    lane = lax.broadcasted_iota(jnp.int32, turned_ref.shape, 1)
    for offset in range(step_freqs):
        frequency = pl.program_id(0) * step_freqs + offset
        left = jnp.where(lane % per_band == frequency, turned_ref[...], 0.0).astype(jnp.bfloat16)
        cross = dot(left, partner_ref[...]) * scale
        for partner in range(partners):
            for part in range(2):
                out_ref[0, partner, part, offset] = cross[
                    part * LANES : (part + 1) * LANES, partner * LANES : (partner + 1) * LANES
                ]


SMEM = pl.BlockSpec(memory_space=pltpu.SMEM)
VMEM = pl.BlockSpec(memory_space=pltpu.VMEM)


def shards(tiles, freqs, field_count, fields, slot_tile_ids, neighbour_tile_ids, neighbour_rotation_code, paired_tile_ids):
    field = fields.reshape(fields.shape[2], fields.shape[3])
    samples = field.shape[0]
    devices = freqs * field_count
    per_band = FREQS // devices
    rows = samples // SEGLEN * 2 * per_band
    total = freqs * rows
    partners = paired_tile_ids.shape[1]
    tile = lax.axis_index("tiles").astype(jnp.int32).reshape(1)
    place = (lax.axis_index("freq") * field_count + lax.axis_index("field")).astype(jnp.int32).reshape(1)

    def swap(value, axes, count, step):
        return lax.ppermute(value, axes, [(i, i ^ step) for i in range(count)])

    piece = jax.ShapeDtypeStruct((2 * rows + CORNER_ROWS, LANES), jnp.bfloat16)
    pieces = pl.pallas_call(
        functools.partial(transform_kernel, devices),
        out_shape=[piece] * devices,
        in_specs=[SMEM] + [VMEM] * 8,
        out_specs=[VMEM] * devices,
        scratch_shapes=[pltpu.VMEM((samples, 2 * LANES), jnp.float32)],
        name="transform",
    )(place, field, *cell_tables(), *time_tables(devices, samples))
    pieces = [pieces[0]] + [
        swap(pieces[step], ("freq", "field"), devices, step) for step in range(1, devices)
    ]

    cell_map, corner_map = pl.pallas_call(
        placement_kernel,
        out_shape=[
            jax.ShapeDtypeStruct((tiles * LANES, (1 + partners) * LANES), jnp.bfloat16),
            jax.ShapeDtypeStruct((tiles * CORNER_ROWS, (1 + partners) * LANES), jnp.bfloat16),
        ],
        in_specs=[SMEM] * 5,
        out_specs=[VMEM] * 2,
        scratch_shapes=[
            pltpu.SMEM((tiles,), jnp.int32),
            pltpu.VMEM((tiles * LANES, (1 + partners) * LANES), jnp.float32),
            pltpu.VMEM((tiles * CORNER_ROWS, (1 + partners) * LANES), jnp.float32),
        ],
        name="placement",
    )(tile, slot_tile_ids, neighbour_tile_ids, neighbour_rotation_code, paired_tile_ids)

    band, height = pl.pallas_call(
        functools.partial(collect_kernel, devices),
        out_shape=[
            jax.ShapeDtypeStruct((3 * total + CORNER_ROWS, LANES), jnp.bfloat16),
            jax.ShapeDtypeStruct((total, LANES), jnp.bfloat16),
        ],
        in_specs=[SMEM] + [VMEM] * devices,
        out_specs=[VMEM] * 2,
        scratch_shapes=[pltpu.VMEM((4 * total, LANES), jnp.bfloat16)],
        name="collect",
    )(place, *pieces)
    bands = [band] + [swap(band, "tiles", tiles, step) for step in range(1, tiles)]

    segments = freqs * samples // SEGLEN
    scale = 1.0 / (segments * SEGLEN * 0.375)
    step_freqs = 2
    block = (1, partners, 2, step_freqs, LANES, LANES)
    return pl.pallas_call(
        functools.partial(density_kernel, tiles, scale, per_band),
        out_shape=jax.ShapeDtypeStruct((1, partners, 2, per_band, LANES, LANES), jnp.float32),
        grid=(per_band // step_freqs,),
        in_specs=[SMEM] * 3 + [VMEM] * (3 + tiles),
        out_specs=pl.BlockSpec(block, lambda i: (0, 0, 0, i, 0, 0)),
        scratch_shapes=[
            pltpu.VMEM((2 * LANES, total), jnp.float32),
            pltpu.VMEM((total, partners * LANES), jnp.bfloat16),
        ],
        name="density",
    )(tile, slot_tile_ids, paired_tile_ids, height, cell_map, corner_map, *bands)


def solution(mesh):
    placed = (P("field", "tiles", ("groups", "freq"), None), P(), P(), P(), P("tiles", None))
    return jax.shard_map(
        functools.partial(shards, mesh.shape["tiles"], mesh.shape["freq"], mesh.shape["field"]),
        mesh=mesh,
        in_specs=placed,
        out_specs=P(("groups", "tiles"), None, None, ("freq", "field"), None, None),
        check_vma=False,
    )
```

time: 70 us -> 24.4 us (0.35)
  blocking collectives: 45.8 us -> 0 us
  Pallas kernels: 0 us -> 9.81 us
  local copies, waits for them, and re-layouts: 9.18 us -> 1.25 us
  other arithmetic: 7.23 us -> 0 us
  starting transfers between devices: 3.26 us -> 7.47 us
  waiting for transfers between devices: 2.42 us -> 5.62 us
  between operations: 1.03 us -> 0.02 us
  matrix products: 0.77 us -> 0 us
    all_gather x3 -> x0, blocking collectives: 42 us -> none  [the longest x1 15.1 us: shards(): lax.all_gather(tile_edges(field, SIDE), 'tiles', axis=0, tiled=True)]
    pallas_call x0 -> x4, Pallas kernels: none -> 9.81 us  [the longest x1 3.64 us: shards(): pl.pallas_call(functools.partial(density_kernel, tiles, scale, per_band),...]
    ppermute x0 -> x6, starting transfers between devices: none -> 7.47 us  [swap(): return lax.ppermute(value, axes, [(i, i ^ step) for i in range(count)])]
    ppermute x0 -> x6, waiting for transfers between devices: none -> 5.62 us  [swap(): return lax.ppermute(value, axes, [(i, i ^ step) for i in range(count)])]
    all_to_all x1 -> x0, blocking collectives: 3.75 us -> none  [shards(): lax.all_to_all(lax.all_to_all(spectra[None], 'freq', split_axis=4, concat...]
    all_to_all x1 -> x0, starting transfers between devices: 3.26 us -> none  [shards(): lax.all_to_all(spectra[None], 'freq', split_axis=4, concat_axis=2, tiled=...]
    reduce_sum x4 -> x0, other arithmetic: 2.87 us -> none  [the longest x1 1.29 us: coarse_sums(): jnp.sum(blocks, axis=(-3, -1))]
    convert_element_type x9 -> x0, other arithmetic: 2.62 us -> none  [the longest x2 2.21 us: smooth_step(): values = field.astype(jnp.float32)]
  transfers between devices with their start and end apart: 1 -> 6, of which waited for: 1 -> 3; matrix products, arithmetic and copies ran while one was open for 1% -> 0% of each run, Pallas kernels for 0% -> 9%
where the time goes in v1:
time: 24.4 us; the launch traced here: 24.2 us
  Pallas kernels  9.81 us (40%)
  starting transfers between devices  7.47 us (31%)
  waiting for transfers between devices  5.62 us (23%)
  local copies, waits for them, and re-layouts  1.25 us (5%)
    ppermute x6, starting transfers between devices, swap(): return lax.ppermute(value, axes, [(i, i ^ step) for i in range(count)])  7.47 us
    ppermute x6, waiting for transfers between devices, swap(): return lax.ppermute(value, axes, [(i, i ^ step) for i in range(count)])  5.62 us
    pallas_call x1, Pallas kernels, shards(): pl.pallas_call(functools.partial(density_kernel, tiles, scale, per_band),...  3.64 us
    pallas_call x1, Pallas kernels, shards(): pl.pallas_call(functools.partial(transform_kernel, devices), out_shape=[p...  2.5 us
    pallas_call x1, Pallas kernels, shards(): pl.pallas_call(placement_kernel, out_shape=[jax.ShapeDtypeStruct((tiles *...  2.24 us
    pallas_call x1, Pallas kernels, shards(): pl.pallas_call(functools.partial(collect_kernel, devices), out_shape=[jax...  1.42 us
    unnamed x12, local copies, waits for them, and re-layouts  1.25 us
  transfers between devices with their start and end apart: 6, of which 3 were waited for; matrix products, arithmetic and copies ran while one was open for 0% of the time, Pallas kernels for 9%

profile of v1, /device:TPU:0, one launch (start us, length us, event | category | flops | bytes accessed | tf_op | source)
XLA Modules:
  0.0 24.2 jit_solution(13334660789487247905)
XLA Ops:
  0.0 2.5 %transform.1 = (bf16[80,128]{1,0:T(8,128)(2,1)}, bf16[80,128]{1,0:T(8,128)(2,1)}, bf16[80,128]{1,0:T(8,128)(2,1)}, bf16[80,128]{1,0:T(8,128)(2,1)}) custom-call(s32[1]{0:T(128)} %bitcast.1.place_ref, bf16[128,1024]{1,0:T(8,128)(2,1)} %bitcast.3, bf16[1024,256]{1,0:T(8,128)(2,1)} %constant.27.clone.cells_ref, bf16[16,128]{1,0:T(8,128)(2,1)} %constant.28.clone.first_ref, ...), custom_call_target="tpu_custom_call" | custom-call | tf_op jit(solution)/shard_map/transform/pallas_call | solution.py:294
  2.5 0.5 %collective-permute-start = (bf16[80,128]{1,0:T(8,128)(2,1)}, bf16[80,128]{1,0:T(8,128)(2,1)S(1)}, u32[]{:S(2)}, u32[]{:S(2)}) collective-permute-start(bf16[80,128]{1,0:T(8,128)(2,1)} %get-tuple-element.14), channel_id=1, source_target_pairs={{0,1},{1,0},{2,3},{3,2},{4,5},{5,4},{6,7},{7,6},{8,9},{9,8},{10,11... | collective-permute-start | bytes 61448 | tf_op jit(solution)/shard_map/ppermute | solution.py:291
  3.0 2.6 %collective-permute-start.1 = (bf16[80,128]{1,0:T(8,128)(2,1)}, bf16[80,128]{1,0:T(8,128)(2,1)S(1)}, u32[]{:S(2)}, u32[]{:S(2)}) collective-permute-start(bf16[80,128]{1,0:T(8,128)(2,1)} %get-tuple-element.15), channel_id=1, source_target_pairs={{0,2},{1,3},{2,0},{3,1},{4,6},{5,7},{6,4},{7,5},{8,10},{9,11},{10,... | collective-permute-start | bytes 61448 | tf_op jit(solution)/shard_map/ppermute | solution.py:291
  5.5 0.1 collective-permute-start.2
  5.6 0.0 collective-permute-done.rest_1_
  5.6 0.0 copy-start.3
  5.6 1.9 %collective-permute-done.1.rest_2_ = bf16[80,128]{1,0:T(8,128)(2,1)S(1)} collective-permute-done((bf16[80,128]{1,0:T(8,128)(2,1)}, bf16[80,128]{1,0:T(8,128)(2,1)S(1)}, u32[]{:S(2)}, u32[]{:S(2)}) %collective-permute-start.1) | collective-permute-done | bytes 20512 | tf_op jit(solution)/shard_map/ppermute | solution.py:291
  7.5 0.0 copy-start.4
  7.5 1.4 %collective-permute-done.2.rest_3_ = bf16[80,128]{1,0:T(8,128)(2,1)S(1)} collective-permute-done((bf16[80,128]{1,0:T(8,128)(2,1)}, bf16[80,128]{1,0:T(8,128)(2,1)S(1)}, u32[]{:S(2)}, u32[]{:S(2)}) %collective-permute-start.2) | collective-permute-done | bytes 20512 | tf_op jit(solution)/shard_map/ppermute | solution.py:291
  8.9 0.0 copy-start.5
  8.9 0.0 copy-done.3
  8.9 0.0 copy-done.4
  8.9 0.6 %copy-done.5 = bf16[80,128]{1,0:T(8,128)(2,1)} copy-done((bf16[80,128]{1,0:T(8,128)(2,1)}, bf16[80,128]{1,0:T(8,128)(2,1)S(1)}, u32[]{:S(2)}) %copy-start.5) | copy-done | bytes 20504
  9.5 1.4 %collect.1 = (bf16[208,128]{1,0:T(8,128)(2,1)}, bf16[64,128]{1,0:T(8,128)(2,1)}) custom-call(s32[1]{0:T(128)} %bitcast.1.place_ref, bf16[80,128]{1,0:T(8,128)(2,1)} %get-tuple-element.13.rest_0_, bf16[80,128]{1,0:T(8,128)(2,1)} %copy-done.3, bf16[80,128]{1,0:T(8,128)(2,1)} %copy-done.4, bf16[80,128]{1,0:T(8,128)(2,1)} %copy-done.5), custom_call_target="tpu_custom_call" | custom-call | tf_op jit(solution)/shard_map/collect/pallas_call | solution.py:322
  11.0 3.6 %collective-permute-start.5 = (bf16[208,128]{1,0:T(8,128)(2,1)}, bf16[208,128]{1,0:T(8,128)(2,1)S(1)}, u32[]{:S(2)}, u32[]{:S(2)}) collective-permute-start(bf16[208,128]{1,0:T(8,128)(2,1)} %get-tuple-element.20.rest_0_), channel_id=1, source_target_pairs={{0,12},{4,8},{8,4},{12,0},{1,13},{5,9},{9,5},{13,1},{2,14},{6,10},... | collective-permute-start | bytes 159752 | tf_op jit(solution)/shard_map/ppermute | solution.py:291
  14.6 0.0 collective-permute-start.4
  14.6 0.8 %collective-permute-start.3 = (bf16[208,128]{1,0:T(8,128)(2,1)}, bf16[208,128]{1,0:T(8,128)(2,1)S(1)}, u32[]{:S(2)}, u32[]{:S(2)}) collective-permute-start(bf16[208,128]{1,0:T(8,128)(2,1)} %get-tuple-element.20.rest_0_), channel_id=1, source_target_pairs={{0,4},{4,0},{8,12},{12,8},{1,5},{5,1},{9,13},{13,9},{2,6},{6,2},{1... | collective-permute-start | bytes 159752 | tf_op jit(solution)/shard_map/ppermute | solution.py:291
  15.3 2.2 %placement.1 = (bf16[512,384]{1,0:T(8,128)(2,1)}, bf16[64,384]{1,0:T(8,128)(2,1)}) custom-call(s32[1]{0:T(128)} %bitcast.tile_ref, s32[4]{0:T(128)} %ids_ref.3, s32[4,4]{1,0:T(4,128)} %near_ids_ref.1, s32[4,4]{1,0:T(4,128)} %codes_ref.1, s32[1,2]{1,0:T(1,128)} %paired_ref.3), custom_call_target="tpu_custom_call" | custom-call | tf_op jit(solution)/shard_map/placement/pallas_call | solution.py:306
  17.6 0.0 collective-permute-done.5.rest_3_
  17.6 0.0 copy-start
  17.6 2.3 %collective-permute-done.4.rest_2_ = bf16[208,128]{1,0:T(8,128)(2,1)S(1)} collective-permute-done((bf16[208,128]{1,0:T(8,128)(2,1)}, bf16[208,128]{1,0:T(8,128)(2,1)S(1)}, u32[]{:S(2)}, u32[]{:S(2)}) %collective-permute-start.4) | collective-permute-done | bytes 53280 | tf_op jit(solution)/shard_map/ppermute | solution.py:291
  19.9 0.0 copy-start.1
  19.9 0.0 collective-permute-done.3.rest_1_
  19.9 0.0 copy-start.2
  19.9 0.0 copy-done
  19.9 0.6 %copy-done.1 = bf16[208,128]{1,0:T(8,128)(2,1)} copy-done((bf16[208,128]{1,0:T(8,128)(2,1)}, bf16[208,128]{1,0:T(8,128)(2,1)S(1)}, u32[]{:S(2)}) %copy-start.1) | copy-done | bytes 53272
  20.5 0.0 copy-done.2
  20.5 3.6 %density.1 = f32[1,2,2,8,128,128]{5,4,3,2,1,0:T(8,128)} custom-call(s32[1]{0:T(128)} %bitcast.tile_ref, s32[4]{0:T(128)} %ids_ref.3, s32[1,2]{1,0:T(1,128)} %paired_ref.3, bf16[64,128]{1,0:T(8,128)(2,1)} %get-tuple-element.17.height_ref, bf16[512,384]{1,0:T(8,128)(2,1)} %get-tuple-element.18.map_ref, bf16[64,384]{1,0:T(8,128)(2,1)} %get-tuple-element.19.corner_map_ref, ...), custom_call_target="tpu_custom_call" | custom-call | tf_op jit(solution)/shard_map/density/pallas_call | solution.py:339
Async XLA Ops:
  2.5 3.1 %collective-permute-start = (bf16[80,128]{1,0:T(8,128)(2,1)}, bf16[80,128]{1,0:T(8,128)(2,1)S(1)}, u32[]{:S(2)}, u32[]{:S(2)}) collective-permute-start(bf16[80,128]{1,0:T(8,128)(2,1)} %get-tuple-element.14), channel_id=1, source_target_pairs={{0,1},{1,0},{2,3},{3,2},{4,5},{5,4},{6,7},{7,6},{8,9},{9,8},{10,11... | collective-permute-start | bytes 61448 | tf_op jit(solution)/shard_map/ppermute | solution.py:291
  3.0 4.5 %collective-permute-start.1 = (bf16[80,128]{1,0:T(8,128)(2,1)}, bf16[80,128]{1,0:T(8,128)(2,1)S(1)}, u32[]{:S(2)}, u32[]{:S(2)}) collective-permute-start(bf16[80,128]{1,0:T(8,128)(2,1)} %get-tuple-element.15), channel_id=1, source_target_pairs={{0,2},{1,3},{2,0},{3,1},{4,6},{5,7},{6,4},{7,5},{8,10},{9,11},{10,... | collective-permute-start | bytes 61448 | tf_op jit(solution)/shard_map/ppermute | solution.py:291
  5.5 3.4 %collective-permute-start.2 = (bf16[80,128]{1,0:T(8,128)(2,1)}, bf16[80,128]{1,0:T(8,128)(2,1)S(1)}, u32[]{:S(2)}, u32[]{:S(2)}) collective-permute-start(bf16[80,128]{1,0:T(8,128)(2,1)} %get-tuple-element.16), channel_id=1, source_target_pairs={{0,3},{1,2},{2,1},{3,0},{4,7},{5,6},{6,5},{7,4},{8,11},{9,10},{10,... | collective-permute-start | bytes 61448 | tf_op jit(solution)/shard_map/ppermute | solution.py:291
  5.6 3.3 %copy-start.3 = (bf16[80,128]{1,0:T(8,128)(2,1)}, bf16[80,128]{1,0:T(8,128)(2,1)S(1)}, u32[]{:S(2)}) copy-start(bf16[80,128]{1,0:T(8,128)(2,1)S(1)} %collective-permute-done.rest_1_) | copy-start | bytes 61444
  7.5 1.5 %copy-start.4 = (bf16[80,128]{1,0:T(8,128)(2,1)}, bf16[80,128]{1,0:T(8,128)(2,1)S(1)}, u32[]{:S(2)}) copy-start(bf16[80,128]{1,0:T(8,128)(2,1)S(1)} %collective-permute-done.1.rest_2_) | copy-start | bytes 61444
  8.9 0.6 %copy-start.5 = (bf16[80,128]{1,0:T(8,128)(2,1)}, bf16[80,128]{1,0:T(8,128)(2,1)S(1)}, u32[]{:S(2)}) copy-start(bf16[80,128]{1,0:T(8,128)(2,1)S(1)} %collective-permute-done.2.rest_3_) | copy-start | bytes 61444
  11.0 6.6 %collective-permute-start.5 = (bf16[208,128]{1,0:T(8,128)(2,1)}, bf16[208,128]{1,0:T(8,128)(2,1)S(1)}, u32[]{:S(2)}, u32[]{:S(2)}) collective-permute-start(bf16[208,128]{1,0:T(8,128)(2,1)} %get-tuple-element.20.rest_0_), channel_id=1, source_target_pairs={{0,12},{4,8},{8,4},{12,0},{1,13},{5,9},{9,5},{13,1},{2,14},{6,10},... | collective-permute-start | bytes 159752 | tf_op jit(solution)/shard_map/ppermute | solution.py:291
  14.6 5.3 %collective-permute-start.4 = (bf16[208,128]{1,0:T(8,128)(2,1)}, bf16[208,128]{1,0:T(8,128)(2,1)S(1)}, u32[]{:S(2)}, u32[]{:S(2)}) collective-permute-start(bf16[208,128]{1,0:T(8,128)(2,1)} %get-tuple-element.20.rest_0_), channel_id=1, source_target_pairs={{0,8},{4,12},{8,0},{12,4},{1,9},{5,13},{9,1},{13,5},{2,10},{6,14},... | collective-permute-start | bytes 159752 | tf_op jit(solution)/shard_map/ppermute | solution.py:291
  14.6 5.3 %collective-permute-start.3 = (bf16[208,128]{1,0:T(8,128)(2,1)}, bf16[208,128]{1,0:T(8,128)(2,1)S(1)}, u32[]{:S(2)}, u32[]{:S(2)}) collective-permute-start(bf16[208,128]{1,0:T(8,128)(2,1)} %get-tuple-element.20.rest_0_), channel_id=1, source_target_pairs={{0,4},{4,0},{8,12},{12,8},{1,5},{5,1},{9,13},{13,9},{2,6},{6,2},{1... | collective-permute-start | bytes 159752 | tf_op jit(solution)/shard_map/ppermute | solution.py:291
  17.6 2.3 %copy-start = (bf16[208,128]{1,0:T(8,128)(2,1)}, bf16[208,128]{1,0:T(8,128)(2,1)S(1)}, u32[]{:S(2)}) copy-start(bf16[208,128]{1,0:T(8,128)(2,1)S(1)} %collective-permute-done.5.rest_3_) | copy-start | bytes 159748
  19.9 0.6 %copy-start.1 = (bf16[208,128]{1,0:T(8,128)(2,1)}, bf16[208,128]{1,0:T(8,128)(2,1)S(1)}, u32[]{:S(2)}) copy-start(bf16[208,128]{1,0:T(8,128)(2,1)S(1)} %collective-permute-done.4.rest_2_) | copy-start | bytes 159748
  19.9 0.6 %copy-start.2 = (bf16[208,128]{1,0:T(8,128)(2,1)}, bf16[208,128]{1,0:T(8,128)(2,1)S(1)}, u32[]{:S(2)}) copy-start(bf16[208,128]{1,0:T(8,128)(2,1)S(1)} %collective-permute-done.3.rest_1_) | copy-start | bytes 159748

commit v2 on v1

--- a/solution.py
+++ b/solution.py
@@ -290,7 +290,7 @@
     def swap(value, axes, count, step):
         return lax.ppermute(value, axes, [(i, i ^ step) for i in range(count)])
 
-    piece = jax.ShapeDtypeStruct((2 * rows + CORNER_ROWS, LANES), jnp.bfloat16)
+    piece = pltpu.VMEM((2 * rows + CORNER_ROWS, LANES), jnp.bfloat16)
     pieces = pl.pallas_call(
         functools.partial(transform_kernel, devices),
         out_shape=[piece] * devices,
@@ -306,8 +306,8 @@
     cell_map, corner_map = pl.pallas_call(
         placement_kernel,
         out_shape=[
-            jax.ShapeDtypeStruct((tiles * LANES, (1 + partners) * LANES), jnp.bfloat16),
-            jax.ShapeDtypeStruct((tiles * CORNER_ROWS, (1 + partners) * LANES), jnp.bfloat16),
+            pltpu.VMEM((tiles * LANES, (1 + partners) * LANES), jnp.bfloat16),
+            pltpu.VMEM((tiles * CORNER_ROWS, (1 + partners) * LANES), jnp.bfloat16),
         ],
         in_specs=[SMEM] * 5,
         out_specs=[VMEM] * 2,
@@ -322,14 +322,14 @@
     band, height = pl.pallas_call(
         functools.partial(collect_kernel, devices),
         out_shape=[
-            jax.ShapeDtypeStruct((3 * total + CORNER_ROWS, LANES), jnp.bfloat16),
-            jax.ShapeDtypeStruct((total, LANES), jnp.bfloat16),
+            pltpu.VMEM((3 * total + CORNER_ROWS, LANES), jnp.bfloat16),
+            pltpu.VMEM((total, LANES), jnp.bfloat16),
         ],
         in_specs=[SMEM] + [VMEM] * devices,
         out_specs=[VMEM] * 2,
         scratch_shapes=[pltpu.VMEM((4 * total, LANES), jnp.bfloat16)],
         name="collect",
-    )(place, *pieces)
+    )(place, *map(near, pieces))
     bands = [band] + [swap(band, "tiles", tiles, step) for step in range(1, tiles)]
 
     segments = freqs * samples // SEGLEN
@@ -347,7 +347,11 @@
             pltpu.VMEM((total, partners * LANES), jnp.bfloat16),
         ],
         name="density",
-    )(tile, slot_tile_ids, paired_tile_ids, height, cell_map, corner_map, *bands)
+    )(tile, slot_tile_ids, paired_tile_ids, *map(near, (height, cell_map, corner_map, *bands)))
+
+
+def near(value):
+    return pltpu.with_memory_space_constraint(value, pltpu.VMEM)
 
 
 def solution(mesh):

time: 24.4 us -> 20.3 us (0.83)
  Pallas kernels: 9.81 us -> 6.65 us
  local copies, waits for them, and re-layouts: 1.25 us -> 0 us
  waiting for transfers between devices: 5.62 us -> 5.95 us
    pallas_call x2, Pallas kernels: 3.67 us -> 1.52 us  [the longest x1 1.49 us: shards(): pl.pallas_call(placement_kernel, out_shape=[pltpu.VMEM((tiles * LANES, (1...]
    unnamed x12 -> x0, local copies, waits for them, and re-layouts: 1.25 us -> none
    pallas_call x1, Pallas kernels: 2.5 us -> 1.87 us  [shards(): pl.pallas_call(functools.partial(transform_kernel, devices), out_shape=[p...]
    pallas_call x1, Pallas kernels: 3.64 us -> 3.25 us  [shards(): pl.pallas_call(functools.partial(density_kernel, tiles, scale, per_band),...]
    ppermute x6, waiting for transfers between devices: 5.62 us -> 5.95 us  [swap(): return lax.ppermute(value, axes, [(i, i ^ step) for i in range(count)])]
  transfers between devices with their start and end apart: 6 -> 6, of which waited for: 3 -> 4; matrix products, arithmetic and copies ran while one was open for 0% -> 0% of each run, Pallas kernels for 9% -> 7%
where the time goes in v2:
time: 20.3 us; the launch traced here: 20.2 us
  starting transfers between devices  7.54 us (37%)
  Pallas kernels  6.65 us (33%)
  waiting for transfers between devices  5.95 us (29%)
    ppermute x6, starting transfers between devices, swap(): return lax.ppermute(value, axes, [(i, i ^ step) for i in range(count)])  7.54 us
    ppermute x6, waiting for transfers between devices, swap(): return lax.ppermute(value, axes, [(i, i ^ step) for i in range(count)])  5.95 us
    pallas_call x1, Pallas kernels, shards(): pl.pallas_call(functools.partial(density_kernel, tiles, scale, per_band),...  3.25 us
    pallas_call x1, Pallas kernels, shards(): pl.pallas_call(functools.partial(transform_kernel, devices), out_shape=[p...  1.87 us
    pallas_call x1, Pallas kernels, shards(): pl.pallas_call(placement_kernel, out_shape=[pltpu.VMEM((tiles * LANES, (1...  1.49 us
  transfers between devices with their start and end apart: 6, of which 4 were waited for; matrix products, arithmetic and copies ran while one was open for 0% of the time, Pallas kernels for 7%

profile of v2, /device:TPU:0, one launch (start us, length us, event | category | flops | bytes accessed | tf_op | source)
XLA Modules:
  0.0 20.2 jit_solution(17628285696119820599)
XLA Ops:
  0.0 1.9 %transform.1 = (bf16[80,128]{1,0:T(8,128)(2,1)S(1)}, bf16[80,128]{1,0:T(8,128)(2,1)S(1)}, bf16[80,128]{1,0:T(8,128)(2,1)S(1)}, bf16[80,128]{1,0:T(8,128)(2,1)S(1)}) custom-call(s32[1]{0:T(128)} %bitcast.1.place_ref, bf16[128,1024]{1,0:T(8,128)(2,1)} %bitcast.3, bf16[1024,256]{1,0:T(8,128)(2,1)} %constant.27.clone.cells_ref, ...), custom_call_target="tpu_custom_call" | custom-call | tf_op jit(solution)/shard_map/transform/pallas_call | solution.py:294
  1.9 0.5 %collective-permute-start = (bf16[80,128]{1,0:T(8,128)(2,1)S(1)}, bf16[80,128]{1,0:T(8,128)(2,1)S(1)}, u32[]{:S(2)}, u32[]{:S(2)}) collective-permute-start(bf16[80,128]{1,0:T(8,128)(2,1)S(1)} %get-tuple-element.14), channel_id=1, source_target_pairs={{0,1},{1,0},{2,3},{3,2},{4,5},{5,4},{6,7},{7,6},{8,9},{9,8},{10,11... | collective-permute-start | bytes 61448 | tf_op jit(solution)/shard_map/ppermute | solution.py:291
  2.3 2.6 %collective-permute-start.1 = (bf16[80,128]{1,0:T(8,128)(2,1)S(1)}, bf16[80,128]{1,0:T(8,128)(2,1)S(1)}, u32[]{:S(2)}, u32[]{:S(2)}) collective-permute-start(bf16[80,128]{1,0:T(8,128)(2,1)S(1)} %get-tuple-element.15), channel_id=1, source_target_pairs={{0,2},{1,3},{2,0},{3,1},{4,6},{5,7},{6,4},{7,5},{8,10},{9,11},{10,... | collective-permute-start | bytes 61448 | tf_op jit(solution)/shard_map/ppermute | solution.py:291
  4.9 0.1 collective-permute-start.2
  5.0 0.0 collective-permute-done.rest_1_
  5.0 1.7 %collective-permute-done.1.rest_2_ = bf16[80,128]{1,0:T(8,128)(2,1)S(1)} collective-permute-done((bf16[80,128]{1,0:T(8,128)(2,1)S(1)}, bf16[80,128]{1,0:T(8,128)(2,1)S(1)}, u32[]{:S(2)}, u32[]{:S(2)}) %collective-permute-start.1) | collective-permute-done | bytes 20512 | tf_op jit(solution)/shard_map/ppermute | solution.py:291
  6.7 1.4 %collective-permute-done.2.rest_3_ = bf16[80,128]{1,0:T(8,128)(2,1)S(1)} collective-permute-done((bf16[80,128]{1,0:T(8,128)(2,1)S(1)}, bf16[80,128]{1,0:T(8,128)(2,1)S(1)}, u32[]{:S(2)}, u32[]{:S(2)}) %collective-permute-start.2) | collective-permute-done | bytes 20512 | tf_op jit(solution)/shard_map/ppermute | solution.py:291
  8.1 3.7 %collective-permute-start.5 = (bf16[208,128]{1,0:T(8,128)(2,1)S(1)}, bf16[208,128]{1,0:T(8,128)(2,1)S(1)}, u32[]{:S(2)}, u32[]{:S(2)}) collective-permute-start(bf16[208,128]{1,0:T(8,128)(2,1)S(1)} %get-tuple-element.20.rest_0_), channel_id=1, source_target_pairs={{0,12},{4,8},{8,4},{12,0},{1,13},{5,9},{9,5},{13,1},{2,14},{6,10},... | collective-permute-start | bytes 159752 | tf_op jit(solution)/shard_map/ppermute | solution.py:291
  11.8 0.0 collective-permute-start.4
  11.8 0.8 %collective-permute-start.3 = (bf16[208,128]{1,0:T(8,128)(2,1)S(1)}, bf16[208,128]{1,0:T(8,128)(2,1)S(1)}, u32[]{:S(2)}, u32[]{:S(2)}) collective-permute-start(bf16[208,128]{1,0:T(8,128)(2,1)S(1)} %get-tuple-element.20.rest_0_), channel_id=1, source_target_pairs={{0,4},{4,0},{8,12},{12,8},{1,5},{5,1},{9,13},{13,9},{2,6},{6,2},{1... | collective-permute-start | bytes 159752 | tf_op jit(solution)/shard_map/ppermute | solution.py:291
  12.6 1.5 %placement.1 = (bf16[512,384]{1,0:T(8,128)(2,1)S(1)}, bf16[64,384]{1,0:T(8,128)(2,1)S(1)}) custom-call(s32[1]{0:T(128)} %bitcast.tile_ref, s32[4]{0:T(128)} %ids_ref.3, s32[4,4]{1,0:T(4,128)} %near_ids_ref.1, s32[4,4]{1,0:T(4,128)} %codes_ref.1, s32[1,2]{1,0:T(1,128)} %paired_ref.3), custom_call_target="tpu_custom_call" | custom-call | tf_op jit(solution)/shard_map/placement/pallas_call | solution.py:306
  14.1 0.1 collective-permute-done.5.rest_3_
  14.2 2.7 %collective-permute-done.4.rest_2_ = bf16[208,128]{1,0:T(8,128)(2,1)S(1)} collective-permute-done((bf16[208,128]{1,0:T(8,128)(2,1)S(1)}, bf16[208,128]{1,0:T(8,128)(2,1)S(1)}, u32[]{:S(2)}, u32[]{:S(2)}) %collective-permute-start.4) | collective-permute-done | bytes 53280 | tf_op jit(solution)/shard_map/ppermute | solution.py:291
  16.9 0.0 collective-permute-done.3.rest_1_
  16.9 3.3 %density.1 = f32[1,2,2,8,128,128]{5,4,3,2,1,0:T(8,128)} custom-call(s32[1]{0:T(128)} %bitcast.tile_ref, s32[4]{0:T(128)} %ids_ref.3, s32[1,2]{1,0:T(1,128)} %paired_ref.3, bf16[64,128]{1,0:T(8,128)(2,1)S(1)} %get-tuple-element.17.height_ref, bf16[512,384]{1,0:T(8,128)(2,1)S(1)} %get-tuple-element.18.map_ref, ...), custom_call_target="tpu_custom_call" | custom-call | tf_op jit(solution)/shard_map/density/pallas_call | solution.py:339
  (1 shorter events, 0.0 us)
Async XLA Ops:
  1.9 3.1 %collective-permute-start = (bf16[80,128]{1,0:T(8,128)(2,1)S(1)}, bf16[80,128]{1,0:T(8,128)(2,1)S(1)}, u32[]{:S(2)}, u32[]{:S(2)}) collective-permute-start(bf16[80,128]{1,0:T(8,128)(2,1)S(1)} %get-tuple-element.14), channel_id=1, source_target_pairs={{0,1},{1,0},{2,3},{3,2},{4,5},{5,4},{6,7},{7,6},{8,9},{9,8},{10,11... | collective-permute-start | bytes 61448 | tf_op jit(solution)/shard_map/ppermute | solution.py:291
  2.3 4.3 %collective-permute-start.1 = (bf16[80,128]{1,0:T(8,128)(2,1)S(1)}, bf16[80,128]{1,0:T(8,128)(2,1)S(1)}, u32[]{:S(2)}, u32[]{:S(2)}) collective-permute-start(bf16[80,128]{1,0:T(8,128)(2,1)S(1)} %get-tuple-element.15), channel_id=1, source_target_pairs={{0,2},{1,3},{2,0},{3,1},{4,6},{5,7},{6,4},{7,5},{8,10},{9,11},{10,... | collective-permute-start | bytes 61448 | tf_op jit(solution)/shard_map/ppermute | solution.py:291
  4.9 3.2 %collective-permute-start.2 = (bf16[80,128]{1,0:T(8,128)(2,1)S(1)}, bf16[80,128]{1,0:T(8,128)(2,1)S(1)}, u32[]{:S(2)}, u32[]{:S(2)}) collective-permute-start(bf16[80,128]{1,0:T(8,128)(2,1)S(1)} %get-tuple-element.16), channel_id=1, source_target_pairs={{0,3},{1,2},{2,1},{3,0},{4,7},{5,6},{6,5},{7,4},{8,11},{9,10},{10,... | collective-permute-start | bytes 61448 | tf_op jit(solution)/shard_map/ppermute | solution.py:291
  8.1 6.1 %collective-permute-start.5 = (bf16[208,128]{1,0:T(8,128)(2,1)S(1)}, bf16[208,128]{1,0:T(8,128)(2,1)S(1)}, u32[]{:S(2)}, u32[]{:S(2)}) collective-permute-start(bf16[208,128]{1,0:T(8,128)(2,1)S(1)} %get-tuple-element.20.rest_0_), channel_id=1, source_target_pairs={{0,12},{4,8},{8,4},{12,0},{1,13},{5,9},{9,5},{13,1},{2,14},{6,10},... | collective-permute-start | bytes 159752 | tf_op jit(solution)/shard_map/ppermute | solution.py:291
  11.8 5.1 %collective-permute-start.4 = (bf16[208,128]{1,0:T(8,128)(2,1)S(1)}, bf16[208,128]{1,0:T(8,128)(2,1)S(1)}, u32[]{:S(2)}, u32[]{:S(2)}) collective-permute-start(bf16[208,128]{1,0:T(8,128)(2,1)S(1)} %get-tuple-element.20.rest_0_), channel_id=1, source_target_pairs={{0,8},{4,12},{8,0},{12,4},{1,9},{5,13},{9,1},{13,5},{2,10},{6,14},... | collective-permute-start | bytes 159752 | tf_op jit(solution)/shard_map/ppermute | solution.py:291
  11.8 5.1 %collective-permute-start.3 = (bf16[208,128]{1,0:T(8,128)(2,1)S(1)}, bf16[208,128]{1,0:T(8,128)(2,1)S(1)}, u32[]{:S(2)}, u32[]{:S(2)}) collective-permute-start(bf16[208,128]{1,0:T(8,128)(2,1)S(1)} %get-tuple-element.20.rest_0_), channel_id=1, source_target_pairs={{0,4},{4,0},{8,12},{12,8},{1,5},{5,1},{9,13},{13,9},{2,6},{6,2},{1... | collective-permute-start | bytes 159752 | tf_op jit(solution)/shard_map/ppermute | solution.py:291

commit v3 on v2

--- a/solution.py
+++ b/solution.py
@@ -88,43 +88,41 @@
         table[:, segment, :, :, segment, :] = waves.reshape(2, bands, per_band, SEGLEN).transpose(1, 0, 2, 3)
     table = table.reshape(bands * segments * 2 * per_band, samples)
     high, low = split_bf16(table)
-    return high, low, np.ascontiguousarray(high.T), np.ascontiguousarray(low.T)
+    return high, low
 
 
 def dot(left, right):
     return jnp.dot(left, right, preferred_element_type=jnp.float32)
 
 
-def transform_kernel(
-    devices, place_ref, x_ref, cells_ref, first_ref, last_ref, high_ref, low_ref, high_t_ref, low_t_ref, *rest
-):
-    outs, spectra_ref = rest[:devices], rest[devices]
+def transform_kernel(devices, place_ref, x_ref, cells_ref, first_ref, last_ref, high_ref, low_ref, *outs):
     place = place_ref[0]
     rows = high_ref.shape[0] // devices
+    starts = [pl.multiple_of(jnp.bitwise_xor(place, step) * rows, rows) for step in range(devices)]
+    high = jnp.concatenate([high_ref[pl.ds(start, rows), :] for start in starts], axis=0)
+    low = jnp.concatenate([low_ref[pl.ds(start, rows), :] for start in starts], axis=0)
+    across = (((1,), (1,)), ((), ()))
     x = x_ref[...]
-    sums = dot(x, cells_ref[...])
-    sums_high = sums.astype(jnp.bfloat16)
-    sums_low = (sums - sums_high.astype(jnp.float32)).astype(jnp.bfloat16)
-    high = high_ref[...]
-    spectra_ref[...] = dot(high, sums_high) + (dot(high, sums_low) + dot(low_ref[...], sums_high))
-    across = (((1,), (1,)), ((), ()))
     corners = lax.dot_general(first_ref[...], x[:, :LANES], across, preferred_element_type=jnp.float32)
     corners += lax.dot_general(
         last_ref[...], x[:, SIDE * SIDE - LANES :], across, preferred_element_type=jnp.float32
     )
     corners = corners.astype(jnp.bfloat16)
-    corner_spectra = dot(corners, high_t_ref[...]) + dot(corners, low_t_ref[...])
-    field, half = place % 2, place // 2
-    lane_start = field * (LANES // 2) + half * rows
+    corner_spectra = lax.dot_general(corners, high, across, preferred_element_type=jnp.float32)
+    corner_spectra += lax.dot_general(corners, low, across, preferred_element_type=jnp.float32)
+    sums = dot(x, cells_ref[...])
+    sums_high = sums.astype(jnp.bfloat16)
+    sums_low = (sums - sums_high.astype(jnp.float32)).astype(jnp.bfloat16)
+    spectra = dot(high, sums_high) + (dot(high, sums_low) + dot(low, sums_high))
+    spectra = spectra.astype(jnp.bfloat16)
+    lane_start = (place % 2) * (LANES // 2) + (place // 2) * rows
     lane = lax.broadcasted_iota(jnp.int32, (CORNER_ROWS, LANES), 1)
     mine = (lane >= lane_start) & (lane < lane_start + rows)
     for step in range(devices):
-        band = jnp.bitwise_xor(place, step)
-        start = pl.multiple_of(band * rows, rows)
-        block = spectra_ref[pl.ds(start, rows), :].astype(jnp.bfloat16)
+        block = spectra[step * rows : (step + 1) * rows]
         outs[step][0:rows, :] = block[:, :LANES]
         outs[step][rows : 2 * rows, :] = block[:, LANES:]
-        turned = pltpu.roll(corner_spectra, lax.rem(lane_start - start + LANES, LANES), 1)
+        turned = pltpu.roll(corner_spectra, lax.rem(lane_start - step * rows + LANES, LANES), 1)
         outs[step][2 * rows : 2 * rows + CORNER_ROWS, :] = jnp.where(mine, turned, 0.0).astype(jnp.bfloat16)
 
 
@@ -147,7 +145,17 @@
 
 
 def placement_kernel(
-    tile_ref, ids_ref, near_ids_ref, codes_ref, paired_ref, map_ref, corner_map_ref, slot_ref, wide_ref, corner_ref
+    tile_ref,
+    ids_ref,
+    near_ids_ref,
+    codes_ref,
+    paired_ref,
+    map_ref,
+    corner_map_ref,
+    chosen_ref,
+    slot_ref,
+    wide_ref,
+    corner_ref,
 ):
     slots = ids_ref.shape[0]
     tile = tile_ref[0]
@@ -214,66 +222,68 @@
                 hit = (corner_row == corner) & (corner_cell == target(edge, position))
                 start = pl.multiple_of(jnp.bitwise_xor(tile, other) * CORNER_ROWS, CORNER_ROWS)
                 corner_ref[pl.ds(start, CORNER_ROWS), columns] += hit.astype(jnp.float32)
+    step = lax.broadcasted_iota(jnp.int32, (chosen_ref.shape[0], LANES), 0)
+    for partner in range(partners):
+        wanted_step = jnp.bitwise_xor(tile, wanted[1 + partner])
+        chosen_ref[:, partner * LANES : (partner + 1) * LANES] = (step == wanted_step).astype(jnp.float32)
     map_ref[...] = wide_ref[...].astype(jnp.bfloat16)
     corner_map_ref[...] = corner_ref[...].astype(jnp.bfloat16)
 
 
 def density_kernel(
-    tiles, scale, per_band, tile_ref, ids_ref, paired_ref, height_ref, map_ref, corner_map_ref, *rest
+    tiles, partners, scale, per_band, height_ref, map_ref, corner_map_ref, chosen_ref, *rest
 ):
-    bands, (out_ref, turned_ref, partner_ref) = rest[:tiles], rest[tiles:]
+    bands, (out_ref, cross_ref, sent) = rest[:tiles], rest[tiles:]
     total = height_ref.shape[0]
-    partners = paired_ref.shape[1]
-    step_freqs = out_ref.shape[3]
-
-    @pl.when(pl.program_id(0) == 0)
-    def _():
-        tile = tile_ref[0]
-        height_rims = jnp.concatenate([band[total : 2 * total, :] for band in bands], axis=1)
-        velocity_rims = jnp.concatenate([band[2 * total : 3 * total, :] for band in bands], axis=1)
-        corners = jnp.concatenate([band[3 * total :, :] for band in bands], axis=0)
-        corner_part = lax.dot_general(
-            corners, corner_map_ref[...], (((0,), (0,)), ((), ())), preferred_element_type=jnp.float32
-        )
-        height = height_ref[...].astype(jnp.float32) + dot(height_rims, map_ref[:, :LANES])
-        height = height + corner_part[:total, :LANES]
-        velocity = dot(velocity_rims, map_ref[:, LANES:]) + corner_part[total:, LANES:]
-        own = []
-        for partner in range(partners):
-            slot = jnp.int32(0)
-            for candidate in range(ids_ref.shape[0]):
-                slot = jnp.where(ids_ref[candidate] == paired_ref[0, partner], candidate, slot)
-            wanted = jnp.bitwise_xor(tile, slot)
-            chosen = bands[0][0:total, :]
-            for step in range(1, tiles):
-                chosen = jnp.where(wanted == step, bands[step][0:total, :], chosen)
-            own.append(chosen.astype(jnp.float32))
-        velocity = velocity + jnp.concatenate(own, axis=1)
-        partner_ref[...] = velocity.astype(jnp.bfloat16)
-        height = height.astype(jnp.bfloat16).astype(jnp.float32)
-        row = lax.broadcasted_iota(jnp.int32, height.shape, 0)
-        rotated = jnp.where(
-            (row // per_band) % 2 == 0,
-            pltpu.roll(height, total - per_band, 0),
-            -pltpu.roll(height, per_band, 0),
-        )
-        turned_ref[0:LANES, :] = height.T
-        turned_ref[LANES:, :] = rotated.T
-
-    lane = lax.broadcasted_iota(jnp.int32, turned_ref.shape, 1)
-    for offset in range(step_freqs):
-        frequency = pl.program_id(0) * step_freqs + offset
-        left = jnp.where(lane % per_band == frequency, turned_ref[...], 0.0).astype(jnp.bfloat16)
-        cross = dot(left, partner_ref[...]) * scale
+    height_rims = jnp.concatenate([band[total : 2 * total, :] for band in bands], axis=1)
+    velocity_rims = jnp.concatenate([band[2 * total : 3 * total, :] for band in bands], axis=1)
+    corners = jnp.concatenate([band[3 * total :, :] for band in bands], axis=0)
+    corner_part = lax.dot_general(
+        corners, corner_map_ref[...], (((0,), (0,)), ((), ())), preferred_element_type=jnp.float32
+    )
+    height = height_ref[...].astype(jnp.float32) + dot(height_rims, map_ref[:, :LANES])
+    height = height + corner_part[:total, :LANES]
+    velocity = dot(velocity_rims, map_ref[:, LANES:]) + corner_part[total:, LANES:]
+    for step in range(tiles):
+        own = bands[step][0:total, :].astype(jnp.float32)
+        velocity += jnp.concatenate([own] * partners, axis=1) * chosen_ref[step : step + 1, :]
+    velocity = velocity.astype(jnp.bfloat16)
+    height = height.astype(jnp.bfloat16).astype(jnp.float32)
+    row = lax.broadcasted_iota(jnp.int32, height.shape, 0)
+    rotated = jnp.where(
+        (row // per_band) % 2 == 0,
+        pltpu.roll(height, total - per_band, 0),
+        -pltpu.roll(height, per_band, 0),
+    )
+    turned = jnp.concatenate([height.T, rotated.T], axis=0)
+    lane = lax.broadcasted_iota(jnp.int32, turned.shape, 1)
+    copies = []
+    for frequency in range(per_band):
+        left = jnp.where(lane % per_band == frequency, turned, 0.0).astype(jnp.bfloat16)
+        cross = dot(left, velocity) * scale
         for partner in range(partners):
             for part in range(2):
-                out_ref[0, partner, part, offset] = cross[
+                index = (partner * 2 + part) * per_band + frequency
+                rows = pl.ds(index * LANES, LANES)
+                cross_ref[rows, :] = cross[
                     part * LANES : (part + 1) * LANES, partner * LANES : (partner + 1) * LANES
                 ]
+                copies.append(pltpu.make_async_copy(cross_ref.at[rows], out_ref.at[rows], sent.at[index]))
+                copies[-1].start()
+    for copy in copies:
+        copy.wait()
 
 
 SMEM = pl.BlockSpec(memory_space=pltpu.SMEM)
 VMEM = pl.BlockSpec(memory_space=pltpu.VMEM)
+
+
+def kept(shape, dtype):
+    return pltpu.VMEM(shape, dtype)
+
+
+def near(value):
+    return pltpu.with_memory_space_constraint(value, pltpu.VMEM)
 
 
 def shards(tiles, freqs, field_count, fields, slot_tile_ids, neighbour_tile_ids, neighbour_rotation_code, paired_tile_ids):
@@ -290,27 +300,27 @@
     def swap(value, axes, count, step):
         return lax.ppermute(value, axes, [(i, i ^ step) for i in range(count)])
 
-    piece = pltpu.VMEM((2 * rows + CORNER_ROWS, LANES), jnp.bfloat16)
+    piece = kept((2 * rows + CORNER_ROWS, LANES), jnp.bfloat16)
     pieces = pl.pallas_call(
         functools.partial(transform_kernel, devices),
         out_shape=[piece] * devices,
-        in_specs=[SMEM] + [VMEM] * 8,
+        in_specs=[SMEM] + [VMEM] * 6,
         out_specs=[VMEM] * devices,
-        scratch_shapes=[pltpu.VMEM((samples, 2 * LANES), jnp.float32)],
         name="transform",
     )(place, field, *cell_tables(), *time_tables(devices, samples))
     pieces = [pieces[0]] + [
         swap(pieces[step], ("freq", "field"), devices, step) for step in range(1, devices)
     ]
 
-    cell_map, corner_map = pl.pallas_call(
+    cell_map, corner_map, chosen = pl.pallas_call(
         placement_kernel,
         out_shape=[
-            pltpu.VMEM((tiles * LANES, (1 + partners) * LANES), jnp.bfloat16),
-            pltpu.VMEM((tiles * CORNER_ROWS, (1 + partners) * LANES), jnp.bfloat16),
+            kept((tiles * LANES, (1 + partners) * LANES), jnp.bfloat16),
+            kept((tiles * CORNER_ROWS, (1 + partners) * LANES), jnp.bfloat16),
+            kept((tiles + -tiles % 8, partners * LANES), jnp.float32),
         ],
         in_specs=[SMEM] * 5,
-        out_specs=[VMEM] * 2,
+        out_specs=[VMEM] * 3,
         scratch_shapes=[
             pltpu.SMEM((tiles,), jnp.int32),
             pltpu.VMEM((tiles * LANES, (1 + partners) * LANES), jnp.float32),
@@ -322,8 +332,8 @@
     band, height = pl.pallas_call(
         functools.partial(collect_kernel, devices),
         out_shape=[
-            pltpu.VMEM((3 * total + CORNER_ROWS, LANES), jnp.bfloat16),
-            pltpu.VMEM((total, LANES), jnp.bfloat16),
+            kept((3 * total + CORNER_ROWS, LANES), jnp.bfloat16),
+            kept((total, LANES), jnp.bfloat16),
         ],
         in_specs=[SMEM] + [VMEM] * devices,
         out_specs=[VMEM] * 2,
@@ -334,24 +344,19 @@
 
     segments = freqs * samples // SEGLEN
     scale = 1.0 / (segments * SEGLEN * 0.375)
-    step_freqs = 2
-    block = (1, partners, 2, step_freqs, LANES, LANES)
-    return pl.pallas_call(
-        functools.partial(density_kernel, tiles, scale, per_band),
-        out_shape=jax.ShapeDtypeStruct((1, partners, 2, per_band, LANES, LANES), jnp.float32),
-        grid=(per_band // step_freqs,),
-        in_specs=[SMEM] * 3 + [VMEM] * (3 + tiles),
-        out_specs=pl.BlockSpec(block, lambda i: (0, 0, 0, i, 0, 0)),
+    blocks = partners * 2 * per_band
+    density = pl.pallas_call(
+        functools.partial(density_kernel, tiles, partners, scale, per_band),
+        out_shape=jax.ShapeDtypeStruct((blocks * LANES, LANES), jnp.float32),
+        in_specs=[VMEM] * (4 + tiles),
+        out_specs=pl.BlockSpec(memory_space=pl.ANY),
         scratch_shapes=[
-            pltpu.VMEM((2 * LANES, total), jnp.float32),
-            pltpu.VMEM((total, partners * LANES), jnp.bfloat16),
+            pltpu.VMEM((blocks * LANES, LANES), jnp.float32),
+            pltpu.SemaphoreType.DMA((blocks,)),
         ],
         name="density",
-    )(tile, slot_tile_ids, paired_tile_ids, *map(near, (height, cell_map, corner_map, *bands)))
-
-
-def near(value):
-    return pltpu.with_memory_space_constraint(value, pltpu.VMEM)
+    )(*map(near, (height, cell_map, corner_map, chosen, *bands)))
+    return density.reshape(1, partners, 2, per_band, LANES, LANES)
 
 
 def solution(mesh):

time: 20.3 us -> 19 us (0.936)
  Pallas kernels: 6.65 us -> 5.25 us
    pallas_call x3, Pallas kernels: 4.78 us -> 3.58 us  [the longest x1 2.05 us: shards(): pl.pallas_call(functools.partial(density_kernel, tiles, partners, scale,...]
    pallas_call x1, Pallas kernels: 1.87 us -> 1.66 us  [shards(): pl.pallas_call(functools.partial(transform_kernel, devices), out_shape=[p...]
  transfers between devices with their start and end apart: 6 -> 6, of which waited for: 4 -> 4; matrix products, arithmetic and copies ran while one was open for 0% -> 0% of each run, Pallas kernels for 7% -> 8%
where the time goes in v3:
time: 19 us; the launch traced here: 18.8 us
  starting transfers between devices  7.6 us (40%)
  waiting for transfers between devices  5.95 us (31%)
  Pallas kernels  5.25 us (28%)
    ppermute x6, starting transfers between devices, swap(): return lax.ppermute(value, axes, [(i, i ^ step) for i in range(count)])  7.6 us
    ppermute x6, waiting for transfers between devices, swap(): return lax.ppermute(value, axes, [(i, i ^ step) for i in range(count)])  5.95 us
    pallas_call x1, Pallas kernels, shards(): pl.pallas_call(functools.partial(density_kernel, tiles, partners, scale,...  2.05 us
    pallas_call x1, Pallas kernels, shards(): pl.pallas_call(functools.partial(transform_kernel, devices), out_shape=[p...  1.66 us
    pallas_call x1, Pallas kernels, shards(): pl.pallas_call(placement_kernel, out_shape=[kept((tiles * LANES, (1 + par...  1.5 us
  transfers between devices with their start and end apart: 6, of which 4 were waited for; matrix products, arithmetic and copies ran while one was open for 0% of the time, Pallas kernels for 8%

profile of v3, /device:TPU:0, one launch (start us, length us, event | category | flops | bytes accessed | tf_op | source)
XLA Modules:
  0.0 18.8 jit_solution(847151127817578082)
XLA Ops:
  0.0 1.7 %transform.1 = (bf16[80,128]{1,0:T(8,128)(2,1)S(1)}, bf16[80,128]{1,0:T(8,128)(2,1)S(1)}, bf16[80,128]{1,0:T(8,128)(2,1)S(1)}, bf16[80,128]{1,0:T(8,128)(2,1)S(1)}) custom-call(s32[1]{0:T(128)} %bitcast.place_ref, bf16[128,1024]{1,0:T(8,128)(2,1)} %bitcast.4, bf16[1024,256]{1,0:T(8,128)(2,1)} %constant.23.clone.cells_ref, ...), custom_call_target="tpu_custom_call" | custom-call | tf_op jit(solution)/shard_map/transform/pallas_call | solution.py:304
  1.7 0.5 %collective-permute-start = (bf16[80,128]{1,0:T(8,128)(2,1)S(1)}, bf16[80,128]{1,0:T(8,128)(2,1)S(1)}, u32[]{:S(2)}, u32[]{:S(2)}) collective-permute-start(bf16[80,128]{1,0:T(8,128)(2,1)S(1)} %get-tuple-element.15), channel_id=1, source_target_pairs={{0,1},{1,0},{2,3},{3,2},{4,5},{5,4},{6,7},{7,6},{8,9},{9,8},{10,11... | collective-permute-start | bytes 61448 | tf_op jit(solution)/shard_map/ppermute | solution.py:301
  2.2 2.6 %collective-permute-start.1 = (bf16[80,128]{1,0:T(8,128)(2,1)S(1)}, bf16[80,128]{1,0:T(8,128)(2,1)S(1)}, u32[]{:S(2)}, u32[]{:S(2)}) collective-permute-start(bf16[80,128]{1,0:T(8,128)(2,1)S(1)} %get-tuple-element.16), channel_id=1, source_target_pairs={{0,2},{1,3},{2,0},{3,1},{4,6},{5,7},{6,4},{7,5},{8,10},{9,11},{10,... | collective-permute-start | bytes 61448 | tf_op jit(solution)/shard_map/ppermute | solution.py:301
  4.8 0.1 collective-permute-start.2
  4.8 0.0 collective-permute-done.rest_1_
  4.8 1.7 %collective-permute-done.1.rest_2_ = bf16[80,128]{1,0:T(8,128)(2,1)S(1)} collective-permute-done((bf16[80,128]{1,0:T(8,128)(2,1)S(1)}, bf16[80,128]{1,0:T(8,128)(2,1)S(1)}, u32[]{:S(2)}, u32[]{:S(2)}) %collective-permute-start.1) | collective-permute-done | bytes 20512 | tf_op jit(solution)/shard_map/ppermute | solution.py:301
  6.5 1.4 %collective-permute-done.2.rest_3_ = bf16[80,128]{1,0:T(8,128)(2,1)S(1)} collective-permute-done((bf16[80,128]{1,0:T(8,128)(2,1)S(1)}, bf16[80,128]{1,0:T(8,128)(2,1)S(1)}, u32[]{:S(2)}, u32[]{:S(2)}) %collective-permute-start.2) | collective-permute-done | bytes 20512 | tf_op jit(solution)/shard_map/ppermute | solution.py:301
  8.0 3.7 %collective-permute-start.5 = (bf16[208,128]{1,0:T(8,128)(2,1)S(1)}, bf16[208,128]{1,0:T(8,128)(2,1)S(1)}, u32[]{:S(2)}, u32[]{:S(2)}) collective-permute-start(bf16[208,128]{1,0:T(8,128)(2,1)S(1)} %get-tuple-element.22.rest_0_), channel_id=1, source_target_pairs={{0,12},{4,8},{8,4},{12,0},{1,13},{5,9},{9,5},{13,1},{2,14},{6,10},... | collective-permute-start | bytes 159752 | tf_op jit(solution)/shard_map/ppermute | solution.py:301
  11.7 0.0 collective-permute-start.4
  11.7 0.8 %collective-permute-start.3 = (bf16[208,128]{1,0:T(8,128)(2,1)S(1)}, bf16[208,128]{1,0:T(8,128)(2,1)S(1)}, u32[]{:S(2)}, u32[]{:S(2)}) collective-permute-start(bf16[208,128]{1,0:T(8,128)(2,1)S(1)} %get-tuple-element.22.rest_0_), channel_id=1, source_target_pairs={{0,4},{4,0},{8,12},{12,8},{1,5},{5,1},{9,13},{13,9},{2,6},{6,2},{1... | collective-permute-start | bytes 159752 | tf_op jit(solution)/shard_map/ppermute | solution.py:301
  12.5 1.5 %placement.1 = (bf16[512,384]{1,0:T(8,128)(2,1)S(1)}, bf16[64,384]{1,0:T(8,128)(2,1)S(1)}, f32[8,256]{1,0:T(8,128)S(1)}) custom-call(s32[1]{0:T(128)} %bitcast.2.tile_ref, s32[4]{0:T(128)} %ids_ref.1, s32[4,4]{1,0:T(4,128)} %near_ids_ref.1, s32[4,4]{1,0:T(4,128)} %codes_ref.1, s32[1,2]{1,0:T(1,128)} %paired_ref.1), custom_call_target="tpu_custom_call" | custom-call | tf_op jit(solution)/shard_map/placement/pallas_call | solution.py:315
  14.0 0.1 collective-permute-done.5.rest_3_
  14.1 2.7 %collective-permute-done.4.rest_2_ = bf16[208,128]{1,0:T(8,128)(2,1)S(1)} collective-permute-done((bf16[208,128]{1,0:T(8,128)(2,1)S(1)}, bf16[208,128]{1,0:T(8,128)(2,1)S(1)}, u32[]{:S(2)}, u32[]{:S(2)}) %collective-permute-start.4) | collective-permute-done | bytes 53280 | tf_op jit(solution)/shard_map/ppermute | solution.py:301
  16.8 0.0 collective-permute-done.3.rest_1_
  16.8 2.1 %density.1 = f32[4096,128]{1,0:T(8,128)} custom-call(bf16[64,128]{1,0:T(8,128)(2,1)S(1)} %get-tuple-element.18.height_ref, bf16[512,384]{1,0:T(8,128)(2,1)S(1)} %get-tuple-element.19.map_ref, bf16[64,384]{1,0:T(8,128)(2,1)S(1)} %get-tuple-element.20.corner_map_ref, f32[8,256]{1,0:T(8,128)S(1)} %get-tuple-element.21.chosen_ref, ...), custom_call_target="tpu_custom_call" | custom-call | tf_op jit(solution)/shard_map/density/pallas_call | solution.py:348
  (1 shorter events, 0.0 us)
Async XLA Ops:
  1.7 3.2 %collective-permute-start = (bf16[80,128]{1,0:T(8,128)(2,1)S(1)}, bf16[80,128]{1,0:T(8,128)(2,1)S(1)}, u32[]{:S(2)}, u32[]{:S(2)}) collective-permute-start(bf16[80,128]{1,0:T(8,128)(2,1)S(1)} %get-tuple-element.15), channel_id=1, source_target_pairs={{0,1},{1,0},{2,3},{3,2},{4,5},{5,4},{6,7},{7,6},{8,9},{9,8},{10,11... | collective-permute-start | bytes 61448 | tf_op jit(solution)/shard_map/ppermute | solution.py:301
  2.2 4.3 %collective-permute-start.1 = (bf16[80,128]{1,0:T(8,128)(2,1)S(1)}, bf16[80,128]{1,0:T(8,128)(2,1)S(1)}, u32[]{:S(2)}, u32[]{:S(2)}) collective-permute-start(bf16[80,128]{1,0:T(8,128)(2,1)S(1)} %get-tuple-element.16), channel_id=1, source_target_pairs={{0,2},{1,3},{2,0},{3,1},{4,6},{5,7},{6,4},{7,5},{8,10},{9,11},{10,... | collective-permute-start | bytes 61448 | tf_op jit(solution)/shard_map/ppermute | solution.py:301
  4.8 3.2 %collective-permute-start.2 = (bf16[80,128]{1,0:T(8,128)(2,1)S(1)}, bf16[80,128]{1,0:T(8,128)(2,1)S(1)}, u32[]{:S(2)}, u32[]{:S(2)}) collective-permute-start(bf16[80,128]{1,0:T(8,128)(2,1)S(1)} %get-tuple-element.17), channel_id=1, source_target_pairs={{0,3},{1,2},{2,1},{3,0},{4,7},{5,6},{6,5},{7,4},{8,11},{9,10},{10,... | collective-permute-start | bytes 61448 | tf_op jit(solution)/shard_map/ppermute | solution.py:301
  8.0 6.1 %collective-permute-start.5 = (bf16[208,128]{1,0:T(8,128)(2,1)S(1)}, bf16[208,128]{1,0:T(8,128)(2,1)S(1)}, u32[]{:S(2)}, u32[]{:S(2)}) collective-permute-start(bf16[208,128]{1,0:T(8,128)(2,1)S(1)} %get-tuple-element.22.rest_0_), channel_id=1, source_target_pairs={{0,12},{4,8},{8,4},{12,0},{1,13},{5,9},{9,5},{13,1},{2,14},{6,10},... | collective-permute-start | bytes 159752 | tf_op jit(solution)/shard_map/ppermute | solution.py:301
  11.7 5.1 %collective-permute-start.4 = (bf16[208,128]{1,0:T(8,128)(2,1)S(1)}, bf16[208,128]{1,0:T(8,128)(2,1)S(1)}, u32[]{:S(2)}, u32[]{:S(2)}) collective-permute-start(bf16[208,128]{1,0:T(8,128)(2,1)S(1)} %get-tuple-element.22.rest_0_), channel_id=1, source_target_pairs={{0,8},{4,12},{8,0},{12,4},{1,9},{5,13},{9,1},{13,5},{2,10},{6,14},... | collective-permute-start | bytes 159752 | tf_op jit(solution)/shard_map/ppermute | solution.py:301
  11.7 5.1 %collective-permute-start.3 = (bf16[208,128]{1,0:T(8,128)(2,1)S(1)}, bf16[208,128]{1,0:T(8,128)(2,1)S(1)}, u32[]{:S(2)}, u32[]{:S(2)}) collective-permute-start(bf16[208,128]{1,0:T(8,128)(2,1)S(1)} %get-tuple-element.22.rest_0_), channel_id=1, source_target_pairs={{0,4},{4,0},{8,12},{12,8},{1,5},{5,1},{9,13},{13,9},{2,6},{6,2},{1... | collective-permute-start | bytes 159752 | tf_op jit(solution)/shard_map/ppermute | solution.py:301

commit v4 on v3

--- a/solution.py
+++ b/solution.py
@@ -25,6 +25,26 @@
     ((WEST, 1), (EAST, 1)),
     ((NORTH, 0), (SOUTH, 0)),
 )
+
+BAND_ROUTES = ((1, 3, 0, 2), (3, 2, 1, 0), (2, 0, 3, 1))
+TILE_ROUTES = ((1, 2, 0, 3), (2, 3, 1, 0), (3, 0, 2, 1), (0, 1, 3, 2))
+
+
+def routes_for(count, preferred):
+    if len(preferred[0]) == count:
+        return preferred
+    return tuple(tuple(i ^ step for i in range(count)) for step in range(1, count))
+
+
+def senders(route):
+    return tuple(route.index(i) for i in range(len(route)))
+
+
+def look_up(table, index):
+    value = jnp.int32(table[0])
+    for i in range(1, len(table)):
+        value = jnp.where(index == i, table[i], value)
+    return value
 
 
 def split_bf16(values):
@@ -88,32 +108,35 @@
         table[:, segment, :, :, segment, :] = waves.reshape(2, bands, per_band, SEGLEN).transpose(1, 0, 2, 3)
     table = table.reshape(bands * segments * 2 * per_band, samples)
     high, low = split_bf16(table)
-    return high, low
+    return np.concatenate([high, high, low], axis=1)
 
 
 def dot(left, right):
     return jnp.dot(left, right, preferred_element_type=jnp.float32)
 
 
-def transform_kernel(devices, place_ref, x_ref, cells_ref, first_ref, last_ref, high_ref, low_ref, *outs):
+def transform_kernel(routes, place_ref, x_ref, cells_ref, first_ref, last_ref, waves_ref, *outs):
     place = place_ref[0]
-    rows = high_ref.shape[0] // devices
-    starts = [pl.multiple_of(jnp.bitwise_xor(place, step) * rows, rows) for step in range(devices)]
-    high = jnp.concatenate([high_ref[pl.ds(start, rows), :] for start in starts], axis=0)
-    low = jnp.concatenate([low_ref[pl.ds(start, rows), :] for start in starts], axis=0)
+    devices = len(outs)
+    rows = waves_ref.shape[0] // devices
+    bands = [place] + [look_up(route, place) for route in routes]
+    waves = jnp.concatenate(
+        [waves_ref[pl.ds(pl.multiple_of(band * rows, rows), rows), :] for band in bands], axis=0
+    )
     across = (((1,), (1,)), ((), ()))
     x = x_ref[...]
+    samples = x.shape[0]
     corners = lax.dot_general(first_ref[...], x[:, :LANES], across, preferred_element_type=jnp.float32)
     corners += lax.dot_general(
         last_ref[...], x[:, SIDE * SIDE - LANES :], across, preferred_element_type=jnp.float32
     )
     corners = corners.astype(jnp.bfloat16)
-    corner_spectra = lax.dot_general(corners, high, across, preferred_element_type=jnp.float32)
-    corner_spectra += lax.dot_general(corners, low, across, preferred_element_type=jnp.float32)
+    corners = jnp.concatenate([corners, corners], axis=1)
+    corner_spectra = lax.dot_general(corners, waves[:, samples:], across, preferred_element_type=jnp.float32)
     sums = dot(x, cells_ref[...])
     sums_high = sums.astype(jnp.bfloat16)
     sums_low = (sums - sums_high.astype(jnp.float32)).astype(jnp.bfloat16)
-    spectra = dot(high, sums_high) + (dot(high, sums_low) + dot(low, sums_high))
+    spectra = dot(waves, jnp.concatenate([sums_low, sums_high, sums_high], axis=0))
     spectra = spectra.astype(jnp.bfloat16)
     lane_start = (place % 2) * (LANES // 2) + (place // 2) * rows
     lane = lax.broadcasted_iota(jnp.int32, (CORNER_ROWS, LANES), 1)
@@ -126,14 +149,15 @@
         outs[step][2 * rows : 2 * rows + CORNER_ROWS, :] = jnp.where(mine, turned, 0.0).astype(jnp.bfloat16)
 
 
-def collect_kernel(devices, place_ref, *rest):
+def collect_kernel(routes, place_ref, *rest):
+    devices = len(routes) + 1
     blocks, (band_ref, height_ref, held_ref) = rest[:devices], rest[devices:]
     place = place_ref[0]
     rows = (blocks[0].shape[0] - CORNER_ROWS) // 2
     total = height_ref.shape[0]
     corners = jnp.zeros((CORNER_ROWS, LANES), jnp.float32)
     for step in range(devices):
-        source = jnp.bitwise_xor(place, step)
+        source = look_up(senders(routes[step - 1]), place) if step else place
         field, half = source % 2, source // 2
         start = pl.multiple_of(field * total + half * rows, rows)
         held_ref[pl.ds(start, rows), :] = blocks[step][0:rows, :]
@@ -145,6 +169,7 @@
 
 
 def placement_kernel(
+    routes,
     tile_ref,
     ids_ref,
     near_ids_ref,
@@ -154,6 +179,7 @@
     corner_map_ref,
     chosen_ref,
     slot_ref,
+    arrival_ref,
     wide_ref,
     corner_ref,
 ):
@@ -165,6 +191,12 @@
         return carry
 
     lax.fori_loop(0, slots, invert, 0, unroll=slots <= 8)
+    for sender in range(len(routes[0])):
+        steps = [0] * len(routes[0])
+        for step, route in enumerate(routes):
+            if route[sender] != sender:
+                steps[route[sender]] = step + 1
+        arrival_ref[sender] = look_up(steps, tile)
     wide_ref[...] = jnp.zeros_like(wide_ref)
     corner_ref[...] = jnp.zeros_like(corner_ref)
     block = lax.broadcasted_iota(jnp.int32, (BLOCKS, LANES), 0)
@@ -193,14 +225,14 @@
             code = codes_ref[slot, edge]
             touching, reverse = code % 4, code // 4
             pattern = (cell == target(edge, turn(block, reverse))).astype(jnp.float32)
-            start = pl.multiple_of(jnp.bitwise_xor(tile, near) * LANES + touching * BLOCKS, BLOCKS)
+            start = pl.multiple_of(arrival_ref[near] * LANES + touching * BLOCKS, BLOCKS)
             wide_ref[pl.ds(start, BLOCKS), columns] += pattern
             beyond = slot_ref[near_ids_ref[near, touching]]
             beyond_code = codes_ref[near, touching]
             reverse_both = jnp.bitwise_xor(reverse, beyond_code // 4)
             pattern = (cell == target(edge, turn(block, reverse_both))).astype(jnp.float32)
             start = pl.multiple_of(
-                jnp.bitwise_xor(tile, beyond) * LANES + 4 * BLOCKS + (beyond_code % 4) * BLOCKS, BLOCKS
+                arrival_ref[beyond] * LANES + 4 * BLOCKS + (beyond_code % 4) * BLOCKS, BLOCKS
             )
             wide_ref[pl.ds(start, BLOCKS), columns] += pattern
             for end in range(2):
@@ -220,20 +252,20 @@
                         )
                 position = turn((BLOCKS - 1) * end, reverse)
                 hit = (corner_row == corner) & (corner_cell == target(edge, position))
-                start = pl.multiple_of(jnp.bitwise_xor(tile, other) * CORNER_ROWS, CORNER_ROWS)
+                start = pl.multiple_of(arrival_ref[other] * CORNER_ROWS, CORNER_ROWS)
                 corner_ref[pl.ds(start, CORNER_ROWS), columns] += hit.astype(jnp.float32)
     step = lax.broadcasted_iota(jnp.int32, (chosen_ref.shape[0], LANES), 0)
     for partner in range(partners):
-        wanted_step = jnp.bitwise_xor(tile, wanted[1 + partner])
+        wanted_step = arrival_ref[wanted[1 + partner]]
         chosen_ref[:, partner * LANES : (partner + 1) * LANES] = (step == wanted_step).astype(jnp.float32)
     map_ref[...] = wide_ref[...].astype(jnp.bfloat16)
     corner_map_ref[...] = corner_ref[...].astype(jnp.bfloat16)
 
 
 def density_kernel(
-    tiles, partners, scale, per_band, height_ref, map_ref, corner_map_ref, chosen_ref, *rest
+    arrivals, partners, scale, per_band, height_ref, map_ref, corner_map_ref, chosen_ref, *rest
 ):
-    bands, (out_ref, cross_ref, sent) = rest[:tiles], rest[tiles:]
+    bands, (out_ref, cross_ref, sent) = (rest[0], *rest[arrivals - 1 : 0 : -1]), rest[arrivals:]
     total = height_ref.shape[0]
     height_rims = jnp.concatenate([band[total : 2 * total, :] for band in bands], axis=1)
     velocity_rims = jnp.concatenate([band[2 * total : 3 * total, :] for band in bands], axis=1)
@@ -244,7 +276,7 @@
     height = height_ref[...].astype(jnp.float32) + dot(height_rims, map_ref[:, :LANES])
     height = height + corner_part[:total, :LANES]
     velocity = dot(velocity_rims, map_ref[:, LANES:]) + corner_part[total:, LANES:]
-    for step in range(tiles):
+    for step in range(arrivals):
         own = bands[step][0:total, :].astype(jnp.float32)
         velocity += jnp.concatenate([own] * partners, axis=1) * chosen_ref[step : step + 1, :]
     velocity = velocity.astype(jnp.bfloat16)
@@ -297,40 +329,43 @@
     tile = lax.axis_index("tiles").astype(jnp.int32).reshape(1)
     place = (lax.axis_index("freq") * field_count + lax.axis_index("field")).astype(jnp.int32).reshape(1)
 
-    def swap(value, axes, count, step):
-        return lax.ppermute(value, axes, [(i, i ^ step) for i in range(count)])
+    band_routes = routes_for(devices, BAND_ROUTES)
+    tile_routes = routes_for(tiles, TILE_ROUTES)
+    arrivals = len(tile_routes) + 1
 
     piece = kept((2 * rows + CORNER_ROWS, LANES), jnp.bfloat16)
     pieces = pl.pallas_call(
-        functools.partial(transform_kernel, devices),
+        functools.partial(transform_kernel, band_routes),
         out_shape=[piece] * devices,
-        in_specs=[SMEM] + [VMEM] * 6,
+        in_specs=[SMEM] + [VMEM] * 5,
         out_specs=[VMEM] * devices,
         name="transform",
-    )(place, field, *cell_tables(), *time_tables(devices, samples))
+    )(place, field, *cell_tables(), time_tables(devices, samples))
     pieces = [pieces[0]] + [
-        swap(pieces[step], ("freq", "field"), devices, step) for step in range(1, devices)
+        lax.ppermute(piece, ("freq", "field"), list(enumerate(route)))
+        for piece, route in zip(pieces[1:], band_routes)
     ]
 
     cell_map, corner_map, chosen = pl.pallas_call(
-        placement_kernel,
+        functools.partial(placement_kernel, tile_routes),
         out_shape=[
-            kept((tiles * LANES, (1 + partners) * LANES), jnp.bfloat16),
-            kept((tiles * CORNER_ROWS, (1 + partners) * LANES), jnp.bfloat16),
-            kept((tiles + -tiles % 8, partners * LANES), jnp.float32),
+            kept((arrivals * LANES, (1 + partners) * LANES), jnp.bfloat16),
+            kept((arrivals * CORNER_ROWS, (1 + partners) * LANES), jnp.bfloat16),
+            kept((arrivals + -arrivals % 8, partners * LANES), jnp.float32),
         ],
         in_specs=[SMEM] * 5,
         out_specs=[VMEM] * 3,
         scratch_shapes=[
             pltpu.SMEM((tiles,), jnp.int32),
-            pltpu.VMEM((tiles * LANES, (1 + partners) * LANES), jnp.float32),
-            pltpu.VMEM((tiles * CORNER_ROWS, (1 + partners) * LANES), jnp.float32),
+            pltpu.SMEM((tiles,), jnp.int32),
+            pltpu.VMEM((arrivals * LANES, (1 + partners) * LANES), jnp.float32),
+            pltpu.VMEM((arrivals * CORNER_ROWS, (1 + partners) * LANES), jnp.float32),
         ],
         name="placement",
     )(tile, slot_tile_ids, neighbour_tile_ids, neighbour_rotation_code, paired_tile_ids)
 
     band, height = pl.pallas_call(
-        functools.partial(collect_kernel, devices),
+        functools.partial(collect_kernel, band_routes),
         out_shape=[
             kept((3 * total + CORNER_ROWS, LANES), jnp.bfloat16),
             kept((total, LANES), jnp.bfloat16),
@@ -340,15 +375,22 @@
         scratch_shapes=[pltpu.VMEM((4 * total, LANES), jnp.bfloat16)],
         name="collect",
     )(place, *map(near, pieces))
-    bands = [band] + [swap(band, "tiles", tiles, step) for step in range(1, tiles)]
+    bands = [band]
+    for route in tile_routes[::-1]:
+        pairs = []
+        for sender, receiver in enumerate(route):
+            for core in range(field_count):
+                there = receiver * field_count + (core if receiver != sender else field_count - 1 - core)
+                pairs.append((sender * field_count + core, there))
+        bands.append(lax.ppermute(band, ("tiles", "field"), pairs))
 
     segments = freqs * samples // SEGLEN
     scale = 1.0 / (segments * SEGLEN * 0.375)
     blocks = partners * 2 * per_band
     density = pl.pallas_call(
-        functools.partial(density_kernel, tiles, partners, scale, per_band),
+        functools.partial(density_kernel, arrivals, partners, scale, per_band),
         out_shape=jax.ShapeDtypeStruct((blocks * LANES, LANES), jnp.float32),
-        in_specs=[VMEM] * (4 + tiles),
+        in_specs=[VMEM] * (4 + arrivals),
         out_specs=pl.BlockSpec(memory_space=pl.ANY),
         scratch_shapes=[
             pltpu.VMEM((blocks * LANES, LANES), jnp.float32),

time: 19 us -> 17.9 us (0.942)
  waiting for transfers between devices: 5.95 us -> 2.69 us
  starting transfers between devices: 7.6 us -> 9.59 us
    ppermute x6 -> x7, waiting for transfers between devices: 5.95 us -> 2.69 us  [the longest x3 1.48 us: shards(): lax.ppermute(piece, ('freq', 'field'), list(enumerate(route)))]
    ppermute x6 -> x7, starting transfers between devices: 7.6 us -> 9.59 us  [the longest x4 5.46 us: shards(): bands.append(lax.ppermute(band, ('tiles', 'field'), pairs))]
  transfers between devices with their start and end apart: 6 -> 7, of which waited for: 4 -> 4; matrix products, arithmetic and copies ran while one was open for 0% -> 0% of each run, Pallas kernels for 8% -> 8%
where the time goes in v4:
time: 17.9 us; the launch traced here: 17.7 us
  starting transfers between devices  9.59 us (54%)
  Pallas kernels  5.42 us (30%)
  waiting for transfers between devices  2.69 us (15%)
    ppermute x4, starting transfers between devices, shards(): bands.append(lax.ppermute(band, ('tiles', 'field'), pairs))  5.46 us
    ppermute x3, starting transfers between devices, shards(): lax.ppermute(piece, ('freq', 'field'), list(enumerate(route)))  4.14 us
    pallas_call x1, Pallas kernels, shards(): pl.pallas_call(functools.partial(density_kernel, arrivals, partners, scal...  2.07 us
    pallas_call x1, Pallas kernels, shards(): pl.pallas_call(functools.partial(transform_kernel, band_routes), out_shap...  1.83 us
    pallas_call x1, Pallas kernels, shards(): pl.pallas_call(functools.partial(placement_kernel, tile_routes), out_shap...  1.5 us
    ppermute x3, waiting for transfers between devices, shards(): lax.ppermute(piece, ('freq', 'field'), list(enumerate(route)))  1.48 us
    ppermute x4, waiting for transfers between devices, shards(): bands.append(lax.ppermute(band, ('tiles', 'field'), pairs))  1.21 us
  transfers between devices with their start and end apart: 7, of which 4 were waited for; matrix products, arithmetic and copies ran while one was open for 0% of the time, Pallas kernels for 8%

profile of v4, /device:TPU:0, one launch (start us, length us, event | category | flops | bytes accessed | tf_op | source)
XLA Modules:
  0.0 17.7 jit_solution(10520919674870086344)
XLA Ops:
  0.0 1.8 %transform.1 = (bf16[80,128]{1,0:T(8,128)(2,1)S(1)}, bf16[80,128]{1,0:T(8,128)(2,1)S(1)}, bf16[80,128]{1,0:T(8,128)(2,1)S(1)}, bf16[80,128]{1,0:T(8,128)(2,1)S(1)}) custom-call(s32[1]{0:T(128)} %bitcast.place_ref, bf16[128,1024]{1,0:T(8,128)(2,1)} %bitcast.4, bf16[1024,256]{1,0:T(8,128)(2,1)} %constant.21.clone.cells_ref, ...), custom_call_target="tpu_custom_call" | custom-call | tf_op jit(solution)/shard_map/transform/pallas_call | solution.py:337
  1.8 0.5 %collective-permute-start = (bf16[80,128]{1,0:T(8,128)(2,1)S(1)}, bf16[80,128]{1,0:T(8,128)(2,1)S(1)}, u32[]{:S(2)}, u32[]{:S(2)}) collective-permute-start(bf16[80,128]{1,0:T(8,128)(2,1)S(1)} %get-tuple-element.15), channel_id=1, source_target_pairs={{0,1},{1,3},{2,0},{3,2},{4,5},{5,7},{6,4},{7,6},{8,9},{9,11},{10,8... | collective-permute-start | bytes 61448 | tf_op jit(solution)/shard_map/ppermute | solution.py:345
  2.3 2.6 %collective-permute-start.1 = (bf16[80,128]{1,0:T(8,128)(2,1)S(1)}, bf16[80,128]{1,0:T(8,128)(2,1)S(1)}, u32[]{:S(2)}, u32[]{:S(2)}) collective-permute-start(bf16[80,128]{1,0:T(8,128)(2,1)S(1)} %get-tuple-element.16), channel_id=1, source_target_pairs={{0,3},{1,2},{2,1},{3,0},{4,7},{5,6},{6,5},{7,4},{8,11},{9,10},{10,... | collective-permute-start | bytes 61448 | tf_op jit(solution)/shard_map/ppermute | solution.py:345
  4.9 1.1 %collective-permute-start.2 = (bf16[80,128]{1,0:T(8,128)(2,1)S(1)}, bf16[80,128]{1,0:T(8,128)(2,1)S(1)}, u32[]{:S(2)}, u32[]{:S(2)}) collective-permute-start(bf16[80,128]{1,0:T(8,128)(2,1)S(1)} %get-tuple-element.17), channel_id=1, source_target_pairs={{0,2},{1,0},{2,3},{3,1},{4,6},{5,4},{6,7},{7,5},{8,10},{9,8},{10,1... | collective-permute-start | bytes 61448 | tf_op jit(solution)/shard_map/ppermute | solution.py:345
  6.0 0.6 %collective-permute-done.rest_1_ = bf16[80,128]{1,0:T(8,128)(2,1)S(1)} collective-permute-done((bf16[80,128]{1,0:T(8,128)(2,1)S(1)}, bf16[80,128]{1,0:T(8,128)(2,1)S(1)}, u32[]{:S(2)}, u32[]{:S(2)}) %collective-permute-start) | collective-permute-done | bytes 20512 | tf_op jit(solution)/shard_map/ppermute | solution.py:345
  6.6 0.0 collective-permute-done.1.rest_2_
  6.6 0.9 %collective-permute-done.2.rest_3_ = bf16[80,128]{1,0:T(8,128)(2,1)S(1)} collective-permute-done((bf16[80,128]{1,0:T(8,128)(2,1)S(1)}, bf16[80,128]{1,0:T(8,128)(2,1)S(1)}, u32[]{:S(2)}, u32[]{:S(2)}) %collective-permute-start.2) | collective-permute-done | bytes 20512 | tf_op jit(solution)/shard_map/ppermute | solution.py:345
  7.5 1.6 %collective-permute-start.6 = (bf16[208,128]{1,0:T(8,128)(2,1)S(1)}, bf16[208,128]{1,0:T(8,128)(2,1)S(1)}, u32[]{:S(2)}, u32[]{:S(2)}) collective-permute-start(bf16[208,128]{1,0:T(8,128)(2,1)S(1)} %get-tuple-element.22.rest_0_), channel_id=1, source_target_pairs={{0,4},{1,5},{4,8},{5,9},{8,0},{9,1},{12,13},{13,12},{2,6},{3,7},{6... | collective-permute-start | bytes 159752 | tf_op jit(solution)/shard_map/ppermute | solution.py:385
  9.1 1.3 %collective-permute-start.5 = (bf16[208,128]{1,0:T(8,128)(2,1)S(1)}, bf16[208,128]{1,0:T(8,128)(2,1)S(1)}, u32[]{:S(2)}, u32[]{:S(2)}) collective-permute-start(bf16[208,128]{1,0:T(8,128)(2,1)S(1)} %get-tuple-element.22.rest_0_), channel_id=1, source_target_pairs={{0,8},{1,9},{4,12},{5,13},{8,4},{9,5},{12,0},{13,1},{2,10},{3,11},... | collective-permute-start | bytes 159752 | tf_op jit(solution)/shard_map/ppermute | solution.py:385
  10.5 2.5 %collective-permute-start.4 = (bf16[208,128]{1,0:T(8,128)(2,1)S(1)}, bf16[208,128]{1,0:T(8,128)(2,1)S(1)}, u32[]{:S(2)}, u32[]{:S(2)}) collective-permute-start(bf16[208,128]{1,0:T(8,128)(2,1)S(1)} %get-tuple-element.22.rest_0_), channel_id=1, source_target_pairs={{0,12},{1,13},{4,0},{5,1},{8,9},{9,8},{12,4},{13,5},{2,14},{3,15},... | collective-permute-start | bytes 159752 | tf_op jit(solution)/shard_map/ppermute | solution.py:385
  12.9 0.0 collective-permute-start.3
  12.9 1.5 %placement.1 = (bf16[640,384]{1,0:T(8,128)(2,1)S(1)}, bf16[80,384]{1,0:T(8,128)(2,1)S(1)}, f32[8,256]{1,0:T(8,128)S(1)}) custom-call(s32[1]{0:T(128)} %bitcast.2.tile_ref, s32[4]{0:T(128)} %ids_ref.1, s32[4,4]{1,0:T(4,128)} %near_ids_ref.1, s32[4,4]{1,0:T(4,128)} %codes_ref.1, s32[1,2]{1,0:T(1,128)} %paired_ref.1), custom_call_target="tpu_custom_call" | custom-call | tf_op jit(solution)/shard_map/placement/pallas_call | solution.py:349
  14.4 0.0 collective-permute-done.6.rest_4_
  14.5 0.7 %collective-permute-done.5.rest_3_ = bf16[208,128]{1,0:T(8,128)(2,1)S(1)} collective-permute-done((bf16[208,128]{1,0:T(8,128)(2,1)S(1)}, bf16[208,128]{1,0:T(8,128)(2,1)S(1)}, u32[]{:S(2)}, u32[]{:S(2)}) %collective-permute-start.5) | collective-permute-done | bytes 53280 | tf_op jit(solution)/shard_map/ppermute | solution.py:385
  15.2 0.5 %collective-permute-done.4.rest_2_ = bf16[208,128]{1,0:T(8,128)(2,1)S(1)} collective-permute-done((bf16[208,128]{1,0:T(8,128)(2,1)S(1)}, bf16[208,128]{1,0:T(8,128)(2,1)S(1)}, u32[]{:S(2)}, u32[]{:S(2)}) %collective-permute-start.4) | collective-permute-done | bytes 53280 | tf_op jit(solution)/shard_map/ppermute | solution.py:385
  15.7 0.0 collective-permute-done.3.rest_1_
  15.7 2.1 %density.1 = f32[4096,128]{1,0:T(8,128)} custom-call(bf16[64,128]{1,0:T(8,128)(2,1)S(1)} %get-tuple-element.18.height_ref, bf16[640,384]{1,0:T(8,128)(2,1)S(1)} %get-tuple-element.19.map_ref, bf16[80,384]{1,0:T(8,128)(2,1)S(1)} %get-tuple-element.20.corner_map_ref, f32[8,256]{1,0:T(8,128)S(1)} %get-tuple-element.21.chosen_ref, ...), custom_call_target="tpu_custom_call" | custom-call | tf_op jit(solution)/shard_map/density/pallas_call | solution.py:390
  (1 shorter events, 0.0 us)
Async XLA Ops:
  1.8 4.8 %collective-permute-start = (bf16[80,128]{1,0:T(8,128)(2,1)S(1)}, bf16[80,128]{1,0:T(8,128)(2,1)S(1)}, u32[]{:S(2)}, u32[]{:S(2)}) collective-permute-start(bf16[80,128]{1,0:T(8,128)(2,1)S(1)} %get-tuple-element.15), channel_id=1, source_target_pairs={{0,1},{1,3},{2,0},{3,2},{4,5},{5,7},{6,4},{7,6},{8,9},{9,11},{10,8... | collective-permute-start | bytes 61448 | tf_op jit(solution)/shard_map/ppermute | solution.py:345
  2.3 4.3 %collective-permute-start.1 = (bf16[80,128]{1,0:T(8,128)(2,1)S(1)}, bf16[80,128]{1,0:T(8,128)(2,1)S(1)}, u32[]{:S(2)}, u32[]{:S(2)}) collective-permute-start(bf16[80,128]{1,0:T(8,128)(2,1)S(1)} %get-tuple-element.16), channel_id=1, source_target_pairs={{0,3},{1,2},{2,1},{3,0},{4,7},{5,6},{6,5},{7,4},{8,11},{9,10},{10,... | collective-permute-start | bytes 61448 | tf_op jit(solution)/shard_map/ppermute | solution.py:345
  4.9 2.5 %collective-permute-start.2 = (bf16[80,128]{1,0:T(8,128)(2,1)S(1)}, bf16[80,128]{1,0:T(8,128)(2,1)S(1)}, u32[]{:S(2)}, u32[]{:S(2)}) collective-permute-start(bf16[80,128]{1,0:T(8,128)(2,1)S(1)} %get-tuple-element.17), channel_id=1, source_target_pairs={{0,2},{1,0},{2,3},{3,1},{4,6},{5,4},{6,7},{7,5},{8,10},{9,8},{10,1... | collective-permute-start | bytes 61448 | tf_op jit(solution)/shard_map/ppermute | solution.py:345
  7.5 7.0 %collective-permute-start.6 = (bf16[208,128]{1,0:T(8,128)(2,1)S(1)}, bf16[208,128]{1,0:T(8,128)(2,1)S(1)}, u32[]{:S(2)}, u32[]{:S(2)}) collective-permute-start(bf16[208,128]{1,0:T(8,128)(2,1)S(1)} %get-tuple-element.22.rest_0_), channel_id=1, source_target_pairs={{0,4},{1,5},{4,8},{5,9},{8,0},{9,1},{12,13},{13,12},{2,6},{3,7},{6... | collective-permute-start | bytes 159752 | tf_op jit(solution)/shard_map/ppermute | solution.py:385
  9.1 6.1 %collective-permute-start.5 = (bf16[208,128]{1,0:T(8,128)(2,1)S(1)}, bf16[208,128]{1,0:T(8,128)(2,1)S(1)}, u32[]{:S(2)}, u32[]{:S(2)}) collective-permute-start(bf16[208,128]{1,0:T(8,128)(2,1)S(1)} %get-tuple-element.22.rest_0_), channel_id=1, source_target_pairs={{0,8},{1,9},{4,12},{5,13},{8,4},{9,5},{12,0},{13,1},{2,10},{3,11},... | collective-permute-start | bytes 159752 | tf_op jit(solution)/shard_map/ppermute | solution.py:385
  10.5 5.2 %collective-permute-start.4 = (bf16[208,128]{1,0:T(8,128)(2,1)S(1)}, bf16[208,128]{1,0:T(8,128)(2,1)S(1)}, u32[]{:S(2)}, u32[]{:S(2)}) collective-permute-start(bf16[208,128]{1,0:T(8,128)(2,1)S(1)} %get-tuple-element.22.rest_0_), channel_id=1, source_target_pairs={{0,12},{1,13},{4,0},{5,1},{8,9},{9,8},{12,4},{13,5},{2,14},{3,15},... | collective-permute-start | bytes 159752 | tf_op jit(solution)/shard_map/ppermute | solution.py:385
  12.9 2.7 %collective-permute-start.3 = (bf16[208,128]{1,0:T(8,128)(2,1)S(1)}, bf16[208,128]{1,0:T(8,128)(2,1)S(1)}, u32[]{:S(2)}, u32[]{:S(2)}) collective-permute-start(bf16[208,128]{1,0:T(8,128)(2,1)S(1)} %get-tuple-element.22.rest_0_), channel_id=1, source_target_pairs={{0,1},{1,0},{4,5},{5,4},{8,12},{9,13},{12,8},{13,9},{2,3},{3,2},{6... | collective-permute-start | bytes 159752 | tf_op jit(solution)/shard_map/ppermute | solution.py:385

commit v5 on v4

v5 whole, which is shorter than its diff:
```python
import functools
import math

import jax
import jax.numpy as jnp
import ml_dtypes
import numpy as np
from jax import lax
from jax.experimental import pallas as pl
from jax.experimental.pallas import tpu as pltpu
from jax.sharding import PartitionSpec as P

SIDE = 32
SEGLEN = 64
LANES = 128
BLOCKS = SIDE // 2
CORNER_ROWS = 16
FREQS = SEGLEN // 2

NORTH, EAST, SOUTH, WEST = range(4)
HALF = LANES // 2
RIM_LANES = (0, SIDE // 4, SIDE // 4 + BLOCKS, SIDE // 2 + BLOCKS)
CORNER_LANE = SIDE // 2 + 2 * BLOCKS
EDGE_CORNERS = ((0, 1), (1, 3), (2, 3), (0, 2))
END_RIMS = (
    ((WEST, 0), (EAST, 0)),
    ((NORTH, 1), (SOUTH, 1)),
    ((WEST, 1), (EAST, 1)),
    ((NORTH, 0), (SOUTH, 0)),
)

BAND_ROUTES = ((1, 3, 0, 2), (3, 2, 1, 0), (2, 0, 3, 1))
TILE_ROUTES = ((1, 2, 0, 3), (2, 3, 1, 0), (3, 0, 2, 1), (0, 1, 3, 2))


def routes_for(count, preferred):
    if len(preferred[0]) == count:
        return preferred
    return tuple(tuple(i ^ step for i in range(count)) for step in range(1, count))


def senders(route):
    return tuple(route.index(i) for i in range(len(route)))


def look_up(table, index, dtype=jnp.int32):
    value = dtype(table[0])
    for i in range(1, len(table)):
        value = jnp.where(index == i, dtype(table[i]), value)
    return value


def split_bf16(values):
    high = values.astype(ml_dtypes.bfloat16)
    low = (values - high.astype(np.float64)).astype(ml_dtypes.bfloat16)
    return high, low


@functools.lru_cache(maxsize=None)
def cell_tables():
    cells = SIDE * SIDE

    def at(row, column):
        return row * SIDE + column

    near = np.zeros((cells, cells))
    pool = np.zeros((cells, LANES))
    for row in range(SIDE):
        for column in range(SIDE):
            pool[at(row, column), (row // 2) * (SIDE // 4) + column // 4] = 1
            for down, right in ((1, 0), (-1, 0), (0, 1), (0, -1)):
                if 0 <= row + down < SIDE and 0 <= column + right < SIDE:
                    near[at(row + down, column + right), at(row, column)] = 1
    last = SIDE - 1
    outer = [[at(0, i), at(i, last), at(last, i), at(i, 0)] for i in range(SIDE)]
    inner = [[at(1, i), at(i, last - 1), at(last - 1, i), at(i, 1)] for i in range(SIDE)]
    carried = np.zeros((cells, 4 * BLOCKS))
    sums = np.zeros((cells, 4 * BLOCKS))
    for edge in range(4):
        for i in range(SIDE):
            block = edge * BLOCKS + i // 2
            sums[outer[i][edge], block] += 1
            carried[outer[i][edge], block] += 1
            carried[inner[i][edge], block] += 1
            if i > 0:
                carried[outer[i - 1][edge], block] += 2
            if i < last:
                carried[outer[i + 1][edge], block] += 2
    cell_map = np.concatenate([near @ near @ pool, carried, sums], axis=1)
    first_corners = np.zeros((CORNER_ROWS, LANES))
    last_corners = np.zeros((CORNER_ROWS, LANES))
    first_corners[0, 0] = 1
    first_corners[1, last] = 1
    last_corners[2, LANES - SIDE] = 1
    last_corners[3, LANES - 1] = 1
    to_bf16 = lambda table: table.astype(ml_dtypes.bfloat16)
    return to_bf16(cell_map), to_bf16(first_corners), to_bf16(last_corners)


@functools.lru_cache(maxsize=None)
def time_tables(bands, samples):
    per_band = FREQS // bands
    segments = samples // SEGLEN
    time = np.arange(SEGLEN)
    frequency = np.arange(FREQS)
    angles = 2.0 * math.pi / SEGLEN * (frequency[:, None] * time[None, :] % SEGLEN)
    window = 0.5 - 0.5 * np.cos(2.0 * math.pi / SEGLEN * time)
    waves = np.stack([window * np.cos(angles), -window * np.sin(angles)]) / 16.0
    table = np.zeros((bands, segments, 2, per_band, segments, SEGLEN))
    for segment in range(segments):
        table[:, segment, :, :, segment, :] = waves.reshape(2, bands, per_band, SEGLEN).transpose(1, 0, 2, 3)
    table = table.reshape(bands * segments * 2 * per_band, samples)
    return split_bf16(table)


def dot(left, right):
    return jnp.dot(left, right, preferred_element_type=jnp.float32)


def transform_kernel(
    routes,
    place_ref,
    ids_ref,
    near_ids_ref,
    codes_ref,
    paired_ref,
    x_ref,
    cells_ref,
    first_ref,
    last_ref,
    high_ref,
    low_ref,
    near_ref,
    kept_codes_ref,
    partner_ref,
    *rest,
):
    outs, slot_ref = rest[:-1], rest[-1]
    place = place_ref[0]
    devices = len(outs)
    rows = high_ref.shape[0] // devices
    x = x_ref[...]
    sums = dot(x, cells_ref[...])
    bands = [place] + [look_up(route, place) for route in routes]
    starts = [pl.multiple_of(band * rows, rows) for band in bands]
    high = jnp.concatenate([high_ref[pl.ds(start, rows), :] for start in starts], axis=0)
    low = jnp.concatenate([low_ref[pl.ds(start, rows), :] for start in starts], axis=0)
    across = (((1,), (1,)), ((), ()))
    corners = lax.dot_general(first_ref[...], x[:, :LANES], across, preferred_element_type=jnp.float32)
    corners += lax.dot_general(
        last_ref[...], x[:, SIDE * SIDE - LANES :], across, preferred_element_type=jnp.float32
    )
    corners = corners.astype(jnp.bfloat16)
    corner_spectra = lax.dot_general(corners, high, across, preferred_element_type=jnp.float32)
    corner_spectra += lax.dot_general(corners, low, across, preferred_element_type=jnp.float32)
    sums_high = sums.astype(jnp.bfloat16)
    sums_low = (sums - sums_high.astype(jnp.float32)).astype(jnp.bfloat16)
    spectra = dot(
        jnp.concatenate([high, high, low], axis=1), jnp.concatenate([sums_high, sums_low, sums_high], axis=0)
    )
    spectra = spectra.astype(jnp.bfloat16)
    lane_start = (place % 2) * (LANES // 2) + (place // 2) * rows
    lane = lax.broadcasted_iota(jnp.int32, (CORNER_ROWS, LANES), 1)
    mine = (lane >= lane_start) & (lane < lane_start + rows)
    for step in range(devices):
        block = spectra[step * rows : (step + 1) * rows]
        outs[step][0:rows, :] = block[:, :LANES]
        outs[step][rows : 2 * rows, :] = block[:, LANES:]
        turned = pltpu.roll(corner_spectra, lax.rem(lane_start - step * rows + LANES, LANES), 1)
        outs[step][2 * rows : 2 * rows + CORNER_ROWS, :] = jnp.where(mine, turned, 0.0).astype(jnp.bfloat16)
    fill_slots(ids_ref, near_ids_ref, codes_ref, slot_ref, near_ref, kept_codes_ref)
    for partner in range(paired_ref.shape[1]):
        partner_ref[0, partner] = slot_ref[paired_ref[0, partner]]


def collect_kernel(band_routes, tile_routes, place_ref, tile_ref, rim_map_ref, corner_map_ref, *rest):
    devices, arrivals = len(band_routes) + 1, len(tile_routes) + 1
    blocks, rest = rest[:devices], rest[devices:]
    bands, (height_ref, held_ref, rim_ref) = rest[:arrivals], rest[arrivals:]
    place = place_ref[0]
    rows = (blocks[0].shape[0] - CORNER_ROWS) // 2
    total = height_ref.shape[0]
    corners = jnp.zeros((CORNER_ROWS, LANES), jnp.float32)
    for step in range(devices):
        source = look_up(senders(band_routes[step - 1]), place) if step else place
        field, half = source % 2, source // 2
        start = pl.multiple_of(field * total + half * rows, rows)
        held_ref[pl.ds(start, rows), :] = blocks[step][0:rows, :]
        held_ref[pl.ds(2 * total + start, rows), :] = blocks[step][rows : 2 * rows, :]
        corners += blocks[step][2 * rows :, :].astype(jnp.float32)
    corners = corners.astype(jnp.bfloat16)
    height_ref[...] = held_ref[0:total, :]
    row = lax.broadcasted_iota(jnp.int32, (CORNER_ROWS, LANES), 0)
    lane = lax.broadcasted_iota(jnp.int32, (CORNER_ROWS, LANES), 1)
    spread = (lane % HALF == row + CORNER_LANE) & (row < 4)
    spread = jnp.where(spread, 1.0, 0.0).astype(jnp.bfloat16)
    maps = jnp.concatenate([corner_map_ref[...], spread], axis=1)
    corner_part = lax.dot_general(corners, maps, (((0,), (0,)), ((), ())), preferred_element_type=jnp.float32)
    width = rim_map_ref.shape[1]
    rims = dot(held_ref[2 * total : 3 * total, :], rim_map_ref[...]) + corner_part[:total, :width]
    corner_part = corner_part[total:, width:]
    rim_ref[...] = rims
    lane = lax.broadcasted_iota(jnp.int32, (total // 2, LANES), 1)
    for step in range(arrivals):
        bands[step][0:total, :] = held_ref[total : 2 * total, :]
        bands[step][total : 2 * total, :] = held_ref[3 * total : 4 * total, :]
        receiver = look_up(tile_routes[step - 1], tile_ref[0]) if step else tile_ref[0]
        part = rim_ref[:, pl.ds(pl.multiple_of(receiver * LANES, LANES), LANES)] + corner_part
        packed = jnp.where(lane < HALF, part[: total // 2], part[total // 2 :])
        bands[step][2 * total :, :] = packed.astype(jnp.bfloat16)


def rim_lane(edge, position):
    return RIM_LANES[edge] + (position // 2 if edge in (NORTH, SOUTH) else position)


def rim_cell(edge, position):
    across = SIDE // 4
    if edge == NORTH:
        return position
    if edge == EAST:
        return position * across + across - 1
    if edge == SOUTH:
        return LANES - across + position
    return position * across


def turn(position, reverse):
    return position + reverse * (BLOCKS - 1 - 2 * position)


def fill_slots(ids_ref, near_ids_ref, codes_ref, slot_ref, near_ref, kept_codes_ref):
    slots = ids_ref.shape[0]

    def invert(slot, carry):
        slot_ref[ids_ref[slot]] = slot
        return carry

    def find(slot, carry):
        for edge in range(4):
            near_ref[slot, edge] = slot_ref[near_ids_ref[slot, edge]]
            kept_codes_ref[slot, edge] = codes_ref[slot, edge]
        return carry

    lax.fori_loop(0, slots, invert, 0, unroll=slots <= 8)
    lax.fori_loop(0, slots, find, 0, unroll=slots <= 8)


def edge_terms(slot, edge, near_ref, codes_ref):
    near = near_ref[slot, edge]
    code = codes_ref[slot, edge]
    touching, reverse = code % 4, code // 4
    beyond_code = codes_ref[near, touching]
    carried = (near, touching, reverse)
    summed = (near_ref[near, touching], beyond_code % 4, jnp.bitwise_xor(reverse, beyond_code // 4))
    ends = []
    for end in range(2):
        rim_edge = look_up([END_RIMS[option][end][0] for option in range(4)], touching)
        rim_end = look_up([END_RIMS[option][end][1] for option in range(4)], touching)
        other_code = codes_ref[near, rim_edge]
        other_end = jnp.bitwise_xor(rim_end, other_code // 4)
        corner = look_up([EDGE_CORNERS[i // 2][i % 2] for i in range(8)], other_code % 4 * 2 + other_end)
        ends.append((near_ref[near, rim_edge], corner, turn((BLOCKS - 1) * end, reverse)))
    return carried, summed, ends


def rim_map_kernel(tile_ref, near_ref, codes_ref, rim_map_ref, corner_map_ref, wide_ref, corner_ref):
    tile = tile_ref[0]
    wide_ref[...] = jnp.zeros_like(wide_ref)
    corner_ref[...] = jnp.zeros_like(corner_ref)
    block = lax.broadcasted_iota(jnp.int32, (BLOCKS, LANES), 0)
    lane = lax.broadcasted_iota(jnp.int32, (BLOCKS, LANES), 1) % HALF
    corner_row = lax.broadcasted_iota(jnp.int32, (CORNER_ROWS, LANES), 0)
    corner_lane = lax.broadcasted_iota(jnp.int32, (CORNER_ROWS, LANES), 1) % HALF

    def fill(slot, carry):
        columns = pl.ds(pl.multiple_of(slot * LANES, LANES), LANES)
        for edge in range(4):
            carried, summed, ends = edge_terms(slot, edge, near_ref, codes_ref)
            for base, (source, source_edge, reverse) in ((0, carried), (4 * BLOCKS, summed)):
                hit = (lane == rim_lane(edge, turn(block, reverse))) & (source == tile)
                start = pl.multiple_of(base + source_edge * BLOCKS, BLOCKS)
                wide_ref[pl.ds(start, BLOCKS), columns] += hit.astype(jnp.float32)
            for source, corner, position in ends:
                hit = (corner_row == corner) & (corner_lane == rim_lane(edge, position)) & (source == tile)
                corner_ref[:, columns] += hit.astype(jnp.float32)
        return carry

    slots = near_ref.shape[0]
    lax.fori_loop(0, slots, fill, 0, unroll=slots <= 8)
    rim_map_ref[...] = wide_ref[...].astype(jnp.bfloat16)
    corner_map_ref[...] = corner_ref[...].astype(jnp.bfloat16)


def partner_map_kernel(
    routes,
    tile_ref,
    near_ref,
    codes_ref,
    partner_ref,
    velocity_map_ref,
    rim_map_ref,
    chosen_ref,
    arrival_ref,
    wide_ref,
    rim_ref,
):
    tile = tile_ref[0]
    row = lax.broadcasted_iota(jnp.int32, (LANES, LANES), 0) % HALF
    cell = lax.broadcasted_iota(jnp.int32, (LANES, LANES), 1)
    placed = jnp.zeros((LANES, LANES), jnp.bool_)
    for edge in range(4):
        count = SIDE // 4 if edge in (NORTH, SOUTH) else BLOCKS
        position = row - RIM_LANES[edge]
        placed |= (position >= 0) & (position < count) & (cell == rim_cell(edge, position))
    placed = placed.astype(jnp.float32)
    wide_ref[...] = jnp.zeros_like(wide_ref)
    rim_ref[...] = jnp.zeros_like(rim_ref)
    rim_ref[0:LANES, 0:LANES] = placed
    for step, route in enumerate(routes):
        sent = look_up([float(receiver != sender) for sender, receiver in enumerate(route)], tile, jnp.float32)
        rim_ref[(step + 1) * LANES : (step + 2) * LANES, 0:LANES] = placed * sent
    for sender in range(len(routes[0])):
        steps = [0] * len(routes[0])
        for step, route in enumerate(routes):
            if route[sender] != sender:
                steps[route[sender]] = step + 1
        arrival_ref[sender] = look_up(steps, tile)
    block = lax.broadcasted_iota(jnp.int32, (BLOCKS, LANES), 0)
    cell = lax.broadcasted_iota(jnp.int32, (BLOCKS, LANES), 1)
    corner_row = lax.broadcasted_iota(jnp.int32, (8, LANES), 0)
    corner_cell = lax.broadcasted_iota(jnp.int32, (8, LANES), 1)
    step = lax.broadcasted_iota(jnp.int32, (chosen_ref.shape[0], LANES), 0)

    def target(edge, position):
        return rim_cell(edge, position // 2 if edge in (NORTH, SOUTH) else position)

    for partner in range(partner_ref.shape[1]):
        slot = partner_ref[0, partner]
        columns = slice(partner * LANES, (partner + 1) * LANES)
        rim_columns = slice((partner + 1) * LANES, (partner + 2) * LANES)
        chosen_ref[:, columns] = (step == arrival_ref[slot]).astype(jnp.float32)
        for edge in range(4):
            carried, summed, ends = edge_terms(slot, edge, near_ref, codes_ref)
            for base, (source, source_edge, reverse) in ((0, carried), (4 * BLOCKS, summed)):
                hit = cell == target(edge, turn(block, reverse))
                start = pl.multiple_of(arrival_ref[source] * LANES + base + source_edge * BLOCKS, BLOCKS)
                wide_ref[pl.ds(start, BLOCKS), columns] += hit.astype(jnp.float32)
            for source, corner, position in ends:
                hit = (corner_row == corner) & (corner_cell == target(edge, position))
                for base in (CORNER_LANE, HALF + CORNER_LANE):
                    start = pl.multiple_of(arrival_ref[source] * LANES + base, 8)
                    rim_ref[pl.ds(start, 8), rim_columns] += hit.astype(jnp.float32)
    velocity_map_ref[...] = wide_ref[...].astype(jnp.bfloat16)
    rim_map_ref[...] = rim_ref[...].astype(jnp.bfloat16)


def density_kernel(
    arrivals, partners, scale, per_band, height_ref, velocity_map_ref, rim_map_ref, chosen_ref, *rest
):
    bands, (out_ref, cross_ref, sent) = rest[:arrivals], rest[arrivals:]
    total = height_ref.shape[0]
    rims = jnp.concatenate([band[2 * total :, :] for band in bands], axis=1)
    first_half = lax.broadcasted_iota(jnp.int32, rims.shape, 1) % LANES < HALF
    rims = rims.astype(jnp.float32)
    rims = jnp.concatenate([jnp.where(first_half, rims, 0.0), jnp.where(first_half, 0.0, rims)], axis=0)
    rims = dot(rims.astype(jnp.bfloat16), rim_map_ref[...])
    height = height_ref[...].astype(jnp.float32) + rims[:, :LANES]
    velocity = dot(jnp.concatenate([band[total : 2 * total, :] for band in bands], axis=1), velocity_map_ref[...])
    velocity += rims[:, LANES:]
    for step in range(arrivals):
        own = bands[step][0:total, :].astype(jnp.float32)
        velocity += jnp.concatenate([own] * partners, axis=1) * chosen_ref[step : step + 1, :]
    velocity = velocity.astype(jnp.bfloat16)
    height = height.astype(jnp.bfloat16).astype(jnp.float32)
    row = lax.broadcasted_iota(jnp.int32, height.shape, 0)
    rotated = jnp.where(
        (row // per_band) % 2 == 0,
        pltpu.roll(height, total - per_band, 0),
        -pltpu.roll(height, per_band, 0),
    )
    turned = jnp.concatenate([height.T, rotated.T], axis=0)
    lane = lax.broadcasted_iota(jnp.int32, turned.shape, 1)
    copies = []
    for frequency in range(per_band):
        left = jnp.where(lane % per_band == frequency, turned, 0.0).astype(jnp.bfloat16)
        cross = dot(left, velocity) * scale
        for partner in range(partners):
            for part in range(2):
                index = (partner * 2 + part) * per_band + frequency
                rows = pl.ds(index * LANES, LANES)
                cross_ref[rows, :] = cross[
                    part * LANES : (part + 1) * LANES, partner * LANES : (partner + 1) * LANES
                ]
                copies.append(pltpu.make_async_copy(cross_ref.at[rows], out_ref.at[rows], sent.at[index]))
                copies[-1].start()
    for copy in copies:
        copy.wait()


SMEM = pl.BlockSpec(memory_space=pltpu.SMEM)
VMEM = pl.BlockSpec(memory_space=pltpu.VMEM)


def kept(shape, dtype):
    return pltpu.VMEM(shape, dtype)


def scalars(shape, dtype):
    return pltpu.SMEM(shape, dtype)


def near_scalars(value):
    return pltpu.with_memory_space_constraint(value, pltpu.SMEM)


def near(value):
    return pltpu.with_memory_space_constraint(value, pltpu.VMEM)


def shards(tiles, freqs, field_count, fields, slot_tile_ids, neighbour_tile_ids, neighbour_rotation_code, paired_tile_ids):
    field = fields.reshape(fields.shape[2], fields.shape[3])
    samples = field.shape[0]
    devices = freqs * field_count
    per_band = FREQS // devices
    rows = samples // SEGLEN * 2 * per_band
    total = freqs * rows
    partners = paired_tile_ids.shape[1]
    tile = lax.axis_index("tiles").astype(jnp.int32).reshape(1)
    place = (lax.axis_index("freq") * field_count + lax.axis_index("field")).astype(jnp.int32).reshape(1)

    band_routes = routes_for(devices, BAND_ROUTES)
    tile_routes = routes_for(tiles, TILE_ROUTES)
    arrivals = len(tile_routes) + 1

    piece = kept((2 * rows + CORNER_ROWS, LANES), jnp.bfloat16)
    slots = slot_tile_ids.shape[0]
    near_slots, codes, partner_slots, *pieces = pl.pallas_call(
        functools.partial(transform_kernel, band_routes),
        out_shape=[
            scalars((slots, 4), jnp.int32),
            scalars((slots, 4), jnp.int32),
            scalars((1, partners), jnp.int32),
        ]
        + [piece] * devices,
        in_specs=[SMEM] * 5 + [VMEM] * 6,
        out_specs=[SMEM] * 3 + [VMEM] * devices,
        scratch_shapes=[pltpu.SMEM((slots,), jnp.int32)],
        name="transform",
    )(
        place,
        slot_tile_ids,
        neighbour_tile_ids,
        neighbour_rotation_code,
        paired_tile_ids,
        field,
        *cell_tables(),
        *time_tables(devices, samples),
    )
    near_slots, codes, partner_slots = map(near_scalars, (near_slots, codes, partner_slots))
    pieces = [pieces[0]] + [
        lax.ppermute(piece, ("freq", "field"), list(enumerate(route)))
        for piece, route in zip(pieces[1:], band_routes)
    ]

    rim_map, corner_map = pl.pallas_call(
        rim_map_kernel,
        out_shape=[
            kept((LANES, slots * LANES), jnp.bfloat16),
            kept((CORNER_ROWS, slots * LANES), jnp.bfloat16),
        ],
        in_specs=[SMEM] * 3,
        out_specs=[VMEM] * 2,
        scratch_shapes=[
            pltpu.VMEM((LANES, slots * LANES), jnp.float32),
            pltpu.VMEM((CORNER_ROWS, slots * LANES), jnp.float32),
        ],
        name="rim_map",
    )(tile, near_slots, codes)

    *sent, height = pl.pallas_call(
        functools.partial(collect_kernel, band_routes, tile_routes),
        out_shape=[kept((5 * total // 2, LANES), jnp.bfloat16)] * arrivals + [kept((total, LANES), jnp.bfloat16)],
        in_specs=[SMEM] * 2 + [VMEM] * (2 + devices),
        out_specs=[VMEM] * (arrivals + 1),
        scratch_shapes=[
            pltpu.VMEM((4 * total, LANES), jnp.bfloat16),
            pltpu.VMEM((total, slots * LANES), jnp.float32),
        ],
        name="collect",
    )(place, tile, *map(near, (rim_map, corner_map, *pieces)))

    velocity_map, rim_map, chosen = pl.pallas_call(
        functools.partial(partner_map_kernel, tile_routes),
        out_shape=[
            kept((arrivals * LANES, partners * LANES), jnp.bfloat16),
            kept((arrivals * LANES, (1 + partners) * LANES), jnp.bfloat16),
            kept((arrivals + -arrivals % 8, partners * LANES), jnp.float32),
        ],
        in_specs=[SMEM] * 4,
        out_specs=[VMEM] * 3,
        scratch_shapes=[
            pltpu.SMEM((slots,), jnp.int32),
            pltpu.VMEM((arrivals * LANES, partners * LANES), jnp.float32),
            pltpu.VMEM((arrivals * LANES, (1 + partners) * LANES), jnp.float32),
        ],
        name="partner_map",
    )(tile, near_slots, codes, partner_slots)

    bands = [sent[0]]
    for band, route in zip(sent[1:], tile_routes):
        pairs = []
        for sender, receiver in enumerate(route):
            for core in range(field_count):
                there = receiver * field_count + (core if receiver != sender else field_count - 1 - core)
                pairs.append((sender * field_count + core, there))
        bands.append(lax.ppermute(band, ("tiles", "field"), pairs))

    segments = freqs * samples // SEGLEN
    scale = 1.0 / (segments * SEGLEN * 0.375)
    blocks = partners * 2 * per_band
    density = pl.pallas_call(
        functools.partial(density_kernel, arrivals, partners, scale, per_band),
        out_shape=jax.ShapeDtypeStruct((blocks * LANES, LANES), jnp.float32),
        in_specs=[VMEM] * (4 + arrivals),
        out_specs=pl.BlockSpec(memory_space=pl.ANY),
        scratch_shapes=[
            pltpu.VMEM((blocks * LANES, LANES), jnp.float32),
            pltpu.SemaphoreType.DMA((blocks,)),
        ],
        name="density",
    )(*map(near, (height, velocity_map, rim_map, chosen, *bands)))
    return density.reshape(1, partners, 2, per_band, LANES, LANES)


def solution(mesh):
    placed = (P("field", "tiles", ("groups", "freq"), None), P(), P(), P(), P("tiles", None))
    return jax.shard_map(
        functools.partial(shards, mesh.shape["tiles"], mesh.shape["freq"], mesh.shape["field"]),
        mesh=mesh,
        in_specs=placed,
        out_specs=P(("groups", "tiles"), None, None, ("freq", "field"), None, None),
        check_vma=False,
    )
```

time: 17.9 us -> 17.5 us (0.978)
  waiting for transfers between devices: 2.69 us -> 2.31 us
    ppermute x3, waiting for transfers between devices: 1.48 us -> 0.61 us  [shards(): lax.ppermute(piece, ('freq', 'field'), list(enumerate(route)))]
    ppermute x4, waiting for transfers between devices: 1.21 us -> 1.69 us  [shards(): bands.append(lax.ppermute(band, ('tiles', 'field'), pairs))]
    pallas_call x1, Pallas kernels: 1.83 us -> 1.61 us  [shards(): pl.pallas_call(functools.partial(transform_kernel, band_routes), out_shap...]
    pallas_call x2 -> x3, Pallas kernels: 1.52 us -> 1.74 us  [the longest x1 0.84 us: shards(): pl.pallas_call(rim_map_kernel, out_shape=[kept((LANES, slots * LANES), jn...]
  transfers between devices with their start and end apart: 7 -> 7, of which waited for: 4 -> 3; matrix products, arithmetic and copies ran while one was open for 0% -> 0% of each run, Pallas kernels for 8% -> 8%
where the time goes in v5:
time: 17.5 us; the launch traced here: 17.3 us
  starting transfers between devices  9.59 us (55%)
  Pallas kernels  5.39 us (31%)
  waiting for transfers between devices  2.31 us (13%)
    ppermute x4, starting transfers between devices, shards(): bands.append(lax.ppermute(band, ('tiles', 'field'), pairs))  5.46 us
    ppermute x3, starting transfers between devices, shards(): lax.ppermute(piece, ('freq', 'field'), list(enumerate(route)))  4.14 us
    pallas_call x1, Pallas kernels, shards(): pl.pallas_call(functools.partial(density_kernel, arrivals, partners, scal...  2.05 us
    ppermute x4, waiting for transfers between devices, shards(): bands.append(lax.ppermute(band, ('tiles', 'field'), pairs))  1.69 us
    pallas_call x1, Pallas kernels, shards(): pl.pallas_call(functools.partial(transform_kernel, band_routes), out_shap...  1.61 us
    pallas_call x1, Pallas kernels, shards(): pl.pallas_call(rim_map_kernel, out_shape=[kept((LANES, slots * LANES), jn...  0.84 us
    ppermute x3, waiting for transfers between devices, shards(): lax.ppermute(piece, ('freq', 'field'), list(enumerate(route)))  0.61 us
    pallas_call x1, Pallas kernels, shards(): pl.pallas_call(functools.partial(partner_map_kernel, tile_routes), out_sh...  0.61 us
  transfers between devices with their start and end apart: 7, of which 3 were waited for; matrix products, arithmetic and copies ran while one was open for 0% of the time, Pallas kernels for 8%

profile of v5, /device:TPU:0, one launch (start us, length us, event | category | flops | bytes accessed | tf_op | source)
XLA Modules:
  0.0 17.3 jit_solution(3308478634616346012)
XLA Ops:
  0.0 1.6 %transform.1 = (s32[4,4]{1,0:T(4,128)S(4)}, s32[4,4]{1,0:T(4,128)S(4)}, s32[1,2]{1,0:T(1,128)S(4)}, bf16[80,128]{1,0:T(8,128)(2,1)S(1)}, bf16[80,128]{1,0:T(8,12...) custom-call(s32[1]{0:T(128)} %bitcast.place_ref, s32[4]{0:T(128)} %ids_ref.1, s32[4,4]{1,0:T(4,128)} %near_ids_ref.1, ...), custom_call_target="tpu_custom_call" | custom-call | tf_op jit(solution)/shard_map/transform/pallas_call | solution.py:438
  1.6 0.5 %collective-permute-start = (bf16[80,128]{1,0:T(8,128)(2,1)S(1)}, bf16[80,128]{1,0:T(8,128)(2,1)S(1)}, u32[]{:S(2)}, u32[]{:S(2)}) collective-permute-start(bf16[80,128]{1,0:T(8,128)(2,1)S(1)} %get-tuple-element.28), channel_id=1, source_target_pairs={{0,1},{1,3},{2,0},{3,2},{4,5},{5,7},{6,4},{7,6},{8,9},{9,11},{10,8... | collective-permute-start | bytes 61448 | tf_op jit(solution)/shard_map/ppermute | solution.py:462
  2.1 2.6 %collective-permute-start.1 = (bf16[80,128]{1,0:T(8,128)(2,1)S(1)}, bf16[80,128]{1,0:T(8,128)(2,1)S(1)}, u32[]{:S(2)}, u32[]{:S(2)}) collective-permute-start(bf16[80,128]{1,0:T(8,128)(2,1)S(1)} %get-tuple-element.29), channel_id=1, source_target_pairs={{0,3},{1,2},{2,1},{3,0},{4,7},{5,6},{6,5},{7,4},{8,11},{9,10},{10,... | collective-permute-start | bytes 61448 | tf_op jit(solution)/shard_map/ppermute | solution.py:462
  4.7 1.1 %collective-permute-start.2 = (bf16[80,128]{1,0:T(8,128)(2,1)S(1)}, bf16[80,128]{1,0:T(8,128)(2,1)S(1)}, u32[]{:S(2)}, u32[]{:S(2)}) collective-permute-start(bf16[80,128]{1,0:T(8,128)(2,1)S(1)} %get-tuple-element.30), channel_id=1, source_target_pairs={{0,2},{1,0},{2,3},{3,1},{4,6},{5,4},{6,7},{7,5},{8,10},{9,8},{10,1... | collective-permute-start | bytes 61448 | tf_op jit(solution)/shard_map/ppermute | solution.py:462
  5.8 0.8 %rim_map.1 = (bf16[128,512]{1,0:T(8,128)(2,1)S(1)}, bf16[16,512]{1,0:T(8,128)(2,1)S(1)}) custom-call(s32[1]{0:T(128)} %bitcast.1.tile_ref, s32[4,4]{1,0:T(4,128)S(4)} %get-tuple-element.23.near_ref, s32[4,4]{1,0:T(4,128)S(4)} %get-tuple-element.24.codes_ref), custom_call_target="tpu_custom_call" | custom-call | tf_op jit(solution)/shard_map/rim_map/pallas_call | solution.py:466
  6.6 0.0 collective-permute-done.rest_1_
  6.6 0.0 collective-permute-done.1.rest_2_
  6.6 0.6 %collective-permute-done.2.rest_3_ = bf16[80,128]{1,0:T(8,128)(2,1)S(1)} collective-permute-done((bf16[80,128]{1,0:T(8,128)(2,1)S(1)}, bf16[80,128]{1,0:T(8,128)(2,1)S(1)}, u32[]{:S(2)}, u32[]{:S(2)}) %collective-permute-start.2) | collective-permute-done | bytes 20512 | tf_op jit(solution)/shard_map/ppermute | solution.py:462
  7.2 0.3 %collect.1 = (bf16[160,128]{1,0:T(8,128)(2,1)S(1)}, bf16[160,128]{1,0:T(8,128)(2,1)S(1)}, bf16[160,128]{1,0:T(8,128)(2,1)S(1)}, bf16[160,128]{1,0:T(8,128)(2,1)S...) custom-call(s32[1]{0:T(128)} %bitcast.place_ref, s32[1]{0:T(128)} %bitcast.1.tile_ref, ...), custom_call_target="tpu_custom_call" | custom-call | tf_op jit(solution)/shard_map/collect/pallas_call | solution.py:481
  7.5 1.6 %collective-permute-start.3 = (bf16[160,128]{1,0:T(8,128)(2,1)S(1)}, bf16[160,128]{1,0:T(8,128)(2,1)S(1)}, u32[]{:S(2)}, u32[]{:S(2)}) collective-permute-start(bf16[160,128]{1,0:T(8,128)(2,1)S(1)} %get-tuple-element.37), channel_id=1, source_target_pairs={{0,4},{1,5},{4,8},{5,9},{8,0},{9,1},{12,13},{13,12},{2,6},{3,7},{6... | collective-permute-start | bytes 122888 | tf_op jit(solution)/shard_map/ppermute | solution.py:517
  9.2 1.3 %collective-permute-start.4 = (bf16[160,128]{1,0:T(8,128)(2,1)S(1)}, bf16[160,128]{1,0:T(8,128)(2,1)S(1)}, u32[]{:S(2)}, u32[]{:S(2)}) collective-permute-start(bf16[160,128]{1,0:T(8,128)(2,1)S(1)} %get-tuple-element.38), channel_id=1, source_target_pairs={{0,8},{1,9},{4,12},{5,13},{8,4},{9,5},{12,0},{13,1},{2,10},{3,11},... | collective-permute-start | bytes 122888 | tf_op jit(solution)/shard_map/ppermute | solution.py:517
  10.5 2.5 %collective-permute-start.5 = (bf16[160,128]{1,0:T(8,128)(2,1)S(1)}, bf16[160,128]{1,0:T(8,128)(2,1)S(1)}, u32[]{:S(2)}, u32[]{:S(2)}) collective-permute-start(bf16[160,128]{1,0:T(8,128)(2,1)S(1)} %get-tuple-element.39), channel_id=1, source_target_pairs={{0,12},{1,13},{4,0},{5,1},{8,9},{9,8},{12,4},{13,5},{2,14},{3,15},... | collective-permute-start | bytes 122888 | tf_op jit(solution)/shard_map/ppermute | solution.py:517
  13.0 0.0 collective-permute-start.6
  13.0 0.6 %partner_map.1 = (bf16[640,256]{1,0:T(8,128)(2,1)S(1)}, bf16[640,384]{1,0:T(8,128)(2,1)S(1)}, f32[8,256]{1,0:T(8,128)S(1)}) custom-call(s32[1]{0:T(128)} %bitcast.1.tile_ref, s32[4,4]{1,0:T(4,128)S(4)} %get-tuple-element.23.near_ref, s32[4,4]{1,0:T(4,128)S(4)} %get-tuple-element.24.codes_ref, s32[1,2]{1,0:T(1,128)S(4)} %get-tuple-element.32.partner_ref), custom_call_target="tpu_custom_call" | custom-call | tf_op jit(solution)/shard_map/partner_map/pallas_call | solution.py:493
  13.6 0.0 collective-permute-done.3.rest_1_
  13.6 1.4 %collective-permute-done.4.rest_2_ = bf16[160,128]{1,0:T(8,128)(2,1)S(1)} collective-permute-done((bf16[160,128]{1,0:T(8,128)(2,1)S(1)}, bf16[160,128]{1,0:T(8,128)(2,1)S(1)}, u32[]{:S(2)}, u32[]{:S(2)}) %collective-permute-start.4) | collective-permute-done | bytes 40992 | tf_op jit(solution)/shard_map/ppermute | solution.py:517
  15.0 0.3 %collective-permute-done.5.rest_3_ = bf16[160,128]{1,0:T(8,128)(2,1)S(1)} collective-permute-done((bf16[160,128]{1,0:T(8,128)(2,1)S(1)}, bf16[160,128]{1,0:T(8,128)(2,1)S(1)}, u32[]{:S(2)}, u32[]{:S(2)}) %collective-permute-start.5) | collective-permute-done | bytes 40992 | tf_op jit(solution)/shard_map/ppermute | solution.py:517
  15.3 0.0 collective-permute-done.6.rest_4_
  15.3 2.0 %density.1 = f32[4096,128]{1,0:T(8,128)} custom-call(bf16[64,128]{1,0:T(8,128)(2,1)S(1)} %get-tuple-element.31.height_ref, bf16[640,256]{1,0:T(8,128)(2,1)S(1)} %get-tuple-element.33.velocity_map_ref, bf16[640,384]{1,0:T(8,128)(2,1)S(1)} %get-tuple-element.34.rim_map_ref, f32[8,256]{1,0:T(8,128)S(1)} %get-tuple-element.35.chosen_ref, ...), custom_call_target="tpu_custom_call" | custom-call | tf_op jit(solution)/shard_map/density/pallas_call | solution.py:522
Async XLA Ops:
  1.6 5.0 %collective-permute-start = (bf16[80,128]{1,0:T(8,128)(2,1)S(1)}, bf16[80,128]{1,0:T(8,128)(2,1)S(1)}, u32[]{:S(2)}, u32[]{:S(2)}) collective-permute-start(bf16[80,128]{1,0:T(8,128)(2,1)S(1)} %get-tuple-element.28), channel_id=1, source_target_pairs={{0,1},{1,3},{2,0},{3,2},{4,5},{5,7},{6,4},{7,6},{8,9},{9,11},{10,8... | collective-permute-start | bytes 61448 | tf_op jit(solution)/shard_map/ppermute | solution.py:462
  2.1 4.5 %collective-permute-start.1 = (bf16[80,128]{1,0:T(8,128)(2,1)S(1)}, bf16[80,128]{1,0:T(8,128)(2,1)S(1)}, u32[]{:S(2)}, u32[]{:S(2)}) collective-permute-start(bf16[80,128]{1,0:T(8,128)(2,1)S(1)} %get-tuple-element.29), channel_id=1, source_target_pairs={{0,3},{1,2},{2,1},{3,0},{4,7},{5,6},{6,5},{7,4},{8,11},{9,10},{10,... | collective-permute-start | bytes 61448 | tf_op jit(solution)/shard_map/ppermute | solution.py:462
  4.7 2.5 %collective-permute-start.2 = (bf16[80,128]{1,0:T(8,128)(2,1)S(1)}, bf16[80,128]{1,0:T(8,128)(2,1)S(1)}, u32[]{:S(2)}, u32[]{:S(2)}) collective-permute-start(bf16[80,128]{1,0:T(8,128)(2,1)S(1)} %get-tuple-element.30), channel_id=1, source_target_pairs={{0,2},{1,0},{2,3},{3,1},{4,6},{5,4},{6,7},{7,5},{8,10},{9,8},{10,1... | collective-permute-start | bytes 61448 | tf_op jit(solution)/shard_map/ppermute | solution.py:462
  7.5 6.1 %collective-permute-start.3 = (bf16[160,128]{1,0:T(8,128)(2,1)S(1)}, bf16[160,128]{1,0:T(8,128)(2,1)S(1)}, u32[]{:S(2)}, u32[]{:S(2)}) collective-permute-start(bf16[160,128]{1,0:T(8,128)(2,1)S(1)} %get-tuple-element.37), channel_id=1, source_target_pairs={{0,4},{1,5},{4,8},{5,9},{8,0},{9,1},{12,13},{13,12},{2,6},{3,7},{6... | collective-permute-start | bytes 122888 | tf_op jit(solution)/shard_map/ppermute | solution.py:517
  9.2 5.8 %collective-permute-start.4 = (bf16[160,128]{1,0:T(8,128)(2,1)S(1)}, bf16[160,128]{1,0:T(8,128)(2,1)S(1)}, u32[]{:S(2)}, u32[]{:S(2)}) collective-permute-start(bf16[160,128]{1,0:T(8,128)(2,1)S(1)} %get-tuple-element.38), channel_id=1, source_target_pairs={{0,8},{1,9},{4,12},{5,13},{8,4},{9,5},{12,0},{13,1},{2,10},{3,11},... | collective-permute-start | bytes 122888 | tf_op jit(solution)/shard_map/ppermute | solution.py:517
  10.5 4.8 %collective-permute-start.5 = (bf16[160,128]{1,0:T(8,128)(2,1)S(1)}, bf16[160,128]{1,0:T(8,128)(2,1)S(1)}, u32[]{:S(2)}, u32[]{:S(2)}) collective-permute-start(bf16[160,128]{1,0:T(8,128)(2,1)S(1)} %get-tuple-element.39), channel_id=1, source_target_pairs={{0,12},{1,13},{4,0},{5,1},{8,9},{9,8},{12,4},{13,5},{2,14},{3,15},... | collective-permute-start | bytes 122888 | tf_op jit(solution)/shard_map/ppermute | solution.py:517
  13.0 2.3 %collective-permute-start.6 = (bf16[160,128]{1,0:T(8,128)(2,1)S(1)}, bf16[160,128]{1,0:T(8,128)(2,1)S(1)}, u32[]{:S(2)}, u32[]{:S(2)}) collective-permute-start(bf16[160,128]{1,0:T(8,128)(2,1)S(1)} %get-tuple-element.40), channel_id=1, source_target_pairs={{0,1},{1,0},{4,5},{5,4},{8,12},{9,13},{12,8},{13,9},{2,3},{3,2},{6... | collective-permute-start | bytes 122888 | tf_op jit(solution)/shard_map/ppermute | solution.py:517

commit v6 on v5

--- a/solution.py
+++ b/solution.py
@@ -21,6 +21,7 @@
 HALF = LANES // 2
 RIM_LANES = (0, SIDE // 4, SIDE // 4 + BLOCKS, SIDE // 2 + BLOCKS)
 CORNER_LANE = SIDE // 2 + 2 * BLOCKS
+HEIGHT_CORNER_LANE = CORNER_LANE + 8
 EDGE_CORNERS = ((0, 1), (1, 3), (2, 3), (0, 2))
 END_RIMS = (
     ((WEST, 0), (EAST, 0)),
@@ -30,7 +31,7 @@
 )
 
 BAND_ROUTES = ((1, 3, 0, 2), (3, 2, 1, 0), (2, 0, 3, 1))
-TILE_ROUTES = ((1, 2, 0, 3), (2, 3, 1, 0), (3, 0, 2, 1), (0, 1, 3, 2))
+TILE_ROUTES = ((1, 3, 2, 0), (2, 1, 0, 3), (3, 0, 1, 2), (0, 2, 3, 1))
 
 
 def routes_for(count, preferred):
@@ -94,7 +95,7 @@
     last_corners[2, LANES - SIDE] = 1
     last_corners[3, LANES - 1] = 1
     to_bf16 = lambda table: table.astype(ml_dtypes.bfloat16)
-    return to_bf16(cell_map), to_bf16(first_corners), to_bf16(last_corners)
+    return cell_map.astype(ml_dtypes.float8_e4m3fn), to_bf16(first_corners), to_bf16(last_corners)
 
 
 @functools.lru_cache(maxsize=None)
@@ -140,7 +141,7 @@
     devices = len(outs)
     rows = high_ref.shape[0] // devices
     x = x_ref[...]
-    sums = dot(x, cells_ref[...])
+    sums = dot(x, cells_ref[...].astype(jnp.bfloat16))
     bands = [place] + [look_up(route, place) for route in routes]
     starts = [pl.multiple_of(band * rows, rows) for band in bands]
     high = jnp.concatenate([high_ref[pl.ds(start, rows), :] for start in starts], axis=0)
@@ -173,10 +174,10 @@
         partner_ref[0, partner] = slot_ref[paired_ref[0, partner]]
 
 
-def collect_kernel(band_routes, tile_routes, place_ref, tile_ref, rim_map_ref, corner_map_ref, *rest):
+def collect_kernel(band_routes, tile_routes, place_ref, tile_ref, rim_map_ref, *rest):
     devices, arrivals = len(band_routes) + 1, len(tile_routes) + 1
     blocks, rest = rest[:devices], rest[devices:]
-    bands, (height_ref, held_ref, rim_ref) = rest[:arrivals], rest[arrivals:]
+    bands, (height_ref, held_ref) = rest[:arrivals], rest[arrivals:]
     place = place_ref[0]
     rows = (blocks[0].shape[0] - CORNER_ROWS) // 2
     total = height_ref.shape[0]
@@ -188,24 +189,23 @@
         held_ref[pl.ds(start, rows), :] = blocks[step][0:rows, :]
         held_ref[pl.ds(2 * total + start, rows), :] = blocks[step][rows : 2 * rows, :]
         corners += blocks[step][2 * rows :, :].astype(jnp.float32)
-    corners = corners.astype(jnp.bfloat16)
     height_ref[...] = held_ref[0:total, :]
-    row = lax.broadcasted_iota(jnp.int32, (CORNER_ROWS, LANES), 0)
-    lane = lax.broadcasted_iota(jnp.int32, (CORNER_ROWS, LANES), 1)
-    spread = (lane % HALF == row + CORNER_LANE) & (row < 4)
-    spread = jnp.where(spread, 1.0, 0.0).astype(jnp.bfloat16)
-    maps = jnp.concatenate([corner_map_ref[...], spread], axis=1)
-    corner_part = lax.dot_general(corners, maps, (((0,), (0,)), ((), ())), preferred_element_type=jnp.float32)
-    width = rim_map_ref.shape[1]
-    rims = dot(held_ref[2 * total : 3 * total, :], rim_map_ref[...]) + corner_part[:total, :width]
-    corner_part = corner_part[total:, width:]
-    rim_ref[...] = rims
+    row = lax.broadcasted_iota(jnp.int32, (CORNER_ROWS, 2 * LANES), 0)
+    lane = lax.broadcasted_iota(jnp.int32, (CORNER_ROWS, 2 * LANES), 1)
+    first = jnp.where(lane < LANES, HEIGHT_CORNER_LANE, CORNER_LANE)
+    spread = jnp.where((lane % HALF == row + first) & (row < 4), 1.0, 0.0).astype(jnp.bfloat16)
+    corners = lax.dot_general(
+        corners.astype(jnp.bfloat16), spread, (((0,), (0,)), ((), ())), preferred_element_type=jnp.float32
+    )
+    corners = corners[:total, :LANES] + corners[total:, LANES:]
     lane = lax.broadcasted_iota(jnp.int32, (total // 2, LANES), 1)
+    rims = held_ref[2 * total : 3 * total, :]
     for step in range(arrivals):
         bands[step][0:total, :] = held_ref[total : 2 * total, :]
         bands[step][total : 2 * total, :] = held_ref[3 * total : 4 * total, :]
         receiver = look_up(tile_routes[step - 1], tile_ref[0]) if step else tile_ref[0]
-        part = rim_ref[:, pl.ds(pl.multiple_of(receiver * LANES, LANES), LANES)] + corner_part
+        columns = pl.ds(pl.multiple_of(receiver * LANES, LANES), LANES)
+        part = dot(rims, rim_map_ref[:, columns]) + corners
         packed = jnp.where(lane < HALF, part[: total // 2], part[total // 2 :])
         bands[step][2 * total :, :] = packed.astype(jnp.bfloat16)
 
@@ -264,32 +264,25 @@
     return carried, summed, ends
 
 
-def rim_map_kernel(tile_ref, near_ref, codes_ref, rim_map_ref, corner_map_ref, wide_ref, corner_ref):
+def rim_map_kernel(tile_ref, near_ref, codes_ref, rim_map_ref, wide_ref):
     tile = tile_ref[0]
     wide_ref[...] = jnp.zeros_like(wide_ref)
-    corner_ref[...] = jnp.zeros_like(corner_ref)
     block = lax.broadcasted_iota(jnp.int32, (BLOCKS, LANES), 0)
     lane = lax.broadcasted_iota(jnp.int32, (BLOCKS, LANES), 1) % HALF
-    corner_row = lax.broadcasted_iota(jnp.int32, (CORNER_ROWS, LANES), 0)
-    corner_lane = lax.broadcasted_iota(jnp.int32, (CORNER_ROWS, LANES), 1) % HALF
 
     def fill(slot, carry):
         columns = pl.ds(pl.multiple_of(slot * LANES, LANES), LANES)
         for edge in range(4):
-            carried, summed, ends = edge_terms(slot, edge, near_ref, codes_ref)
+            carried, summed, _ = edge_terms(slot, edge, near_ref, codes_ref)
             for base, (source, source_edge, reverse) in ((0, carried), (4 * BLOCKS, summed)):
                 hit = (lane == rim_lane(edge, turn(block, reverse))) & (source == tile)
                 start = pl.multiple_of(base + source_edge * BLOCKS, BLOCKS)
                 wide_ref[pl.ds(start, BLOCKS), columns] += hit.astype(jnp.float32)
-            for source, corner, position in ends:
-                hit = (corner_row == corner) & (corner_lane == rim_lane(edge, position)) & (source == tile)
-                corner_ref[:, columns] += hit.astype(jnp.float32)
         return carry
 
     slots = near_ref.shape[0]
     lax.fori_loop(0, slots, fill, 0, unroll=slots <= 8)
     rim_map_ref[...] = wide_ref[...].astype(jnp.bfloat16)
-    corner_map_ref[...] = corner_ref[...].astype(jnp.bfloat16)
 
 
 def partner_map_kernel(
@@ -335,6 +328,16 @@
     def target(edge, position):
         return rim_cell(edge, position // 2 if edge in (NORTH, SOUTH) else position)
 
+    def add_corners(ends, edge, first_lane, columns):
+        for source, corner, position in ends:
+            hit = (corner_row == corner) & (corner_cell == target(edge, position))
+            for base in (first_lane, HALF + first_lane):
+                start = pl.multiple_of(arrival_ref[source] * LANES + base, 8)
+                rim_ref[pl.ds(start, 8), columns] += hit.astype(jnp.float32)
+
+    for edge in range(4):
+        _, _, ends = edge_terms(tile, edge, near_ref, codes_ref)
+        add_corners(ends, edge, HEIGHT_CORNER_LANE, slice(0, LANES))
     for partner in range(partner_ref.shape[1]):
         slot = partner_ref[0, partner]
         columns = slice(partner * LANES, (partner + 1) * LANES)
@@ -346,11 +349,7 @@
                 hit = cell == target(edge, turn(block, reverse))
                 start = pl.multiple_of(arrival_ref[source] * LANES + base + source_edge * BLOCKS, BLOCKS)
                 wide_ref[pl.ds(start, BLOCKS), columns] += hit.astype(jnp.float32)
-            for source, corner, position in ends:
-                hit = (corner_row == corner) & (corner_cell == target(edge, position))
-                for base in (CORNER_LANE, HALF + CORNER_LANE):
-                    start = pl.multiple_of(arrival_ref[source] * LANES + base, 8)
-                    rim_ref[pl.ds(start, 8), rim_columns] += hit.astype(jnp.float32)
+            add_corners(ends, edge, CORNER_LANE, rim_columns)
     velocity_map_ref[...] = wide_ref[...].astype(jnp.bfloat16)
     rim_map_ref[...] = rim_ref[...].astype(jnp.bfloat16)
 
@@ -463,32 +462,23 @@
         for piece, route in zip(pieces[1:], band_routes)
     ]
 
-    rim_map, corner_map = pl.pallas_call(
+    rim_map = pl.pallas_call(
         rim_map_kernel,
-        out_shape=[
-            kept((LANES, slots * LANES), jnp.bfloat16),
-            kept((CORNER_ROWS, slots * LANES), jnp.bfloat16),
-        ],
+        out_shape=kept((LANES, slots * LANES), jnp.bfloat16),
         in_specs=[SMEM] * 3,
-        out_specs=[VMEM] * 2,
-        scratch_shapes=[
-            pltpu.VMEM((LANES, slots * LANES), jnp.float32),
-            pltpu.VMEM((CORNER_ROWS, slots * LANES), jnp.float32),
-        ],
+        out_specs=VMEM,
+        scratch_shapes=[pltpu.VMEM((LANES, slots * LANES), jnp.float32)],
         name="rim_map",
     )(tile, near_slots, codes)
 
     *sent, height = pl.pallas_call(
         functools.partial(collect_kernel, band_routes, tile_routes),
         out_shape=[kept((5 * total // 2, LANES), jnp.bfloat16)] * arrivals + [kept((total, LANES), jnp.bfloat16)],
-        in_specs=[SMEM] * 2 + [VMEM] * (2 + devices),
+        in_specs=[SMEM] * 2 + [VMEM] * (1 + devices),
         out_specs=[VMEM] * (arrivals + 1),
-        scratch_shapes=[
-            pltpu.VMEM((4 * total, LANES), jnp.bfloat16),
-            pltpu.VMEM((total, slots * LANES), jnp.float32),
-        ],
+        scratch_shapes=[pltpu.VMEM((4 * total, LANES), jnp.bfloat16)],
         name="collect",
-    )(place, tile, *map(near, (rim_map, corner_map, *pieces)))
+    )(place, tile, *map(near, (rim_map, *pieces)))
 
     velocity_map, rim_map, chosen = pl.pallas_call(
         functools.partial(partner_map_kernel, tile_routes),

time: 17.5 us -> 17.3 us (0.989)
  waiting for transfers between devices: 2.31 us -> 3.81 us
  starting transfers between devices: 9.59 us -> 8.48 us
  Pallas kernels: 5.39 us -> 4.86 us
    ppermute x4, starting transfers between devices: 5.46 us -> 4.34 us  [shards(): bands.append(lax.ppermute(band, ('tiles', 'field'), pairs))]
    ppermute x4, waiting for transfers between devices: 1.69 us -> 2.63 us  [shards(): bands.append(lax.ppermute(band, ('tiles', 'field'), pairs))]
    ppermute x3, waiting for transfers between devices: 0.61 us -> 1.18 us  [shards(): lax.ppermute(piece, ('freq', 'field'), list(enumerate(route)))]
    pallas_call x1, Pallas kernels: 0.84 us -> 0.29 us  [shards(): pl.pallas_call(rim_map_kernel, out_shape=kept((LANES, slots * LANES), jnp...]
  transfers between devices with their start and end apart: 7 -> 7, of which waited for: 3 -> 5; matrix products, arithmetic and copies ran while one was open for 0% -> 0% of each run, Pallas kernels for 8% -> 6%
where the time goes in v6:
time: 17.3 us; the launch traced here: 17.2 us
  starting transfers between devices  8.48 us (49%)
  Pallas kernels  4.86 us (28%)
  waiting for transfers between devices  3.81 us (22%)
    ppermute x4, starting transfers between devices, shards(): bands.append(lax.ppermute(band, ('tiles', 'field'), pairs))  4.34 us
    ppermute x3, starting transfers between devices, shards(): lax.ppermute(piece, ('freq', 'field'), list(enumerate(route)))  4.14 us
    ppermute x4, waiting for transfers between devices, shards(): bands.append(lax.ppermute(band, ('tiles', 'field'), pairs))  2.63 us
    pallas_call x1, Pallas kernels, shards(): pl.pallas_call(functools.partial(density_kernel, arrivals, partners, scal...  2.04 us
    pallas_call x1, Pallas kernels, shards(): pl.pallas_call(functools.partial(transform_kernel, band_routes), out_shap...  1.53 us
    ppermute x3, waiting for transfers between devices, shards(): lax.ppermute(piece, ('freq', 'field'), list(enumerate(route)))  1.18 us
    pallas_call x1, Pallas kernels, shards(): pl.pallas_call(functools.partial(partner_map_kernel, tile_routes), out_sh...  0.77 us
  transfers between devices with their start and end apart: 7, of which 5 were waited for; matrix products, arithmetic and copies ran while one was open for 0% of the time, Pallas kernels for 6%

profile of v6, /device:TPU:0, one launch (start us, length us, event | category | flops | bytes accessed | tf_op | source)
XLA Modules:
  0.0 17.2 jit_solution(5961123005218903131)
XLA Ops:
  0.0 1.5 %transform.1 = (s32[4,4]{1,0:T(4,128)S(4)}, s32[4,4]{1,0:T(4,128)S(4)}, s32[1,2]{1,0:T(1,128)S(4)}, bf16[80,128]{1,0:T(8,128)(2,1)S(1)}, bf16[80,128]{1,0:T(8,12...) custom-call(s32[1]{0:T(128)} %bitcast.place_ref, s32[4]{0:T(128)} %ids_ref.1, s32[4,4]{1,0:T(4,128)} %near_ids_ref.1, ...), custom_call_target="tpu_custom_call" | custom-call | tf_op jit(solution)/shard_map/transform/pallas_call | solution.py:437
  1.5 0.5 %collective-permute-start = (bf16[80,128]{1,0:T(8,128)(2,1)S(1)}, bf16[80,128]{1,0:T(8,128)(2,1)S(1)}, u32[]{:S(2)}, u32[]{:S(2)}) collective-permute-start(bf16[80,128]{1,0:T(8,128)(2,1)S(1)} %get-tuple-element.24), channel_id=1, source_target_pairs={{0,1},{1,3},{2,0},{3,2},{4,5},{5,7},{6,4},{7,6},{8,9},{9,11},{10,8... | collective-permute-start | bytes 61448 | tf_op jit(solution)/shard_map/ppermute | solution.py:461
  2.0 2.6 %collective-permute-start.1 = (bf16[80,128]{1,0:T(8,128)(2,1)S(1)}, bf16[80,128]{1,0:T(8,128)(2,1)S(1)}, u32[]{:S(2)}, u32[]{:S(2)}) collective-permute-start(bf16[80,128]{1,0:T(8,128)(2,1)S(1)} %get-tuple-element.25), channel_id=1, source_target_pairs={{0,3},{1,2},{2,1},{3,0},{4,7},{5,6},{6,5},{7,4},{8,11},{9,10},{10,... | collective-permute-start | bytes 61448 | tf_op jit(solution)/shard_map/ppermute | solution.py:461
  4.6 1.1 %collective-permute-start.2 = (bf16[80,128]{1,0:T(8,128)(2,1)S(1)}, bf16[80,128]{1,0:T(8,128)(2,1)S(1)}, u32[]{:S(2)}, u32[]{:S(2)}) collective-permute-start(bf16[80,128]{1,0:T(8,128)(2,1)S(1)} %get-tuple-element.26), channel_id=1, source_target_pairs={{0,2},{1,0},{2,3},{3,1},{4,6},{5,4},{6,7},{7,5},{8,10},{9,8},{10,1... | collective-permute-start | bytes 61448 | tf_op jit(solution)/shard_map/ppermute | solution.py:461
  5.7 0.3 %rim_map.1.rim_map_ref = bf16[128,512]{1,0:T(8,128)(2,1)S(1)} custom-call(s32[1]{0:T(128)} %bitcast.1.tile_ref, s32[4,4]{1,0:T(4,128)S(4)} %get-tuple-element.21.near_ref, s32[4,4]{1,0:T(4,128)S(4)} %get-tuple-element.22.codes_ref), custom_call_target="tpu_custom_call" | custom-call | tf_op jit(solution)/shard_map/rim_map/pallas_call | solution.py:465
  6.0 0.3 %collective-permute-done.rest_1_ = bf16[80,128]{1,0:T(8,128)(2,1)S(1)} collective-permute-done((bf16[80,128]{1,0:T(8,128)(2,1)S(1)}, bf16[80,128]{1,0:T(8,128)(2,1)S(1)}, u32[]{:S(2)}, u32[]{:S(2)}) %collective-permute-start) | collective-permute-done | bytes 20512 | tf_op jit(solution)/shard_map/ppermute | solution.py:461
  6.3 0.0 collective-permute-done.1.rest_2_
  6.3 0.9 %collective-permute-done.2.rest_3_ = bf16[80,128]{1,0:T(8,128)(2,1)S(1)} collective-permute-done((bf16[80,128]{1,0:T(8,128)(2,1)S(1)}, bf16[80,128]{1,0:T(8,128)(2,1)S(1)}, u32[]{:S(2)}, u32[]{:S(2)}) %collective-permute-start.2) | collective-permute-done | bytes 20512 | tf_op jit(solution)/shard_map/ppermute | solution.py:461
  7.2 0.2 %collect.1 = (bf16[160,128]{1,0:T(8,128)(2,1)S(1)}, bf16[160,128]{1,0:T(8,128)(2,1)S(1)}, bf16[160,128]{1,0:T(8,128)(2,1)S(1)}, bf16[160,128]{1,0:T(8,128)(2,1)S...) custom-call(s32[1]{0:T(128)} %bitcast.place_ref, s32[1]{0:T(128)} %bitcast.1.tile_ref, ...), custom_call_target="tpu_custom_call" | custom-call | tf_op jit(solution)/shard_map/collect/pallas_call | solution.py:474
  7.4 1.6 %collective-permute-start.3 = (bf16[160,128]{1,0:T(8,128)(2,1)S(1)}, bf16[160,128]{1,0:T(8,128)(2,1)S(1)}, u32[]{:S(2)}, u32[]{:S(2)}) collective-permute-start(bf16[160,128]{1,0:T(8,128)(2,1)S(1)} %get-tuple-element.33), channel_id=1, source_target_pairs={{0,4},{1,5},{4,12},{5,13},{8,9},{9,8},{12,0},{13,1},{2,6},{3,7},{6... | collective-permute-start | bytes 122888 | tf_op jit(solution)/shard_map/ppermute | solution.py:507
  9.0 1.6 %collective-permute-start.4 = (bf16[160,128]{1,0:T(8,128)(2,1)S(1)}, bf16[160,128]{1,0:T(8,128)(2,1)S(1)}, u32[]{:S(2)}, u32[]{:S(2)}) collective-permute-start(bf16[160,128]{1,0:T(8,128)(2,1)S(1)} %get-tuple-element.34), channel_id=1, source_target_pairs={{0,8},{1,9},{4,5},{5,4},{8,0},{9,1},{12,13},{13,12},{2,10},{3,11},... | collective-permute-start | bytes 122888 | tf_op jit(solution)/shard_map/ppermute | solution.py:507
  10.6 1.1 %collective-permute-start.5 = (bf16[160,128]{1,0:T(8,128)(2,1)S(1)}, bf16[160,128]{1,0:T(8,128)(2,1)S(1)}, u32[]{:S(2)}, u32[]{:S(2)}) collective-permute-start(bf16[160,128]{1,0:T(8,128)(2,1)S(1)} %get-tuple-element.35), channel_id=1, source_target_pairs={{0,12},{1,13},{4,0},{5,1},{8,4},{9,5},{12,8},{13,9},{2,14},{3,15},... | collective-permute-start | bytes 122888 | tf_op jit(solution)/shard_map/ppermute | solution.py:507
  11.7 0.0 collective-permute-start.6
  11.7 0.8 %partner_map.1 = (bf16[640,256]{1,0:T(8,128)(2,1)S(1)}, bf16[640,384]{1,0:T(8,128)(2,1)S(1)}, f32[8,256]{1,0:T(8,128)S(1)}) custom-call(s32[1]{0:T(128)} %bitcast.1.tile_ref, s32[4,4]{1,0:T(4,128)S(4)} %get-tuple-element.21.near_ref, s32[4,4]{1,0:T(4,128)S(4)} %get-tuple-element.22.codes_ref, s32[1,2]{1,0:T(1,128)S(4)} %get-tuple-element.28.partner_ref), custom_call_target="tpu_custom_call" | custom-call | tf_op jit(solution)/shard_map/partner_map/pallas_call | solution.py:483
  12.5 1.0 %collective-permute-done.3.rest_1_ = bf16[160,128]{1,0:T(8,128)(2,1)S(1)} collective-permute-done((bf16[160,128]{1,0:T(8,128)(2,1)S(1)}, bf16[160,128]{1,0:T(8,128)(2,1)S(1)}, u32[]{:S(2)}, u32[]{:S(2)}) %collective-permute-start.3) | collective-permute-done | bytes 40992 | tf_op jit(solution)/shard_map/ppermute | solution.py:507
  13.5 0.9 %collective-permute-done.4.rest_2_ = bf16[160,128]{1,0:T(8,128)(2,1)S(1)} collective-permute-done((bf16[160,128]{1,0:T(8,128)(2,1)S(1)}, bf16[160,128]{1,0:T(8,128)(2,1)S(1)}, u32[]{:S(2)}, u32[]{:S(2)}) %collective-permute-start.4) | collective-permute-done | bytes 40992 | tf_op jit(solution)/shard_map/ppermute | solution.py:507
  14.4 0.8 %collective-permute-done.5.rest_3_ = bf16[160,128]{1,0:T(8,128)(2,1)S(1)} collective-permute-done((bf16[160,128]{1,0:T(8,128)(2,1)S(1)}, bf16[160,128]{1,0:T(8,128)(2,1)S(1)}, u32[]{:S(2)}, u32[]{:S(2)}) %collective-permute-start.5) | collective-permute-done | bytes 40992 | tf_op jit(solution)/shard_map/ppermute | solution.py:507
  15.1 0.0 collective-permute-done.6.rest_4_
  15.1 2.0 %density.1 = f32[4096,128]{1,0:T(8,128)} custom-call(bf16[64,128]{1,0:T(8,128)(2,1)S(1)} %get-tuple-element.27.height_ref, bf16[640,256]{1,0:T(8,128)(2,1)S(1)} %get-tuple-element.29.velocity_map_ref, bf16[640,384]{1,0:T(8,128)(2,1)S(1)} %get-tuple-element.30.rim_map_ref, f32[8,256]{1,0:T(8,128)S(1)} %get-tuple-element.31.chosen_ref, ...), custom_call_target="tpu_custom_call" | custom-call | tf_op jit(solution)/shard_map/density/pallas_call | solution.py:512
Async XLA Ops:
  1.5 4.8 %collective-permute-start = (bf16[80,128]{1,0:T(8,128)(2,1)S(1)}, bf16[80,128]{1,0:T(8,128)(2,1)S(1)}, u32[]{:S(2)}, u32[]{:S(2)}) collective-permute-start(bf16[80,128]{1,0:T(8,128)(2,1)S(1)} %get-tuple-element.24), channel_id=1, source_target_pairs={{0,1},{1,3},{2,0},{3,2},{4,5},{5,7},{6,4},{7,6},{8,9},{9,11},{10,8... | collective-permute-start | bytes 61448 | tf_op jit(solution)/shard_map/ppermute | solution.py:461
  2.0 4.3 %collective-permute-start.1 = (bf16[80,128]{1,0:T(8,128)(2,1)S(1)}, bf16[80,128]{1,0:T(8,128)(2,1)S(1)}, u32[]{:S(2)}, u32[]{:S(2)}) collective-permute-start(bf16[80,128]{1,0:T(8,128)(2,1)S(1)} %get-tuple-element.25), channel_id=1, source_target_pairs={{0,3},{1,2},{2,1},{3,0},{4,7},{5,6},{6,5},{7,4},{8,11},{9,10},{10,... | collective-permute-start | bytes 61448 | tf_op jit(solution)/shard_map/ppermute | solution.py:461
  4.6 2.5 %collective-permute-start.2 = (bf16[80,128]{1,0:T(8,128)(2,1)S(1)}, bf16[80,128]{1,0:T(8,128)(2,1)S(1)}, u32[]{:S(2)}, u32[]{:S(2)}) collective-permute-start(bf16[80,128]{1,0:T(8,128)(2,1)S(1)} %get-tuple-element.26), channel_id=1, source_target_pairs={{0,2},{1,0},{2,3},{3,1},{4,6},{5,4},{6,7},{7,5},{8,10},{9,8},{10,1... | collective-permute-start | bytes 61448 | tf_op jit(solution)/shard_map/ppermute | solution.py:461
  7.4 6.1 %collective-permute-start.3 = (bf16[160,128]{1,0:T(8,128)(2,1)S(1)}, bf16[160,128]{1,0:T(8,128)(2,1)S(1)}, u32[]{:S(2)}, u32[]{:S(2)}) collective-permute-start(bf16[160,128]{1,0:T(8,128)(2,1)S(1)} %get-tuple-element.33), channel_id=1, source_target_pairs={{0,4},{1,5},{4,12},{5,13},{8,9},{9,8},{12,0},{13,1},{2,6},{3,7},{6... | collective-permute-start | bytes 122888 | tf_op jit(solution)/shard_map/ppermute | solution.py:507
  9.0 5.4 %collective-permute-start.4 = (bf16[160,128]{1,0:T(8,128)(2,1)S(1)}, bf16[160,128]{1,0:T(8,128)(2,1)S(1)}, u32[]{:S(2)}, u32[]{:S(2)}) collective-permute-start(bf16[160,128]{1,0:T(8,128)(2,1)S(1)} %get-tuple-element.34), channel_id=1, source_target_pairs={{0,8},{1,9},{4,5},{5,4},{8,0},{9,1},{12,13},{13,12},{2,10},{3,11},... | collective-permute-start | bytes 122888 | tf_op jit(solution)/shard_map/ppermute | solution.py:507
  10.6 4.5 %collective-permute-start.5 = (bf16[160,128]{1,0:T(8,128)(2,1)S(1)}, bf16[160,128]{1,0:T(8,128)(2,1)S(1)}, u32[]{:S(2)}, u32[]{:S(2)}) collective-permute-start(bf16[160,128]{1,0:T(8,128)(2,1)S(1)} %get-tuple-element.35), channel_id=1, source_target_pairs={{0,12},{1,13},{4,0},{5,1},{8,4},{9,5},{12,8},{13,9},{2,14},{3,15},... | collective-permute-start | bytes 122888 | tf_op jit(solution)/shard_map/ppermute | solution.py:507
  11.7 3.4 %collective-permute-start.6 = (bf16[160,128]{1,0:T(8,128)(2,1)S(1)}, bf16[160,128]{1,0:T(8,128)(2,1)S(1)}, u32[]{:S(2)}, u32[]{:S(2)}) collective-permute-start(bf16[160,128]{1,0:T(8,128)(2,1)S(1)} %get-tuple-element.36), channel_id=1, source_target_pairs={{0,1},{1,0},{4,8},{5,9},{8,12},{9,13},{12,4},{13,5},{2,3},{3,2},{6... | collective-permute-start | bytes 122888 | tf_op jit(solution)/shard_map/ppermute | solution.py:507

commit v7 on v6

--- a/solution.py
+++ b/solution.py
@@ -58,7 +58,7 @@
 
 
 @functools.lru_cache(maxsize=None)
-def cell_tables():
+def cell_table():
     cells = SIDE * SIDE
 
     def at(row, column):
@@ -88,18 +88,11 @@
             if i < last:
                 carried[outer[i + 1][edge], block] += 2
     cell_map = np.concatenate([near @ near @ pool, carried, sums], axis=1)
-    first_corners = np.zeros((CORNER_ROWS, LANES))
-    last_corners = np.zeros((CORNER_ROWS, LANES))
-    first_corners[0, 0] = 1
-    first_corners[1, last] = 1
-    last_corners[2, LANES - SIDE] = 1
-    last_corners[3, LANES - 1] = 1
-    to_bf16 = lambda table: table.astype(ml_dtypes.bfloat16)
-    return cell_map.astype(ml_dtypes.float8_e4m3fn), to_bf16(first_corners), to_bf16(last_corners)
+    return cell_map.astype(ml_dtypes.float8_e4m3fn)
 
 
 @functools.lru_cache(maxsize=None)
-def time_tables(bands, samples):
+def time_table(bands, samples):
     per_band = FREQS // bands
     segments = samples // SEGLEN
     time = np.arange(SEGLEN)
@@ -111,7 +104,7 @@
     for segment in range(segments):
         table[:, segment, :, :, segment, :] = waves.reshape(2, bands, per_band, SEGLEN).transpose(1, 0, 2, 3)
     table = table.reshape(bands * segments * 2 * per_band, samples)
-    return split_bf16(table)
+    return np.concatenate(split_bf16(table), axis=0)
 
 
 def dot(left, right):
@@ -127,10 +120,7 @@
     paired_ref,
     x_ref,
     cells_ref,
-    first_ref,
-    last_ref,
-    high_ref,
-    low_ref,
+    waves_ref,
     near_ref,
     kept_codes_ref,
     partner_ref,
@@ -139,17 +129,23 @@
     outs, slot_ref = rest[:-1], rest[-1]
     place = place_ref[0]
     devices = len(outs)
-    rows = high_ref.shape[0] // devices
+    count = waves_ref.shape[0] // 2
+    rows = count // devices
     x = x_ref[...]
     sums = dot(x, cells_ref[...].astype(jnp.bfloat16))
     bands = [place] + [look_up(route, place) for route in routes]
     starts = [pl.multiple_of(band * rows, rows) for band in bands]
-    high = jnp.concatenate([high_ref[pl.ds(start, rows), :] for start in starts], axis=0)
-    low = jnp.concatenate([low_ref[pl.ds(start, rows), :] for start in starts], axis=0)
+    high = jnp.concatenate([waves_ref[pl.ds(start, rows), :] for start in starts], axis=0)
+    low = jnp.concatenate([waves_ref[pl.ds(count + start, rows), :] for start in starts], axis=0)
     across = (((1,), (1,)), ((), ()))
-    corners = lax.dot_general(first_ref[...], x[:, :LANES], across, preferred_element_type=jnp.float32)
+    row = lax.broadcasted_iota(jnp.int32, (CORNER_ROWS, LANES), 0)
+    lane = lax.broadcasted_iota(jnp.int32, (CORNER_ROWS, LANES), 1)
+    first = ((row == 0) & (lane == 0)) | ((row == 1) & (lane == SIDE - 1))
+    last = ((row == 2) & (lane == LANES - SIDE)) | ((row == 3) & (lane == LANES - 1))
+    first, last = (jnp.where(hit, 1.0, 0.0).astype(jnp.bfloat16) for hit in (first, last))
+    corners = lax.dot_general(first, x[:, :LANES], across, preferred_element_type=jnp.float32)
     corners += lax.dot_general(
-        last_ref[...], x[:, SIDE * SIDE - LANES :], across, preferred_element_type=jnp.float32
+        last, x[:, SIDE * SIDE - LANES :], across, preferred_element_type=jnp.float32
     )
     corners = corners.astype(jnp.bfloat16)
     corner_spectra = lax.dot_general(corners, high, across, preferred_element_type=jnp.float32)
@@ -442,7 +438,7 @@
             scalars((1, partners), jnp.int32),
         ]
         + [piece] * devices,
-        in_specs=[SMEM] * 5 + [VMEM] * 6,
+        in_specs=[SMEM] * 5 + [VMEM] * 3,
         out_specs=[SMEM] * 3 + [VMEM] * devices,
         scratch_shapes=[pltpu.SMEM((slots,), jnp.int32)],
         name="transform",
@@ -453,8 +449,8 @@
         neighbour_rotation_code,
         paired_tile_ids,
         field,
-        *cell_tables(),
-        *time_tables(devices, samples),
+        cell_table(),
+        time_table(devices, samples),
     )
     near_slots, codes, partner_slots = map(near_scalars, (near_slots, codes, partner_slots))
     pieces = [pieces[0]] + [

time: 17.3 us -> 17.3 us (level)
  no operation moved by 1% of the time
where the time goes in v7:
time: 17.3 us; the launch traced here: 17.2 us
  starting transfers between devices  8.48 us (49%)
  Pallas kernels  4.84 us (28%)
  waiting for transfers between devices  3.81 us (22%)
    ppermute x4, starting transfers between devices, shards(): bands.append(lax.ppermute(band, ('tiles', 'field'), pairs))  4.34 us
    ppermute x3, starting transfers between devices, shards(): lax.ppermute(piece, ('freq', 'field'), list(enumerate(route)))  4.14 us
    ppermute x4, waiting for transfers between devices, shards(): bands.append(lax.ppermute(band, ('tiles', 'field'), pairs))  2.63 us
    pallas_call x1, Pallas kernels, shards(): pl.pallas_call(functools.partial(density_kernel, arrivals, partners, scal...  2.05 us
    pallas_call x1, Pallas kernels, shards(): pl.pallas_call(functools.partial(transform_kernel, band_routes), out_shap...  1.51 us
    ppermute x3, waiting for transfers between devices, shards(): lax.ppermute(piece, ('freq', 'field'), list(enumerate(route)))  1.18 us
    pallas_call x1, Pallas kernels, shards(): pl.pallas_call(functools.partial(partner_map_kernel, tile_routes), out_sh...  0.77 us
  transfers between devices with their start and end apart: 7, of which 5 were waited for; matrix products, arithmetic and copies ran while one was open for 0% of the time, Pallas kernels for 6%

profile of v7, /device:TPU:0, one launch (start us, length us, event | category | flops | bytes accessed | tf_op | source)
XLA Modules:
  0.0 17.2 jit_solution(17259618507002043015)
XLA Ops:
  0.0 1.5 %transform.1 = (s32[4,4]{1,0:T(4,128)S(4)}, s32[4,4]{1,0:T(4,128)S(4)}, s32[1,2]{1,0:T(1,128)S(4)}, bf16[80,128]{1,0:T(8,128)(2,1)S(1)}, bf16[80,128]{1,0:T(8,12...) custom-call(s32[1]{0:T(128)} %bitcast.place_ref, s32[4]{0:T(128)} %ids_ref.1, s32[4,4]{1,0:T(4,128)} %near_ids_ref.1, ...), custom_call_target="tpu_custom_call" | custom-call | tf_op jit(solution)/shard_map/transform/pallas_call | solution.py:433
  1.5 0.5 %collective-permute-start = (bf16[80,128]{1,0:T(8,128)(2,1)S(1)}, bf16[80,128]{1,0:T(8,128)(2,1)S(1)}, u32[]{:S(2)}, u32[]{:S(2)}) collective-permute-start(bf16[80,128]{1,0:T(8,128)(2,1)S(1)} %get-tuple-element.24), channel_id=1, source_target_pairs={{0,1},{1,3},{2,0},{3,2},{4,5},{5,7},{6,4},{7,6},{8,9},{9,11},{10,8... | collective-permute-start | bytes 61448 | tf_op jit(solution)/shard_map/ppermute | solution.py:457
  2.0 2.6 %collective-permute-start.1 = (bf16[80,128]{1,0:T(8,128)(2,1)S(1)}, bf16[80,128]{1,0:T(8,128)(2,1)S(1)}, u32[]{:S(2)}, u32[]{:S(2)}) collective-permute-start(bf16[80,128]{1,0:T(8,128)(2,1)S(1)} %get-tuple-element.25), channel_id=1, source_target_pairs={{0,3},{1,2},{2,1},{3,0},{4,7},{5,6},{6,5},{7,4},{8,11},{9,10},{10,... | collective-permute-start | bytes 61448 | tf_op jit(solution)/shard_map/ppermute | solution.py:457
  4.6 1.1 %collective-permute-start.2 = (bf16[80,128]{1,0:T(8,128)(2,1)S(1)}, bf16[80,128]{1,0:T(8,128)(2,1)S(1)}, u32[]{:S(2)}, u32[]{:S(2)}) collective-permute-start(bf16[80,128]{1,0:T(8,128)(2,1)S(1)} %get-tuple-element.26), channel_id=1, source_target_pairs={{0,2},{1,0},{2,3},{3,1},{4,6},{5,4},{6,7},{7,5},{8,10},{9,8},{10,1... | collective-permute-start | bytes 61448 | tf_op jit(solution)/shard_map/ppermute | solution.py:457
  5.7 0.3 %rim_map.1.rim_map_ref = bf16[128,512]{1,0:T(8,128)(2,1)S(1)} custom-call(s32[1]{0:T(128)} %bitcast.1.tile_ref, s32[4,4]{1,0:T(4,128)S(4)} %get-tuple-element.21.near_ref, s32[4,4]{1,0:T(4,128)S(4)} %get-tuple-element.22.codes_ref), custom_call_target="tpu_custom_call" | custom-call | tf_op jit(solution)/shard_map/rim_map/pallas_call | solution.py:461
  6.0 0.3 %collective-permute-done.rest_1_ = bf16[80,128]{1,0:T(8,128)(2,1)S(1)} collective-permute-done((bf16[80,128]{1,0:T(8,128)(2,1)S(1)}, bf16[80,128]{1,0:T(8,128)(2,1)S(1)}, u32[]{:S(2)}, u32[]{:S(2)}) %collective-permute-start) | collective-permute-done | bytes 20512 | tf_op jit(solution)/shard_map/ppermute | solution.py:457
  6.3 0.0 collective-permute-done.1.rest_2_
  6.3 0.9 %collective-permute-done.2.rest_3_ = bf16[80,128]{1,0:T(8,128)(2,1)S(1)} collective-permute-done((bf16[80,128]{1,0:T(8,128)(2,1)S(1)}, bf16[80,128]{1,0:T(8,128)(2,1)S(1)}, u32[]{:S(2)}, u32[]{:S(2)}) %collective-permute-start.2) | collective-permute-done | bytes 20512 | tf_op jit(solution)/shard_map/ppermute | solution.py:457
  7.1 0.2 %collect.1 = (bf16[160,128]{1,0:T(8,128)(2,1)S(1)}, bf16[160,128]{1,0:T(8,128)(2,1)S(1)}, bf16[160,128]{1,0:T(8,128)(2,1)S(1)}, bf16[160,128]{1,0:T(8,128)(2,1)S...) custom-call(s32[1]{0:T(128)} %bitcast.place_ref, s32[1]{0:T(128)} %bitcast.1.tile_ref, ...), custom_call_target="tpu_custom_call" | custom-call | tf_op jit(solution)/shard_map/collect/pallas_call | solution.py:470
  7.4 1.6 %collective-permute-start.3 = (bf16[160,128]{1,0:T(8,128)(2,1)S(1)}, bf16[160,128]{1,0:T(8,128)(2,1)S(1)}, u32[]{:S(2)}, u32[]{:S(2)}) collective-permute-start(bf16[160,128]{1,0:T(8,128)(2,1)S(1)} %get-tuple-element.33), channel_id=1, source_target_pairs={{0,4},{1,5},{4,12},{5,13},{8,9},{9,8},{12,0},{13,1},{2,6},{3,7},{6... | collective-permute-start | bytes 122888 | tf_op jit(solution)/shard_map/ppermute | solution.py:503
  9.0 1.6 %collective-permute-start.4 = (bf16[160,128]{1,0:T(8,128)(2,1)S(1)}, bf16[160,128]{1,0:T(8,128)(2,1)S(1)}, u32[]{:S(2)}, u32[]{:S(2)}) collective-permute-start(bf16[160,128]{1,0:T(8,128)(2,1)S(1)} %get-tuple-element.34), channel_id=1, source_target_pairs={{0,8},{1,9},{4,5},{5,4},{8,0},{9,1},{12,13},{13,12},{2,10},{3,11},... | collective-permute-start | bytes 122888 | tf_op jit(solution)/shard_map/ppermute | solution.py:503
  10.6 1.1 %collective-permute-start.5 = (bf16[160,128]{1,0:T(8,128)(2,1)S(1)}, bf16[160,128]{1,0:T(8,128)(2,1)S(1)}, u32[]{:S(2)}, u32[]{:S(2)}) collective-permute-start(bf16[160,128]{1,0:T(8,128)(2,1)S(1)} %get-tuple-element.35), channel_id=1, source_target_pairs={{0,12},{1,13},{4,0},{5,1},{8,4},{9,5},{12,8},{13,9},{2,14},{3,15},... | collective-permute-start | bytes 122888 | tf_op jit(solution)/shard_map/ppermute | solution.py:503
  11.7 0.0 collective-permute-start.6
  11.7 0.8 %partner_map.1 = (bf16[640,256]{1,0:T(8,128)(2,1)S(1)}, bf16[640,384]{1,0:T(8,128)(2,1)S(1)}, f32[8,256]{1,0:T(8,128)S(1)}) custom-call(s32[1]{0:T(128)} %bitcast.1.tile_ref, s32[4,4]{1,0:T(4,128)S(4)} %get-tuple-element.21.near_ref, s32[4,4]{1,0:T(4,128)S(4)} %get-tuple-element.22.codes_ref, s32[1,2]{1,0:T(1,128)S(4)} %get-tuple-element.28.partner_ref), custom_call_target="tpu_custom_call" | custom-call | tf_op jit(solution)/shard_map/partner_map/pallas_call | solution.py:479
  12.5 1.0 %collective-permute-done.3.rest_1_ = bf16[160,128]{1,0:T(8,128)(2,1)S(1)} collective-permute-done((bf16[160,128]{1,0:T(8,128)(2,1)S(1)}, bf16[160,128]{1,0:T(8,128)(2,1)S(1)}, u32[]{:S(2)}, u32[]{:S(2)}) %collective-permute-start.3) | collective-permute-done | bytes 40992 | tf_op jit(solution)/shard_map/ppermute | solution.py:503
  13.5 0.9 %collective-permute-done.4.rest_2_ = bf16[160,128]{1,0:T(8,128)(2,1)S(1)} collective-permute-done((bf16[160,128]{1,0:T(8,128)(2,1)S(1)}, bf16[160,128]{1,0:T(8,128)(2,1)S(1)}, u32[]{:S(2)}, u32[]{:S(2)}) %collective-permute-start.4) | collective-permute-done | bytes 40992 | tf_op jit(solution)/shard_map/ppermute | solution.py:503
  14.4 0.8 %collective-permute-done.5.rest_3_ = bf16[160,128]{1,0:T(8,128)(2,1)S(1)} collective-permute-done((bf16[160,128]{1,0:T(8,128)(2,1)S(1)}, bf16[160,128]{1,0:T(8,128)(2,1)S(1)}, u32[]{:S(2)}, u32[]{:S(2)}) %collective-permute-start.5) | collective-permute-done | bytes 40992 | tf_op jit(solution)/shard_map/ppermute | solution.py:503
  15.1 0.0 collective-permute-done.6.rest_4_
  15.1 2.0 %density.1 = f32[4096,128]{1,0:T(8,128)} custom-call(bf16[64,128]{1,0:T(8,128)(2,1)S(1)} %get-tuple-element.27.height_ref, bf16[640,256]{1,0:T(8,128)(2,1)S(1)} %get-tuple-element.29.velocity_map_ref, bf16[640,384]{1,0:T(8,128)(2,1)S(1)} %get-tuple-element.30.rim_map_ref, f32[8,256]{1,0:T(8,128)S(1)} %get-tuple-element.31.chosen_ref, ...), custom_call_target="tpu_custom_call" | custom-call | tf_op jit(solution)/shard_map/density/pallas_call | solution.py:508
Async XLA Ops:
  1.5 4.8 %collective-permute-start = (bf16[80,128]{1,0:T(8,128)(2,1)S(1)}, bf16[80,128]{1,0:T(8,128)(2,1)S(1)}, u32[]{:S(2)}, u32[]{:S(2)}) collective-permute-start(bf16[80,128]{1,0:T(8,128)(2,1)S(1)} %get-tuple-element.24), channel_id=1, source_target_pairs={{0,1},{1,3},{2,0},{3,2},{4,5},{5,7},{6,4},{7,6},{8,9},{9,11},{10,8... | collective-permute-start | bytes 61448 | tf_op jit(solution)/shard_map/ppermute | solution.py:457
  2.0 4.3 %collective-permute-start.1 = (bf16[80,128]{1,0:T(8,128)(2,1)S(1)}, bf16[80,128]{1,0:T(8,128)(2,1)S(1)}, u32[]{:S(2)}, u32[]{:S(2)}) collective-permute-start(bf16[80,128]{1,0:T(8,128)(2,1)S(1)} %get-tuple-element.25), channel_id=1, source_target_pairs={{0,3},{1,2},{2,1},{3,0},{4,7},{5,6},{6,5},{7,4},{8,11},{9,10},{10,... | collective-permute-start | bytes 61448 | tf_op jit(solution)/shard_map/ppermute | solution.py:457
  4.6 2.5 %collective-permute-start.2 = (bf16[80,128]{1,0:T(8,128)(2,1)S(1)}, bf16[80,128]{1,0:T(8,128)(2,1)S(1)}, u32[]{:S(2)}, u32[]{:S(2)}) collective-permute-start(bf16[80,128]{1,0:T(8,128)(2,1)S(1)} %get-tuple-element.26), channel_id=1, source_target_pairs={{0,2},{1,0},{2,3},{3,1},{4,6},{5,4},{6,7},{7,5},{8,10},{9,8},{10,1... | collective-permute-start | bytes 61448 | tf_op jit(solution)/shard_map/ppermute | solution.py:457
  7.4 6.1 %collective-permute-start.3 = (bf16[160,128]{1,0:T(8,128)(2,1)S(1)}, bf16[160,128]{1,0:T(8,128)(2,1)S(1)}, u32[]{:S(2)}, u32[]{:S(2)}) collective-permute-start(bf16[160,128]{1,0:T(8,128)(2,1)S(1)} %get-tuple-element.33), channel_id=1, source_target_pairs={{0,4},{1,5},{4,12},{5,13},{8,9},{9,8},{12,0},{13,1},{2,6},{3,7},{6... | collective-permute-start | bytes 122888 | tf_op jit(solution)/shard_map/ppermute | solution.py:503
  9.0 5.4 %collective-permute-start.4 = (bf16[160,128]{1,0:T(8,128)(2,1)S(1)}, bf16[160,128]{1,0:T(8,128)(2,1)S(1)}, u32[]{:S(2)}, u32[]{:S(2)}) collective-permute-start(bf16[160,128]{1,0:T(8,128)(2,1)S(1)} %get-tuple-element.34), channel_id=1, source_target_pairs={{0,8},{1,9},{4,5},{5,4},{8,0},{9,1},{12,13},{13,12},{2,10},{3,11},... | collective-permute-start | bytes 122888 | tf_op jit(solution)/shard_map/ppermute | solution.py:503
  10.6 4.5 %collective-permute-start.5 = (bf16[160,128]{1,0:T(8,128)(2,1)S(1)}, bf16[160,128]{1,0:T(8,128)(2,1)S(1)}, u32[]{:S(2)}, u32[]{:S(2)}) collective-permute-start(bf16[160,128]{1,0:T(8,128)(2,1)S(1)} %get-tuple-element.35), channel_id=1, source_target_pairs={{0,12},{1,13},{4,0},{5,1},{8,4},{9,5},{12,8},{13,9},{2,14},{3,15},... | collective-permute-start | bytes 122888 | tf_op jit(solution)/shard_map/ppermute | solution.py:503
  11.7 3.4 %collective-permute-start.6 = (bf16[160,128]{1,0:T(8,128)(2,1)S(1)}, bf16[160,128]{1,0:T(8,128)(2,1)S(1)}, u32[]{:S(2)}, u32[]{:S(2)}) collective-permute-start(bf16[160,128]{1,0:T(8,128)(2,1)S(1)} %get-tuple-element.36), channel_id=1, source_target_pairs={{0,1},{1,0},{4,8},{5,9},{8,12},{9,13},{12,4},{13,5},{2,3},{3,2},{6... | collective-permute-start | bytes 122888 | tf_op jit(solution)/shard_map/ppermute | solution.py:503

commit v8 on v7

--- a/solution.py
+++ b/solution.py
@@ -350,22 +350,41 @@
     rim_map_ref[...] = rim_ref[...].astype(jnp.bfloat16)
 
 
-def density_kernel(
-    arrivals, partners, scale, per_band, height_ref, velocity_map_ref, rim_map_ref, chosen_ref, *rest
-):
-    bands, (out_ref, cross_ref, sent) = rest[:arrivals], rest[arrivals:]
-    total = height_ref.shape[0]
+def add_arrivals(height, velocity, first, bands, velocity_map_ref, rim_map_ref, chosen_ref):
+    total = height.shape[0]
+    partners = velocity.shape[1] // LANES
+    rows = slice(first * LANES, (first + len(bands)) * LANES)
     rims = jnp.concatenate([band[2 * total :, :] for band in bands], axis=1)
     first_half = lax.broadcasted_iota(jnp.int32, rims.shape, 1) % LANES < HALF
     rims = rims.astype(jnp.float32)
     rims = jnp.concatenate([jnp.where(first_half, rims, 0.0), jnp.where(first_half, 0.0, rims)], axis=0)
-    rims = dot(rims.astype(jnp.bfloat16), rim_map_ref[...])
-    height = height_ref[...].astype(jnp.float32) + rims[:, :LANES]
-    velocity = dot(jnp.concatenate([band[total : 2 * total, :] for band in bands], axis=1), velocity_map_ref[...])
-    velocity += rims[:, LANES:]
-    for step in range(arrivals):
-        own = bands[step][0:total, :].astype(jnp.float32)
-        velocity += jnp.concatenate([own] * partners, axis=1) * chosen_ref[step : step + 1, :]
+    rims = dot(rims.astype(jnp.bfloat16), rim_map_ref[rows, :])
+    pairs = jnp.concatenate([band[total : 2 * total, :] for band in bands], axis=1)
+    velocity = velocity + dot(pairs, velocity_map_ref[rows, :]) + rims[:, LANES:]
+    for step, band in enumerate(bands):
+        own = band[0:total, :].astype(jnp.float32)
+        chosen = chosen_ref[first + step : first + step + 1, :]
+        velocity += jnp.concatenate([own] * partners, axis=1) * chosen
+    return height + rims[:, :LANES], velocity
+
+
+def early_kernel(height_ref, velocity_map_ref, rim_map_ref, chosen_ref, *rest):
+    bands, (height_sum_ref, velocity_sum_ref) = rest[:-2], rest[-2:]
+    height = height_ref[...].astype(jnp.float32)
+    velocity = jnp.zeros(velocity_sum_ref.shape, jnp.float32)
+    height, velocity = add_arrivals(height, velocity, 0, bands, velocity_map_ref, rim_map_ref, chosen_ref)
+    height_sum_ref[...] = height
+    velocity_sum_ref[...] = velocity
+
+
+def density_kernel(
+    early, partners, scale, per_band, height_ref, velocity_ref, velocity_map_ref, rim_map_ref, chosen_ref, *rest
+):
+    bands, (out_ref, cross_ref, sent) = rest[:-3], rest[-3:]
+    total = height_ref.shape[0]
+    height, velocity = add_arrivals(
+        height_ref[...], velocity_ref[...], early, bands, velocity_map_ref, rim_map_ref, chosen_ref
+    )
     velocity = velocity.astype(jnp.bfloat16)
     height = height.astype(jnp.bfloat16).astype(jnp.float32)
     row = lax.broadcasted_iota(jnp.int32, height.shape, 0)
@@ -502,20 +521,29 @@
                 pairs.append((sender * field_count + core, there))
         bands.append(lax.ppermute(band, ("tiles", "field"), pairs))
 
+    early = arrivals - 2
+    height, velocity = pl.pallas_call(
+        early_kernel,
+        out_shape=[kept((total, LANES), jnp.float32), kept((total, partners * LANES), jnp.float32)],
+        in_specs=[VMEM] * (4 + early),
+        out_specs=[VMEM] * 2,
+        name="early",
+    )(*map(near, (height, velocity_map, rim_map, chosen, *bands[:early])))
+
     segments = freqs * samples // SEGLEN
     scale = 1.0 / (segments * SEGLEN * 0.375)
     blocks = partners * 2 * per_band
     density = pl.pallas_call(
-        functools.partial(density_kernel, arrivals, partners, scale, per_band),
+        functools.partial(density_kernel, early, partners, scale, per_band),
         out_shape=jax.ShapeDtypeStruct((blocks * LANES, LANES), jnp.float32),
-        in_specs=[VMEM] * (4 + arrivals),
+        in_specs=[VMEM] * (5 + arrivals - early),
         out_specs=pl.BlockSpec(memory_space=pl.ANY),
         scratch_shapes=[
             pltpu.VMEM((blocks * LANES, LANES), jnp.float32),
             pltpu.SemaphoreType.DMA((blocks,)),
         ],
         name="density",
-    )(*map(near, (height, velocity_map, rim_map, chosen, *bands)))
+    )(*map(near, (height, velocity, velocity_map, rim_map, chosen, *bands[early:])))
     return density.reshape(1, partners, 2, per_band, LANES, LANES)
 
 

time: 17.3 us -> 17.2 us (level)
  waiting for transfers between devices: 3.81 us -> 3.6 us
    ppermute x4, waiting for transfers between devices: 2.63 us -> 2.41 us  [shards(): bands.append(lax.ppermute(band, ('tiles', 'field'), pairs))]
    pallas_call x1 -> x2, Pallas kernels: 2.05 us -> 2.18 us  [the longest x1 1.98 us: shards(): pl.pallas_call(functools.partial(density_kernel, early, partners, scale,...]
  transfers between devices with their start and end apart: 7 -> 7, of which waited for: 5 -> 5; matrix products, arithmetic and copies ran while one was open for 0% -> 0% of each run, Pallas kernels for 6% -> 7%
where the time goes in v8:
time: 17.2 us; the launch traced here: 17.1 us
  starting transfers between devices  8.48 us (49%)
  Pallas kernels  4.98 us (29%)
  waiting for transfers between devices  3.6 us (21%)
    ppermute x4, starting transfers between devices, shards(): bands.append(lax.ppermute(band, ('tiles', 'field'), pairs))  4.34 us
    ppermute x3, starting transfers between devices, shards(): lax.ppermute(piece, ('freq', 'field'), list(enumerate(route)))  4.14 us
    ppermute x4, waiting for transfers between devices, shards(): bands.append(lax.ppermute(band, ('tiles', 'field'), pairs))  2.41 us
    pallas_call x1, Pallas kernels, shards(): pl.pallas_call(functools.partial(density_kernel, early, partners, scale,...  1.98 us
    pallas_call x1, Pallas kernels, shards(): pl.pallas_call(functools.partial(transform_kernel, band_routes), out_shap...  1.51 us
    ppermute x3, waiting for transfers between devices, shards(): lax.ppermute(piece, ('freq', 'field'), list(enumerate(route)))  1.18 us
    pallas_call x1, Pallas kernels, shards(): pl.pallas_call(functools.partial(partner_map_kernel, tile_routes), out_sh...  0.77 us
  transfers between devices with their start and end apart: 7, of which 5 were waited for; matrix products, arithmetic and copies ran while one was open for 0% of the time, Pallas kernels for 7%

profile of v8, /device:TPU:0, one launch (start us, length us, event | category | flops | bytes accessed | tf_op | source)
XLA Modules:
  0.0 17.1 jit_solution(16556357212958180334)
XLA Ops:
  0.0 1.5 %transform.1 = (s32[4,4]{1,0:T(4,128)S(4)}, s32[4,4]{1,0:T(4,128)S(4)}, s32[1,2]{1,0:T(1,128)S(4)}, bf16[80,128]{1,0:T(8,128)(2,1)S(1)}, bf16[80,128]{1,0:T(8,12...) custom-call(s32[1]{0:T(128)} %bitcast.place_ref, s32[4]{0:T(128)} %ids_ref.1, s32[4,4]{1,0:T(4,128)} %near_ids_ref.1, ...), custom_call_target="tpu_custom_call" | custom-call | tf_op jit(solution)/shard_map/transform/pallas_call | solution.py:452
  1.5 0.5 %collective-permute-start = (bf16[80,128]{1,0:T(8,128)(2,1)S(1)}, bf16[80,128]{1,0:T(8,128)(2,1)S(1)}, u32[]{:S(2)}, u32[]{:S(2)}) collective-permute-start(bf16[80,128]{1,0:T(8,128)(2,1)S(1)} %get-tuple-element.26), channel_id=1, source_target_pairs={{0,1},{1,3},{2,0},{3,2},{4,5},{5,7},{6,4},{7,6},{8,9},{9,11},{10,8... | collective-permute-start | bytes 61448 | tf_op jit(solution)/shard_map/ppermute | solution.py:476
  2.0 2.6 %collective-permute-start.1 = (bf16[80,128]{1,0:T(8,128)(2,1)S(1)}, bf16[80,128]{1,0:T(8,128)(2,1)S(1)}, u32[]{:S(2)}, u32[]{:S(2)}) collective-permute-start(bf16[80,128]{1,0:T(8,128)(2,1)S(1)} %get-tuple-element.27), channel_id=1, source_target_pairs={{0,3},{1,2},{2,1},{3,0},{4,7},{5,6},{6,5},{7,4},{8,11},{9,10},{10,... | collective-permute-start | bytes 61448 | tf_op jit(solution)/shard_map/ppermute | solution.py:476
  4.6 1.1 %collective-permute-start.2 = (bf16[80,128]{1,0:T(8,128)(2,1)S(1)}, bf16[80,128]{1,0:T(8,128)(2,1)S(1)}, u32[]{:S(2)}, u32[]{:S(2)}) collective-permute-start(bf16[80,128]{1,0:T(8,128)(2,1)S(1)} %get-tuple-element.28), channel_id=1, source_target_pairs={{0,2},{1,0},{2,3},{3,1},{4,6},{5,4},{6,7},{7,5},{8,10},{9,8},{10,1... | collective-permute-start | bytes 61448 | tf_op jit(solution)/shard_map/ppermute | solution.py:476
  5.7 0.3 %rim_map.1.rim_map_ref = bf16[128,512]{1,0:T(8,128)(2,1)S(1)} custom-call(s32[1]{0:T(128)} %bitcast.1.tile_ref, s32[4,4]{1,0:T(4,128)S(4)} %get-tuple-element.23.near_ref, s32[4,4]{1,0:T(4,128)S(4)} %get-tuple-element.24.codes_ref), custom_call_target="tpu_custom_call" | custom-call | tf_op jit(solution)/shard_map/rim_map/pallas_call | solution.py:480
  6.0 0.3 %collective-permute-done.rest_1_ = bf16[80,128]{1,0:T(8,128)(2,1)S(1)} collective-permute-done((bf16[80,128]{1,0:T(8,128)(2,1)S(1)}, bf16[80,128]{1,0:T(8,128)(2,1)S(1)}, u32[]{:S(2)}, u32[]{:S(2)}) %collective-permute-start) | collective-permute-done | bytes 20512 | tf_op jit(solution)/shard_map/ppermute | solution.py:476
  6.3 0.0 collective-permute-done.1.rest_2_
  6.3 0.9 %collective-permute-done.2.rest_3_ = bf16[80,128]{1,0:T(8,128)(2,1)S(1)} collective-permute-done((bf16[80,128]{1,0:T(8,128)(2,1)S(1)}, bf16[80,128]{1,0:T(8,128)(2,1)S(1)}, u32[]{:S(2)}, u32[]{:S(2)}) %collective-permute-start.2) | collective-permute-done | bytes 20512 | tf_op jit(solution)/shard_map/ppermute | solution.py:476
  7.1 0.2 %collect.1 = (bf16[160,128]{1,0:T(8,128)(2,1)S(1)}, bf16[160,128]{1,0:T(8,128)(2,1)S(1)}, bf16[160,128]{1,0:T(8,128)(2,1)S(1)}, bf16[160,128]{1,0:T(8,128)(2,1)S...) custom-call(s32[1]{0:T(128)} %bitcast.place_ref, s32[1]{0:T(128)} %bitcast.1.tile_ref, ...), custom_call_target="tpu_custom_call" | custom-call | tf_op jit(solution)/shard_map/collect/pallas_call | solution.py:489
  7.4 1.6 %collective-permute-start.3 = (bf16[160,128]{1,0:T(8,128)(2,1)S(1)}, bf16[160,128]{1,0:T(8,128)(2,1)S(1)}, u32[]{:S(2)}, u32[]{:S(2)}) collective-permute-start(bf16[160,128]{1,0:T(8,128)(2,1)S(1)} %get-tuple-element.35), channel_id=1, source_target_pairs={{0,4},{1,5},{4,12},{5,13},{8,9},{9,8},{12,0},{13,1},{2,6},{3,7},{6... | collective-permute-start | bytes 122888 | tf_op jit(solution)/shard_map/ppermute | solution.py:522
  9.0 1.6 %collective-permute-start.4 = (bf16[160,128]{1,0:T(8,128)(2,1)S(1)}, bf16[160,128]{1,0:T(8,128)(2,1)S(1)}, u32[]{:S(2)}, u32[]{:S(2)}) collective-permute-start(bf16[160,128]{1,0:T(8,128)(2,1)S(1)} %get-tuple-element.36), channel_id=1, source_target_pairs={{0,8},{1,9},{4,5},{5,4},{8,0},{9,1},{12,13},{13,12},{2,10},{3,11},... | collective-permute-start | bytes 122888 | tf_op jit(solution)/shard_map/ppermute | solution.py:522
  10.6 1.1 %collective-permute-start.5 = (bf16[160,128]{1,0:T(8,128)(2,1)S(1)}, bf16[160,128]{1,0:T(8,128)(2,1)S(1)}, u32[]{:S(2)}, u32[]{:S(2)}) collective-permute-start(bf16[160,128]{1,0:T(8,128)(2,1)S(1)} %get-tuple-element.39), channel_id=1, source_target_pairs={{0,12},{1,13},{4,0},{5,1},{8,4},{9,5},{12,8},{13,9},{2,14},{3,15},... | collective-permute-start | bytes 122888 | tf_op jit(solution)/shard_map/ppermute | solution.py:522
  11.7 0.0 collective-permute-start.6
  11.7 0.8 %partner_map.1 = (bf16[640,256]{1,0:T(8,128)(2,1)S(1)}, bf16[640,384]{1,0:T(8,128)(2,1)S(1)}, f32[8,256]{1,0:T(8,128)S(1)}) custom-call(s32[1]{0:T(128)} %bitcast.1.tile_ref, s32[4,4]{1,0:T(4,128)S(4)} %get-tuple-element.23.near_ref, s32[4,4]{1,0:T(4,128)S(4)} %get-tuple-element.24.codes_ref, s32[1,2]{1,0:T(1,128)S(4)} %get-tuple-element.30.partner_ref), custom_call_target="tpu_custom_call" | custom-call | tf_op jit(solution)/shard_map/partner_map/pallas_call | solution.py:498
  12.5 1.0 %collective-permute-done.3.rest_1_ = bf16[160,128]{1,0:T(8,128)(2,1)S(1)} collective-permute-done((bf16[160,128]{1,0:T(8,128)(2,1)S(1)}, bf16[160,128]{1,0:T(8,128)(2,1)S(1)}, u32[]{:S(2)}, u32[]{:S(2)}) %collective-permute-start.3) | collective-permute-done | bytes 40992 | tf_op jit(solution)/shard_map/ppermute | solution.py:522
  13.5 0.9 %collective-permute-done.4.rest_2_ = bf16[160,128]{1,0:T(8,128)(2,1)S(1)} collective-permute-done((bf16[160,128]{1,0:T(8,128)(2,1)S(1)}, bf16[160,128]{1,0:T(8,128)(2,1)S(1)}, u32[]{:S(2)}, u32[]{:S(2)}) %collective-permute-start.4) | collective-permute-done | bytes 40992 | tf_op jit(solution)/shard_map/ppermute | solution.py:522
  14.4 0.2 %early.1 = (f32[64,128]{1,0:T(8,128)S(1)}, f32[64,256]{1,0:T(8,128)S(1)}) custom-call(bf16[64,128]{1,0:T(8,128)(2,1)S(1)} %get-tuple-element.29.height_ref, bf16[640,256]{1,0:T(8,128)(2,1)S(1)} %get-tuple-element.31.velocity_map_ref, bf16[640,384]{1,0:T(8,128)(2,1)S(1)} %get-tuple-element.32.rim_map_ref, f32[8,256]{1,0:T(8,128)S(1)} %get-tuple-element.33.chosen_ref, ...), custom_call_target="tpu_custom_call" | custom-call | tf_op jit(solution)/shard_map/early/pallas_call | solution.py:525
  14.6 0.6 %collective-permute-done.5.rest_0_ = bf16[160,128]{1,0:T(8,128)(2,1)S(1)} collective-permute-done((bf16[160,128]{1,0:T(8,128)(2,1)S(1)}, bf16[160,128]{1,0:T(8,128)(2,1)S(1)}, u32[]{:S(2)}, u32[]{:S(2)}) %collective-permute-start.5) | collective-permute-done | bytes 40992 | tf_op jit(solution)/shard_map/ppermute | solution.py:522
  15.1 0.0 collective-permute-done.6.rest_1_
  15.1 2.0 %density.1 = f32[4096,128]{1,0:T(8,128)} custom-call(f32[64,128]{1,0:T(8,128)S(1)} %get-tuple-element.37.height_ref, f32[64,256]{1,0:T(8,128)S(1)} %get-tuple-element.38.velocity_ref, bf16[640,256]{1,0:T(8,128)(2,1)S(1)} %get-tuple-element.31.velocity_map_ref, bf16[640,384]{1,0:T(8,128)(2,1)S(1)} %get-tuple-element.32.rim_map_ref, ...), custom_call_target="tpu_custom_call" | custom-call | tf_op jit(solution)/shard_map/density/pallas_call | solution.py:536
Async XLA Ops:
  1.5 4.8 %collective-permute-start = (bf16[80,128]{1,0:T(8,128)(2,1)S(1)}, bf16[80,128]{1,0:T(8,128)(2,1)S(1)}, u32[]{:S(2)}, u32[]{:S(2)}) collective-permute-start(bf16[80,128]{1,0:T(8,128)(2,1)S(1)} %get-tuple-element.26), channel_id=1, source_target_pairs={{0,1},{1,3},{2,0},{3,2},{4,5},{5,7},{6,4},{7,6},{8,9},{9,11},{10,8... | collective-permute-start | bytes 61448 | tf_op jit(solution)/shard_map/ppermute | solution.py:476
  2.0 4.3 %collective-permute-start.1 = (bf16[80,128]{1,0:T(8,128)(2,1)S(1)}, bf16[80,128]{1,0:T(8,128)(2,1)S(1)}, u32[]{:S(2)}, u32[]{:S(2)}) collective-permute-start(bf16[80,128]{1,0:T(8,128)(2,1)S(1)} %get-tuple-element.27), channel_id=1, source_target_pairs={{0,3},{1,2},{2,1},{3,0},{4,7},{5,6},{6,5},{7,4},{8,11},{9,10},{10,... | collective-permute-start | bytes 61448 | tf_op jit(solution)/shard_map/ppermute | solution.py:476
  4.6 2.5 %collective-permute-start.2 = (bf16[80,128]{1,0:T(8,128)(2,1)S(1)}, bf16[80,128]{1,0:T(8,128)(2,1)S(1)}, u32[]{:S(2)}, u32[]{:S(2)}) collective-permute-start(bf16[80,128]{1,0:T(8,128)(2,1)S(1)} %get-tuple-element.28), channel_id=1, source_target_pairs={{0,2},{1,0},{2,3},{3,1},{4,6},{5,4},{6,7},{7,5},{8,10},{9,8},{10,1... | collective-permute-start | bytes 61448 | tf_op jit(solution)/shard_map/ppermute | solution.py:476
  7.4 6.1 %collective-permute-start.3 = (bf16[160,128]{1,0:T(8,128)(2,1)S(1)}, bf16[160,128]{1,0:T(8,128)(2,1)S(1)}, u32[]{:S(2)}, u32[]{:S(2)}) collective-permute-start(bf16[160,128]{1,0:T(8,128)(2,1)S(1)} %get-tuple-element.35), channel_id=1, source_target_pairs={{0,4},{1,5},{4,12},{5,13},{8,9},{9,8},{12,0},{13,1},{2,6},{3,7},{6... | collective-permute-start | bytes 122888 | tf_op jit(solution)/shard_map/ppermute | solution.py:522
  9.0 5.4 %collective-permute-start.4 = (bf16[160,128]{1,0:T(8,128)(2,1)S(1)}, bf16[160,128]{1,0:T(8,128)(2,1)S(1)}, u32[]{:S(2)}, u32[]{:S(2)}) collective-permute-start(bf16[160,128]{1,0:T(8,128)(2,1)S(1)} %get-tuple-element.36), channel_id=1, source_target_pairs={{0,8},{1,9},{4,5},{5,4},{8,0},{9,1},{12,13},{13,12},{2,10},{3,11},... | collective-permute-start | bytes 122888 | tf_op jit(solution)/shard_map/ppermute | solution.py:522
  10.6 4.5 %collective-permute-start.5 = (bf16[160,128]{1,0:T(8,128)(2,1)S(1)}, bf16[160,128]{1,0:T(8,128)(2,1)S(1)}, u32[]{:S(2)}, u32[]{:S(2)}) collective-permute-start(bf16[160,128]{1,0:T(8,128)(2,1)S(1)} %get-tuple-element.39), channel_id=1, source_target_pairs={{0,12},{1,13},{4,0},{5,1},{8,4},{9,5},{12,8},{13,9},{2,14},{3,15},... | collective-permute-start | bytes 122888 | tf_op jit(solution)/shard_map/ppermute | solution.py:522
  11.7 3.4 %collective-permute-start.6 = (bf16[160,128]{1,0:T(8,128)(2,1)S(1)}, bf16[160,128]{1,0:T(8,128)(2,1)S(1)}, u32[]{:S(2)}, u32[]{:S(2)}) collective-permute-start(bf16[160,128]{1,0:T(8,128)(2,1)S(1)} %get-tuple-element.40), channel_id=1, source_target_pairs={{0,1},{1,0},{4,8},{5,9},{8,12},{9,13},{12,4},{13,5},{2,3},{3,2},{6... | collective-permute-start | bytes 122888 | tf_op jit(solution)/shard_map/ppermute | solution.py:522

commit v9 on v8

--- a/solution.py
+++ b/solution.py
@@ -30,7 +30,7 @@
     ((NORTH, 0), (SOUTH, 0)),
 )
 
-BAND_ROUTES = ((1, 3, 0, 2), (3, 2, 1, 0), (2, 0, 3, 1))
+BAND_ROUTES = ((2, 3, 0, 1), (3, 2, 1, 0), (1, 0, 3, 2))
 TILE_ROUTES = ((1, 3, 2, 0), (2, 1, 0, 3), (3, 0, 1, 2), (0, 2, 3, 1))
 
 

time: 17.2 us -> 17.3 us (level)
  waiting for transfers between devices: 3.6 us -> 4.79 us
  starting transfers between devices: 8.48 us -> 7.3 us
    ppermute x3, waiting for transfers between devices: 1.18 us -> 2.72 us  [shards(): lax.ppermute(piece, ('freq', 'field'), list(enumerate(route)))]
    ppermute x3, starting transfers between devices: 4.14 us -> 3.2 us  [shards(): lax.ppermute(piece, ('freq', 'field'), list(enumerate(route)))]
    ppermute x4, waiting for transfers between devices: 2.41 us -> 2.07 us  [shards(): bands.append(lax.ppermute(band, ('tiles', 'field'), pairs))]
    ppermute x4, starting transfers between devices: 4.34 us -> 4.11 us  [shards(): bands.append(lax.ppermute(band, ('tiles', 'field'), pairs))]
where the time goes in v9:
time: 17.3 us; the launch traced here: 17.1 us
  starting transfers between devices  7.3 us (42%)
  Pallas kernels  4.98 us (29%)
  waiting for transfers between devices  4.79 us (28%)
    ppermute x4, starting transfers between devices, shards(): bands.append(lax.ppermute(band, ('tiles', 'field'), pairs))  4.11 us
    ppermute x3, starting transfers between devices, shards(): lax.ppermute(piece, ('freq', 'field'), list(enumerate(route)))  3.2 us
    ppermute x3, waiting for transfers between devices, shards(): lax.ppermute(piece, ('freq', 'field'), list(enumerate(route)))  2.72 us
    ppermute x4, waiting for transfers between devices, shards(): bands.append(lax.ppermute(band, ('tiles', 'field'), pairs))  2.07 us
    pallas_call x1, Pallas kernels, shards(): pl.pallas_call(functools.partial(density_kernel, early, partners, scale,...  1.98 us
    pallas_call x1, Pallas kernels, shards(): pl.pallas_call(functools.partial(transform_kernel, band_routes), out_shap...  1.51 us
    pallas_call x1, Pallas kernels, shards(): pl.pallas_call(functools.partial(partner_map_kernel, tile_routes), out_sh...  0.77 us
  transfers between devices with their start and end apart: 7, of which 5 were waited for; matrix products, arithmetic and copies ran while one was open for 0% of the time, Pallas kernels for 7%

profile of v9, /device:TPU:0, one launch (start us, length us, event | category | flops | bytes accessed | tf_op | source)
XLA Modules:
  0.0 17.1 jit_solution(3376104189011069190)
XLA Ops:
  0.0 1.5 %transform.1 = (s32[4,4]{1,0:T(4,128)S(4)}, s32[4,4]{1,0:T(4,128)S(4)}, s32[1,2]{1,0:T(1,128)S(4)}, bf16[80,128]{1,0:T(8,128)(2,1)S(1)}, bf16[80,128]{1,0:T(8,12...) custom-call(s32[1]{0:T(128)} %bitcast.place_ref, s32[4]{0:T(128)} %ids_ref.1, s32[4,4]{1,0:T(4,128)} %near_ids_ref.1, ...), custom_call_target="tpu_custom_call" | custom-call | tf_op jit(solution)/shard_map/transform/pallas_call | solution.py:452
  1.5 3.0 %collective-permute-start = (bf16[80,128]{1,0:T(8,128)(2,1)S(1)}, bf16[80,128]{1,0:T(8,128)(2,1)S(1)}, u32[]{:S(2)}, u32[]{:S(2)}) collective-permute-start(bf16[80,128]{1,0:T(8,128)(2,1)S(1)} %get-tuple-element.26), channel_id=1, source_target_pairs={{0,2},{1,3},{2,0},{3,1},{4,6},{5,7},{6,4},{7,5},{8,10},{9,11},{10,... | collective-permute-start | bytes 61448 | tf_op jit(solution)/shard_map/ppermute | solution.py:476
  4.5 0.0 collective-permute-start.1
  4.5 0.2 %collective-permute-start.2 = (bf16[80,128]{1,0:T(8,128)(2,1)S(1)}, bf16[80,128]{1,0:T(8,128)(2,1)S(1)}, u32[]{:S(2)}, u32[]{:S(2)}) collective-permute-start(bf16[80,128]{1,0:T(8,128)(2,1)S(1)} %get-tuple-element.28), channel_id=1, source_target_pairs={{0,1},{1,0},{2,3},{3,2},{4,5},{5,4},{6,7},{7,6},{8,9},{9,8},{10,11... | collective-permute-start | bytes 61448 | tf_op jit(solution)/shard_map/ppermute | solution.py:476
  4.7 0.3 %rim_map.1.rim_map_ref = bf16[128,512]{1,0:T(8,128)(2,1)S(1)} custom-call(s32[1]{0:T(128)} %bitcast.1.tile_ref, s32[4,4]{1,0:T(4,128)S(4)} %get-tuple-element.23.near_ref, s32[4,4]{1,0:T(4,128)S(4)} %get-tuple-element.24.codes_ref), custom_call_target="tpu_custom_call" | custom-call | tf_op jit(solution)/shard_map/rim_map/pallas_call | solution.py:480
  5.0 1.3 %collective-permute-done.rest_1_ = bf16[80,128]{1,0:T(8,128)(2,1)S(1)} collective-permute-done((bf16[80,128]{1,0:T(8,128)(2,1)S(1)}, bf16[80,128]{1,0:T(8,128)(2,1)S(1)}, u32[]{:S(2)}, u32[]{:S(2)}) %collective-permute-start) | collective-permute-done | bytes 20512 | tf_op jit(solution)/shard_map/ppermute | solution.py:476
  6.3 1.4 %collective-permute-done.1.rest_2_ = bf16[80,128]{1,0:T(8,128)(2,1)S(1)} collective-permute-done((bf16[80,128]{1,0:T(8,128)(2,1)S(1)}, bf16[80,128]{1,0:T(8,128)(2,1)S(1)}, u32[]{:S(2)}, u32[]{:S(2)}) %collective-permute-start.1) | collective-permute-done | bytes 20512 | tf_op jit(solution)/shard_map/ppermute | solution.py:476
  7.7 0.0 collective-permute-done.2.rest_3_
  7.7 0.2 %collect.1 = (bf16[160,128]{1,0:T(8,128)(2,1)S(1)}, bf16[160,128]{1,0:T(8,128)(2,1)S(1)}, bf16[160,128]{1,0:T(8,128)(2,1)S(1)}, bf16[160,128]{1,0:T(8,128)(2,1)S...) custom-call(s32[1]{0:T(128)} %bitcast.place_ref, s32[1]{0:T(128)} %bitcast.1.tile_ref, ...), custom_call_target="tpu_custom_call" | custom-call | tf_op jit(solution)/shard_map/collect/pallas_call | solution.py:489
  8.0 1.6 %collective-permute-start.3 = (bf16[160,128]{1,0:T(8,128)(2,1)S(1)}, bf16[160,128]{1,0:T(8,128)(2,1)S(1)}, u32[]{:S(2)}, u32[]{:S(2)}) collective-permute-start(bf16[160,128]{1,0:T(8,128)(2,1)S(1)} %get-tuple-element.35), channel_id=1, source_target_pairs={{0,4},{1,5},{4,12},{5,13},{8,9},{9,8},{12,0},{13,1},{2,6},{3,7},{6... | collective-permute-start | bytes 122888 | tf_op jit(solution)/shard_map/ppermute | solution.py:522
  9.6 1.1 %collective-permute-start.4 = (bf16[160,128]{1,0:T(8,128)(2,1)S(1)}, bf16[160,128]{1,0:T(8,128)(2,1)S(1)}, u32[]{:S(2)}, u32[]{:S(2)}) collective-permute-start(bf16[160,128]{1,0:T(8,128)(2,1)S(1)} %get-tuple-element.36), channel_id=1, source_target_pairs={{0,8},{1,9},{4,5},{5,4},{8,0},{9,1},{12,13},{13,12},{2,10},{3,11},... | collective-permute-start | bytes 122888 | tf_op jit(solution)/shard_map/ppermute | solution.py:522
  10.7 1.2 %collective-permute-start.5 = (bf16[160,128]{1,0:T(8,128)(2,1)S(1)}, bf16[160,128]{1,0:T(8,128)(2,1)S(1)}, u32[]{:S(2)}, u32[]{:S(2)}) collective-permute-start(bf16[160,128]{1,0:T(8,128)(2,1)S(1)} %get-tuple-element.39), channel_id=1, source_target_pairs={{0,12},{1,13},{4,0},{5,1},{8,4},{9,5},{12,8},{13,9},{2,14},{3,15},... | collective-permute-start | bytes 122888 | tf_op jit(solution)/shard_map/ppermute | solution.py:522
  11.8 0.2 %collective-permute-start.6 = (bf16[160,128]{1,0:T(8,128)(2,1)S(1)}, bf16[160,128]{1,0:T(8,128)(2,1)S(1)}, u32[]{:S(2)}, u32[]{:S(2)}) collective-permute-start(bf16[160,128]{1,0:T(8,128)(2,1)S(1)} %get-tuple-element.40), channel_id=1, source_target_pairs={{0,1},{1,0},{4,8},{5,9},{8,12},{9,13},{12,4},{13,5},{2,3},{3,2},{6... | collective-permute-start | bytes 122888 | tf_op jit(solution)/shard_map/ppermute | solution.py:522
  12.1 0.8 %partner_map.1 = (bf16[640,256]{1,0:T(8,128)(2,1)S(1)}, bf16[640,384]{1,0:T(8,128)(2,1)S(1)}, f32[8,256]{1,0:T(8,128)S(1)}) custom-call(s32[1]{0:T(128)} %bitcast.1.tile_ref, s32[4,4]{1,0:T(4,128)S(4)} %get-tuple-element.23.near_ref, s32[4,4]{1,0:T(4,128)S(4)} %get-tuple-element.24.codes_ref, s32[1,2]{1,0:T(1,128)S(4)} %get-tuple-element.30.partner_ref), custom_call_target="tpu_custom_call" | custom-call | tf_op jit(solution)/shard_map/partner_map/pallas_call | solution.py:498
  12.8 1.3 %collective-permute-done.3.rest_1_ = bf16[160,128]{1,0:T(8,128)(2,1)S(1)} collective-permute-done((bf16[160,128]{1,0:T(8,128)(2,1)S(1)}, bf16[160,128]{1,0:T(8,128)(2,1)S(1)}, u32[]{:S(2)}, u32[]{:S(2)}) %collective-permute-start.3) | collective-permute-done | bytes 40992 | tf_op jit(solution)/shard_map/ppermute | solution.py:522
  14.2 0.4 %collective-permute-done.4.rest_2_ = bf16[160,128]{1,0:T(8,128)(2,1)S(1)} collective-permute-done((bf16[160,128]{1,0:T(8,128)(2,1)S(1)}, bf16[160,128]{1,0:T(8,128)(2,1)S(1)}, u32[]{:S(2)}, u32[]{:S(2)}) %collective-permute-start.4) | collective-permute-done | bytes 40992 | tf_op jit(solution)/shard_map/ppermute | solution.py:522
  14.6 0.2 %early.1 = (f32[64,128]{1,0:T(8,128)S(1)}, f32[64,256]{1,0:T(8,128)S(1)}) custom-call(bf16[64,128]{1,0:T(8,128)(2,1)S(1)} %get-tuple-element.29.height_ref, bf16[640,256]{1,0:T(8,128)(2,1)S(1)} %get-tuple-element.31.velocity_map_ref, bf16[640,384]{1,0:T(8,128)(2,1)S(1)} %get-tuple-element.32.rim_map_ref, f32[8,256]{1,0:T(8,128)S(1)} %get-tuple-element.33.chosen_ref, ...), custom_call_target="tpu_custom_call" | custom-call | tf_op jit(solution)/shard_map/early/pallas_call | solution.py:525
  14.8 0.3 %collective-permute-done.5.rest_0_ = bf16[160,128]{1,0:T(8,128)(2,1)S(1)} collective-permute-done((bf16[160,128]{1,0:T(8,128)(2,1)S(1)}, bf16[160,128]{1,0:T(8,128)(2,1)S(1)}, u32[]{:S(2)}, u32[]{:S(2)}) %collective-permute-start.5) | collective-permute-done | bytes 40992 | tf_op jit(solution)/shard_map/ppermute | solution.py:522
  15.1 0.0 collective-permute-done.6.rest_1_
  15.1 2.0 %density.1 = f32[4096,128]{1,0:T(8,128)} custom-call(f32[64,128]{1,0:T(8,128)S(1)} %get-tuple-element.37.height_ref, f32[64,256]{1,0:T(8,128)S(1)} %get-tuple-element.38.velocity_ref, bf16[640,256]{1,0:T(8,128)(2,1)S(1)} %get-tuple-element.31.velocity_map_ref, bf16[640,384]{1,0:T(8,128)(2,1)S(1)} %get-tuple-element.32.rim_map_ref, ...), custom_call_target="tpu_custom_call" | custom-call | tf_op jit(solution)/shard_map/density/pallas_call | solution.py:536
Async XLA Ops:
  1.5 4.8 %collective-permute-start = (bf16[80,128]{1,0:T(8,128)(2,1)S(1)}, bf16[80,128]{1,0:T(8,128)(2,1)S(1)}, u32[]{:S(2)}, u32[]{:S(2)}) collective-permute-start(bf16[80,128]{1,0:T(8,128)(2,1)S(1)} %get-tuple-element.26), channel_id=1, source_target_pairs={{0,2},{1,3},{2,0},{3,1},{4,6},{5,7},{6,4},{7,5},{8,10},{9,11},{10,... | collective-permute-start | bytes 61448 | tf_op jit(solution)/shard_map/ppermute | solution.py:476
  4.5 3.2 %collective-permute-start.1 = (bf16[80,128]{1,0:T(8,128)(2,1)S(1)}, bf16[80,128]{1,0:T(8,128)(2,1)S(1)}, u32[]{:S(2)}, u32[]{:S(2)}) collective-permute-start(bf16[80,128]{1,0:T(8,128)(2,1)S(1)} %get-tuple-element.27), channel_id=1, source_target_pairs={{0,3},{1,2},{2,1},{3,0},{4,7},{5,6},{6,5},{7,4},{8,11},{9,10},{10,... | collective-permute-start | bytes 61448 | tf_op jit(solution)/shard_map/ppermute | solution.py:476
  4.5 3.2 %collective-permute-start.2 = (bf16[80,128]{1,0:T(8,128)(2,1)S(1)}, bf16[80,128]{1,0:T(8,128)(2,1)S(1)}, u32[]{:S(2)}, u32[]{:S(2)}) collective-permute-start(bf16[80,128]{1,0:T(8,128)(2,1)S(1)} %get-tuple-element.28), channel_id=1, source_target_pairs={{0,1},{1,0},{2,3},{3,2},{4,5},{5,4},{6,7},{7,6},{8,9},{9,8},{10,11... | collective-permute-start | bytes 61448 | tf_op jit(solution)/shard_map/ppermute | solution.py:476
  8.0 6.2 %collective-permute-start.3 = (bf16[160,128]{1,0:T(8,128)(2,1)S(1)}, bf16[160,128]{1,0:T(8,128)(2,1)S(1)}, u32[]{:S(2)}, u32[]{:S(2)}) collective-permute-start(bf16[160,128]{1,0:T(8,128)(2,1)S(1)} %get-tuple-element.35), channel_id=1, source_target_pairs={{0,4},{1,5},{4,12},{5,13},{8,9},{9,8},{12,0},{13,1},{2,6},{3,7},{6... | collective-permute-start | bytes 122888 | tf_op jit(solution)/shard_map/ppermute | solution.py:522
  9.6 5.0 %collective-permute-start.4 = (bf16[160,128]{1,0:T(8,128)(2,1)S(1)}, bf16[160,128]{1,0:T(8,128)(2,1)S(1)}, u32[]{:S(2)}, u32[]{:S(2)}) collective-permute-start(bf16[160,128]{1,0:T(8,128)(2,1)S(1)} %get-tuple-element.36), channel_id=1, source_target_pairs={{0,8},{1,9},{4,5},{5,4},{8,0},{9,1},{12,13},{13,12},{2,10},{3,11},... | collective-permute-start | bytes 122888 | tf_op jit(solution)/shard_map/ppermute | solution.py:522
  10.7 4.5 %collective-permute-start.5 = (bf16[160,128]{1,0:T(8,128)(2,1)S(1)}, bf16[160,128]{1,0:T(8,128)(2,1)S(1)}, u32[]{:S(2)}, u32[]{:S(2)}) collective-permute-start(bf16[160,128]{1,0:T(8,128)(2,1)S(1)} %get-tuple-element.39), channel_id=1, source_target_pairs={{0,12},{1,13},{4,0},{5,1},{8,4},{9,5},{12,8},{13,9},{2,14},{3,15},... | collective-permute-start | bytes 122888 | tf_op jit(solution)/shard_map/ppermute | solution.py:522
  11.8 3.3 %collective-permute-start.6 = (bf16[160,128]{1,0:T(8,128)(2,1)S(1)}, bf16[160,128]{1,0:T(8,128)(2,1)S(1)}, u32[]{:S(2)}, u32[]{:S(2)}) collective-permute-start(bf16[160,128]{1,0:T(8,128)(2,1)S(1)} %get-tuple-element.40), channel_id=1, source_target_pairs={{0,1},{1,0},{4,8},{5,9},{8,12},{9,13},{12,4},{13,5},{2,3},{3,2},{6... | collective-permute-start | bytes 122888 | tf_op jit(solution)/shard_map/ppermute | solution.py:522

commit v10 on v9

--- a/solution.py
+++ b/solution.py
@@ -521,7 +521,7 @@
                 pairs.append((sender * field_count + core, there))
         bands.append(lax.ppermute(band, ("tiles", "field"), pairs))
 
-    early = arrivals - 2
+    early = arrivals - 3
     height, velocity = pl.pallas_call(
         early_kernel,
         out_shape=[kept((total, LANES), jnp.float32), kept((total, partners * LANES), jnp.float32)],

time: 17.3 us -> 17.3 us (level)
  no operation moved by 1% of the time
where the time goes in v10:
time: 17.3 us; the launch traced here: 17.1 us
  starting transfers between devices  7.3 us (42%)
  Pallas kernels  4.99 us (29%)
  waiting for transfers between devices  4.81 us (28%)
    ppermute x4, starting transfers between devices, shards(): bands.append(lax.ppermute(band, ('tiles', 'field'), pairs))  4.11 us
    ppermute x3, starting transfers between devices, shards(): lax.ppermute(piece, ('freq', 'field'), list(enumerate(route)))  3.2 us
    ppermute x3, waiting for transfers between devices, shards(): lax.ppermute(piece, ('freq', 'field'), list(enumerate(route)))  2.72 us
    ppermute x4, waiting for transfers between devices, shards(): bands.append(lax.ppermute(band, ('tiles', 'field'), pairs))  2.1 us
    pallas_call x1, Pallas kernels, shards(): pl.pallas_call(functools.partial(density_kernel, early, partners, scale,...  2 us
    pallas_call x1, Pallas kernels, shards(): pl.pallas_call(functools.partial(transform_kernel, band_routes), out_shap...  1.51 us
    pallas_call x1, Pallas kernels, shards(): pl.pallas_call(functools.partial(partner_map_kernel, tile_routes), out_sh...  0.77 us
  transfers between devices with their start and end apart: 7, of which 5 were waited for; matrix products, arithmetic and copies ran while one was open for 0% of the time, Pallas kernels for 7%

profile of v10, /device:TPU:0, one launch (start us, length us, event | category | flops | bytes accessed | tf_op | source)
XLA Modules:
  0.0 17.1 jit_solution(7142861320989203812)
XLA Ops:
  0.0 1.5 %transform.1 = (s32[4,4]{1,0:T(4,128)S(4)}, s32[4,4]{1,0:T(4,128)S(4)}, s32[1,2]{1,0:T(1,128)S(4)}, bf16[80,128]{1,0:T(8,128)(2,1)S(1)}, bf16[80,128]{1,0:T(8,12...) custom-call(s32[1]{0:T(128)} %bitcast.place_ref, s32[4]{0:T(128)} %ids_ref.1, s32[4,4]{1,0:T(4,128)} %near_ids_ref.1, ...), custom_call_target="tpu_custom_call" | custom-call | tf_op jit(solution)/shard_map/transform/pallas_call | solution.py:452
  1.5 3.0 %collective-permute-start = (bf16[80,128]{1,0:T(8,128)(2,1)S(1)}, bf16[80,128]{1,0:T(8,128)(2,1)S(1)}, u32[]{:S(2)}, u32[]{:S(2)}) collective-permute-start(bf16[80,128]{1,0:T(8,128)(2,1)S(1)} %get-tuple-element.26), channel_id=1, source_target_pairs={{0,2},{1,3},{2,0},{3,1},{4,6},{5,7},{6,4},{7,5},{8,10},{9,11},{10,... | collective-permute-start | bytes 61448 | tf_op jit(solution)/shard_map/ppermute | solution.py:476
  4.5 0.0 collective-permute-start.1
  4.5 0.2 %collective-permute-start.2 = (bf16[80,128]{1,0:T(8,128)(2,1)S(1)}, bf16[80,128]{1,0:T(8,128)(2,1)S(1)}, u32[]{:S(2)}, u32[]{:S(2)}) collective-permute-start(bf16[80,128]{1,0:T(8,128)(2,1)S(1)} %get-tuple-element.28), channel_id=1, source_target_pairs={{0,1},{1,0},{2,3},{3,2},{4,5},{5,4},{6,7},{7,6},{8,9},{9,8},{10,11... | collective-permute-start | bytes 61448 | tf_op jit(solution)/shard_map/ppermute | solution.py:476
  4.7 0.3 %rim_map.1.rim_map_ref = bf16[128,512]{1,0:T(8,128)(2,1)S(1)} custom-call(s32[1]{0:T(128)} %bitcast.1.tile_ref, s32[4,4]{1,0:T(4,128)S(4)} %get-tuple-element.23.near_ref, s32[4,4]{1,0:T(4,128)S(4)} %get-tuple-element.24.codes_ref), custom_call_target="tpu_custom_call" | custom-call | tf_op jit(solution)/shard_map/rim_map/pallas_call | solution.py:480
  5.0 1.3 %collective-permute-done.rest_1_ = bf16[80,128]{1,0:T(8,128)(2,1)S(1)} collective-permute-done((bf16[80,128]{1,0:T(8,128)(2,1)S(1)}, bf16[80,128]{1,0:T(8,128)(2,1)S(1)}, u32[]{:S(2)}, u32[]{:S(2)}) %collective-permute-start) | collective-permute-done | bytes 20512 | tf_op jit(solution)/shard_map/ppermute | solution.py:476
  6.3 1.4 %collective-permute-done.1.rest_2_ = bf16[80,128]{1,0:T(8,128)(2,1)S(1)} collective-permute-done((bf16[80,128]{1,0:T(8,128)(2,1)S(1)}, bf16[80,128]{1,0:T(8,128)(2,1)S(1)}, u32[]{:S(2)}, u32[]{:S(2)}) %collective-permute-start.1) | collective-permute-done | bytes 20512 | tf_op jit(solution)/shard_map/ppermute | solution.py:476
  7.7 0.0 collective-permute-done.2.rest_3_
  7.7 0.2 %collect.1 = (bf16[160,128]{1,0:T(8,128)(2,1)S(1)}, bf16[160,128]{1,0:T(8,128)(2,1)S(1)}, bf16[160,128]{1,0:T(8,128)(2,1)S(1)}, bf16[160,128]{1,0:T(8,128)(2,1)S...) custom-call(s32[1]{0:T(128)} %bitcast.place_ref, s32[1]{0:T(128)} %bitcast.1.tile_ref, ...), custom_call_target="tpu_custom_call" | custom-call | tf_op jit(solution)/shard_map/collect/pallas_call | solution.py:489
  8.0 1.6 %collective-permute-start.3 = (bf16[160,128]{1,0:T(8,128)(2,1)S(1)}, bf16[160,128]{1,0:T(8,128)(2,1)S(1)}, u32[]{:S(2)}, u32[]{:S(2)}) collective-permute-start(bf16[160,128]{1,0:T(8,128)(2,1)S(1)} %get-tuple-element.35), channel_id=1, source_target_pairs={{0,4},{1,5},{4,12},{5,13},{8,9},{9,8},{12,0},{13,1},{2,6},{3,7},{6... | collective-permute-start | bytes 122888 | tf_op jit(solution)/shard_map/ppermute | solution.py:522
  9.6 1.1 %collective-permute-start.4 = (bf16[160,128]{1,0:T(8,128)(2,1)S(1)}, bf16[160,128]{1,0:T(8,128)(2,1)S(1)}, u32[]{:S(2)}, u32[]{:S(2)}) collective-permute-start(bf16[160,128]{1,0:T(8,128)(2,1)S(1)} %get-tuple-element.38), channel_id=1, source_target_pairs={{0,8},{1,9},{4,5},{5,4},{8,0},{9,1},{12,13},{13,12},{2,10},{3,11},... | collective-permute-start | bytes 122888 | tf_op jit(solution)/shard_map/ppermute | solution.py:522
  10.7 1.2 %collective-permute-start.5 = (bf16[160,128]{1,0:T(8,128)(2,1)S(1)}, bf16[160,128]{1,0:T(8,128)(2,1)S(1)}, u32[]{:S(2)}, u32[]{:S(2)}) collective-permute-start(bf16[160,128]{1,0:T(8,128)(2,1)S(1)} %get-tuple-element.39), channel_id=1, source_target_pairs={{0,12},{1,13},{4,0},{5,1},{8,4},{9,5},{12,8},{13,9},{2,14},{3,15},... | collective-permute-start | bytes 122888 | tf_op jit(solution)/shard_map/ppermute | solution.py:522
  11.8 0.2 %collective-permute-start.6 = (bf16[160,128]{1,0:T(8,128)(2,1)S(1)}, bf16[160,128]{1,0:T(8,128)(2,1)S(1)}, u32[]{:S(2)}, u32[]{:S(2)}) collective-permute-start(bf16[160,128]{1,0:T(8,128)(2,1)S(1)} %get-tuple-element.40), channel_id=1, source_target_pairs={{0,1},{1,0},{4,8},{5,9},{8,12},{9,13},{12,4},{13,5},{2,3},{3,2},{6... | collective-permute-start | bytes 122888 | tf_op jit(solution)/shard_map/ppermute | solution.py:522
  12.1 0.8 %partner_map.1 = (bf16[640,256]{1,0:T(8,128)(2,1)S(1)}, bf16[640,384]{1,0:T(8,128)(2,1)S(1)}, f32[8,256]{1,0:T(8,128)S(1)}) custom-call(s32[1]{0:T(128)} %bitcast.1.tile_ref, s32[4,4]{1,0:T(4,128)S(4)} %get-tuple-element.23.near_ref, s32[4,4]{1,0:T(4,128)S(4)} %get-tuple-element.24.codes_ref, s32[1,2]{1,0:T(1,128)S(4)} %get-tuple-element.30.partner_ref), custom_call_target="tpu_custom_call" | custom-call | tf_op jit(solution)/shard_map/partner_map/pallas_call | solution.py:498
  12.8 1.3 %collective-permute-done.3.rest_1_ = bf16[160,128]{1,0:T(8,128)(2,1)S(1)} collective-permute-done((bf16[160,128]{1,0:T(8,128)(2,1)S(1)}, bf16[160,128]{1,0:T(8,128)(2,1)S(1)}, u32[]{:S(2)}, u32[]{:S(2)}) %collective-permute-start.3) | collective-permute-done | bytes 40992 | tf_op jit(solution)/shard_map/ppermute | solution.py:522
  14.2 0.2 %early.1 = (f32[64,128]{1,0:T(8,128)S(1)}, f32[64,256]{1,0:T(8,128)S(1)}) custom-call(bf16[64,128]{1,0:T(8,128)(2,1)S(1)} %get-tuple-element.29.height_ref, bf16[640,256]{1,0:T(8,128)(2,1)S(1)} %get-tuple-element.31.velocity_map_ref, bf16[640,384]{1,0:T(8,128)(2,1)S(1)} %get-tuple-element.32.rim_map_ref, f32[8,256]{1,0:T(8,128)S(1)} %get-tuple-element.33.chosen_ref, ...), custom_call_target="tpu_custom_call" | custom-call | tf_op jit(solution)/shard_map/early/pallas_call | solution.py:525
  14.4 0.2 %collective-permute-done.4.rest_0_ = bf16[160,128]{1,0:T(8,128)(2,1)S(1)} collective-permute-done((bf16[160,128]{1,0:T(8,128)(2,1)S(1)}, bf16[160,128]{1,0:T(8,128)(2,1)S(1)}, u32[]{:S(2)}, u32[]{:S(2)}) %collective-permute-start.4) | collective-permute-done | bytes 40992 | tf_op jit(solution)/shard_map/ppermute | solution.py:522
  14.6 0.5 %collective-permute-done.5.rest_1_ = bf16[160,128]{1,0:T(8,128)(2,1)S(1)} collective-permute-done((bf16[160,128]{1,0:T(8,128)(2,1)S(1)}, bf16[160,128]{1,0:T(8,128)(2,1)S(1)}, u32[]{:S(2)}, u32[]{:S(2)}) %collective-permute-start.5) | collective-permute-done | bytes 40992 | tf_op jit(solution)/shard_map/ppermute | solution.py:522
  15.1 0.0 collective-permute-done.6.rest_2_
  15.1 2.0 %density.1 = f32[4096,128]{1,0:T(8,128)} custom-call(f32[64,128]{1,0:T(8,128)S(1)} %get-tuple-element.36.height_ref, f32[64,256]{1,0:T(8,128)S(1)} %get-tuple-element.37.velocity_ref, bf16[640,256]{1,0:T(8,128)(2,1)S(1)} %get-tuple-element.31.velocity_map_ref, bf16[640,384]{1,0:T(8,128)(2,1)S(1)} %get-tuple-element.32.rim_map_ref, ...), custom_call_target="tpu_custom_call" | custom-call | tf_op jit(solution)/shard_map/density/pallas_call | solution.py:536
Async XLA Ops:
  1.5 4.8 %collective-permute-start = (bf16[80,128]{1,0:T(8,128)(2,1)S(1)}, bf16[80,128]{1,0:T(8,128)(2,1)S(1)}, u32[]{:S(2)}, u32[]{:S(2)}) collective-permute-start(bf16[80,128]{1,0:T(8,128)(2,1)S(1)} %get-tuple-element.26), channel_id=1, source_target_pairs={{0,2},{1,3},{2,0},{3,1},{4,6},{5,7},{6,4},{7,5},{8,10},{9,11},{10,... | collective-permute-start | bytes 61448 | tf_op jit(solution)/shard_map/ppermute | solution.py:476
  4.5 3.2 %collective-permute-start.1 = (bf16[80,128]{1,0:T(8,128)(2,1)S(1)}, bf16[80,128]{1,0:T(8,128)(2,1)S(1)}, u32[]{:S(2)}, u32[]{:S(2)}) collective-permute-start(bf16[80,128]{1,0:T(8,128)(2,1)S(1)} %get-tuple-element.27), channel_id=1, source_target_pairs={{0,3},{1,2},{2,1},{3,0},{4,7},{5,6},{6,5},{7,4},{8,11},{9,10},{10,... | collective-permute-start | bytes 61448 | tf_op jit(solution)/shard_map/ppermute | solution.py:476
  4.5 3.2 %collective-permute-start.2 = (bf16[80,128]{1,0:T(8,128)(2,1)S(1)}, bf16[80,128]{1,0:T(8,128)(2,1)S(1)}, u32[]{:S(2)}, u32[]{:S(2)}) collective-permute-start(bf16[80,128]{1,0:T(8,128)(2,1)S(1)} %get-tuple-element.28), channel_id=1, source_target_pairs={{0,1},{1,0},{2,3},{3,2},{4,5},{5,4},{6,7},{7,6},{8,9},{9,8},{10,11... | collective-permute-start | bytes 61448 | tf_op jit(solution)/shard_map/ppermute | solution.py:476
  8.0 6.2 %collective-permute-start.3 = (bf16[160,128]{1,0:T(8,128)(2,1)S(1)}, bf16[160,128]{1,0:T(8,128)(2,1)S(1)}, u32[]{:S(2)}, u32[]{:S(2)}) collective-permute-start(bf16[160,128]{1,0:T(8,128)(2,1)S(1)} %get-tuple-element.35), channel_id=1, source_target_pairs={{0,4},{1,5},{4,12},{5,13},{8,9},{9,8},{12,0},{13,1},{2,6},{3,7},{6... | collective-permute-start | bytes 122888 | tf_op jit(solution)/shard_map/ppermute | solution.py:522
  9.6 5.0 %collective-permute-start.4 = (bf16[160,128]{1,0:T(8,128)(2,1)S(1)}, bf16[160,128]{1,0:T(8,128)(2,1)S(1)}, u32[]{:S(2)}, u32[]{:S(2)}) collective-permute-start(bf16[160,128]{1,0:T(8,128)(2,1)S(1)} %get-tuple-element.38), channel_id=1, source_target_pairs={{0,8},{1,9},{4,5},{5,4},{8,0},{9,1},{12,13},{13,12},{2,10},{3,11},... | collective-permute-start | bytes 122888 | tf_op jit(solution)/shard_map/ppermute | solution.py:522
  10.7 4.5 %collective-permute-start.5 = (bf16[160,128]{1,0:T(8,128)(2,1)S(1)}, bf16[160,128]{1,0:T(8,128)(2,1)S(1)}, u32[]{:S(2)}, u32[]{:S(2)}) collective-permute-start(bf16[160,128]{1,0:T(8,128)(2,1)S(1)} %get-tuple-element.39), channel_id=1, source_target_pairs={{0,12},{1,13},{4,0},{5,1},{8,4},{9,5},{12,8},{13,9},{2,14},{3,15},... | collective-permute-start | bytes 122888 | tf_op jit(solution)/shard_map/ppermute | solution.py:522
  11.8 3.3 %collective-permute-start.6 = (bf16[160,128]{1,0:T(8,128)(2,1)S(1)}, bf16[160,128]{1,0:T(8,128)(2,1)S(1)}, u32[]{:S(2)}, u32[]{:S(2)}) collective-permute-start(bf16[160,128]{1,0:T(8,128)(2,1)S(1)} %get-tuple-element.40), channel_id=1, source_target_pairs={{0,1},{1,0},{4,8},{5,9},{8,12},{9,13},{12,4},{13,5},{2,3},{3,2},{6... | collective-permute-start | bytes 122888 | tf_op jit(solution)/shard_map/ppermute | solution.py:522

commit v11 on v9

--- a/solution.py
+++ b/solution.py
@@ -30,7 +30,7 @@
     ((NORTH, 0), (SOUTH, 0)),
 )
 
-BAND_ROUTES = ((2, 3, 0, 1), (3, 2, 1, 0), (1, 0, 3, 2))
+BAND_ROUTES = ((3, 2, 1, 0), (2, 3, 0, 1), (1, 0, 3, 2))
 TILE_ROUTES = ((1, 3, 2, 0), (2, 1, 0, 3), (3, 0, 1, 2), (0, 2, 3, 1))
 
 

time: 17.3 us -> 17.3 us (level)
  no operation moved by 1% of the time
where the time goes in v11:
time: 17.3 us; the launch traced here: 17.1 us
  starting transfers between devices  7.23 us (42%)
  Pallas kernels  4.98 us (29%)
  waiting for transfers between devices  4.89 us (28%)
    ppermute x4, starting transfers between devices, shards(): bands.append(lax.ppermute(band, ('tiles', 'field'), pairs))  4.11 us
    ppermute x3, starting transfers between devices, shards(): lax.ppermute(piece, ('freq', 'field'), list(enumerate(route)))  3.12 us
    ppermute x3, waiting for transfers between devices, shards(): lax.ppermute(piece, ('freq', 'field'), list(enumerate(route)))  2.81 us
    ppermute x4, waiting for transfers between devices, shards(): bands.append(lax.ppermute(band, ('tiles', 'field'), pairs))  2.08 us
    pallas_call x1, Pallas kernels, shards(): pl.pallas_call(functools.partial(density_kernel, early, partners, scale,...  1.98 us
    pallas_call x1, Pallas kernels, shards(): pl.pallas_call(functools.partial(transform_kernel, band_routes), out_shap...  1.51 us
    pallas_call x1, Pallas kernels, shards(): pl.pallas_call(functools.partial(partner_map_kernel, tile_routes), out_sh...  0.77 us
  transfers between devices with their start and end apart: 7, of which 5 were waited for; matrix products, arithmetic and copies ran while one was open for 0% of the time, Pallas kernels for 7%

profile of v11, /device:TPU:0, one launch (start us, length us, event | category | flops | bytes accessed | tf_op | source)
XLA Modules:
  0.0 17.1 jit_solution(8316801527467446478)
XLA Ops:
  0.0 1.5 %transform.1 = (s32[4,4]{1,0:T(4,128)S(4)}, s32[4,4]{1,0:T(4,128)S(4)}, s32[1,2]{1,0:T(1,128)S(4)}, bf16[80,128]{1,0:T(8,128)(2,1)S(1)}, bf16[80,128]{1,0:T(8,12...) custom-call(s32[1]{0:T(128)} %bitcast.place_ref, s32[4]{0:T(128)} %ids_ref.1, s32[4,4]{1,0:T(4,128)} %near_ids_ref.1, ...), custom_call_target="tpu_custom_call" | custom-call | tf_op jit(solution)/shard_map/transform/pallas_call | solution.py:452
  1.5 2.4 %collective-permute-start = (bf16[80,128]{1,0:T(8,128)(2,1)S(1)}, bf16[80,128]{1,0:T(8,128)(2,1)S(1)}, u32[]{:S(2)}, u32[]{:S(2)}) collective-permute-start(bf16[80,128]{1,0:T(8,128)(2,1)S(1)} %get-tuple-element.26), channel_id=1, source_target_pairs={{0,3},{1,2},{2,1},{3,0},{4,7},{5,6},{6,5},{7,4},{8,11},{9,10},{10,... | collective-permute-start | bytes 61448 | tf_op jit(solution)/shard_map/ppermute | solution.py:476
  4.0 0.6 %collective-permute-start.1 = (bf16[80,128]{1,0:T(8,128)(2,1)S(1)}, bf16[80,128]{1,0:T(8,128)(2,1)S(1)}, u32[]{:S(2)}, u32[]{:S(2)}) collective-permute-start(bf16[80,128]{1,0:T(8,128)(2,1)S(1)} %get-tuple-element.27), channel_id=1, source_target_pairs={{0,2},{1,3},{2,0},{3,1},{4,6},{5,7},{6,4},{7,5},{8,10},{9,11},{10,... | collective-permute-start | bytes 61448 | tf_op jit(solution)/shard_map/ppermute | solution.py:476
  4.6 0.0 collective-permute-start.2
  4.6 0.3 %rim_map.1.rim_map_ref = bf16[128,512]{1,0:T(8,128)(2,1)S(1)} custom-call(s32[1]{0:T(128)} %bitcast.1.tile_ref, s32[4,4]{1,0:T(4,128)S(4)} %get-tuple-element.23.near_ref, s32[4,4]{1,0:T(4,128)S(4)} %get-tuple-element.24.codes_ref), custom_call_target="tpu_custom_call" | custom-call | tf_op jit(solution)/shard_map/rim_map/pallas_call | solution.py:480
  4.9 0.5 %collective-permute-done.rest_1_ = bf16[80,128]{1,0:T(8,128)(2,1)S(1)} collective-permute-done((bf16[80,128]{1,0:T(8,128)(2,1)S(1)}, bf16[80,128]{1,0:T(8,128)(2,1)S(1)}, u32[]{:S(2)}, u32[]{:S(2)}) %collective-permute-start) | collective-permute-done | bytes 20512 | tf_op jit(solution)/shard_map/ppermute | solution.py:476
  5.5 2.3 %collective-permute-done.1.rest_2_ = bf16[80,128]{1,0:T(8,128)(2,1)S(1)} collective-permute-done((bf16[80,128]{1,0:T(8,128)(2,1)S(1)}, bf16[80,128]{1,0:T(8,128)(2,1)S(1)}, u32[]{:S(2)}, u32[]{:S(2)}) %collective-permute-start.1) | collective-permute-done | bytes 20512 | tf_op jit(solution)/shard_map/ppermute | solution.py:476
  7.7 0.0 collective-permute-done.2.rest_3_
  7.7 0.2 %collect.1 = (bf16[160,128]{1,0:T(8,128)(2,1)S(1)}, bf16[160,128]{1,0:T(8,128)(2,1)S(1)}, bf16[160,128]{1,0:T(8,128)(2,1)S(1)}, bf16[160,128]{1,0:T(8,128)(2,1)S...) custom-call(s32[1]{0:T(128)} %bitcast.place_ref, s32[1]{0:T(128)} %bitcast.1.tile_ref, ...), custom_call_target="tpu_custom_call" | custom-call | tf_op jit(solution)/shard_map/collect/pallas_call | solution.py:489
  8.0 1.6 %collective-permute-start.3 = (bf16[160,128]{1,0:T(8,128)(2,1)S(1)}, bf16[160,128]{1,0:T(8,128)(2,1)S(1)}, u32[]{:S(2)}, u32[]{:S(2)}) collective-permute-start(bf16[160,128]{1,0:T(8,128)(2,1)S(1)} %get-tuple-element.35), channel_id=1, source_target_pairs={{0,4},{1,5},{4,12},{5,13},{8,9},{9,8},{12,0},{13,1},{2,6},{3,7},{6... | collective-permute-start | bytes 122888 | tf_op jit(solution)/shard_map/ppermute | solution.py:522
  9.6 1.1 %collective-permute-start.4 = (bf16[160,128]{1,0:T(8,128)(2,1)S(1)}, bf16[160,128]{1,0:T(8,128)(2,1)S(1)}, u32[]{:S(2)}, u32[]{:S(2)}) collective-permute-start(bf16[160,128]{1,0:T(8,128)(2,1)S(1)} %get-tuple-element.36), channel_id=1, source_target_pairs={{0,8},{1,9},{4,5},{5,4},{8,0},{9,1},{12,13},{13,12},{2,10},{3,11},... | collective-permute-start | bytes 122888 | tf_op jit(solution)/shard_map/ppermute | solution.py:522
  10.7 1.2 %collective-permute-start.5 = (bf16[160,128]{1,0:T(8,128)(2,1)S(1)}, bf16[160,128]{1,0:T(8,128)(2,1)S(1)}, u32[]{:S(2)}, u32[]{:S(2)}) collective-permute-start(bf16[160,128]{1,0:T(8,128)(2,1)S(1)} %get-tuple-element.39), channel_id=1, source_target_pairs={{0,12},{1,13},{4,0},{5,1},{8,4},{9,5},{12,8},{13,9},{2,14},{3,15},... | collective-permute-start | bytes 122888 | tf_op jit(solution)/shard_map/ppermute | solution.py:522
  11.9 0.2 %collective-permute-start.6 = (bf16[160,128]{1,0:T(8,128)(2,1)S(1)}, bf16[160,128]{1,0:T(8,128)(2,1)S(1)}, u32[]{:S(2)}, u32[]{:S(2)}) collective-permute-start(bf16[160,128]{1,0:T(8,128)(2,1)S(1)} %get-tuple-element.40), channel_id=1, source_target_pairs={{0,1},{1,0},{4,8},{5,9},{8,12},{9,13},{12,4},{13,5},{2,3},{3,2},{6... | collective-permute-start | bytes 122888 | tf_op jit(solution)/shard_map/ppermute | solution.py:522
  12.1 0.8 %partner_map.1 = (bf16[640,256]{1,0:T(8,128)(2,1)S(1)}, bf16[640,384]{1,0:T(8,128)(2,1)S(1)}, f32[8,256]{1,0:T(8,128)S(1)}) custom-call(s32[1]{0:T(128)} %bitcast.1.tile_ref, s32[4,4]{1,0:T(4,128)S(4)} %get-tuple-element.23.near_ref, s32[4,4]{1,0:T(4,128)S(4)} %get-tuple-element.24.codes_ref, s32[1,2]{1,0:T(1,128)S(4)} %get-tuple-element.30.partner_ref), custom_call_target="tpu_custom_call" | custom-call | tf_op jit(solution)/shard_map/partner_map/pallas_call | solution.py:498
  12.9 1.4 %collective-permute-done.3.rest_1_ = bf16[160,128]{1,0:T(8,128)(2,1)S(1)} collective-permute-done((bf16[160,128]{1,0:T(8,128)(2,1)S(1)}, bf16[160,128]{1,0:T(8,128)(2,1)S(1)}, u32[]{:S(2)}, u32[]{:S(2)}) %collective-permute-start.3) | collective-permute-done | bytes 40992 | tf_op jit(solution)/shard_map/ppermute | solution.py:522
  14.2 0.4 %collective-permute-done.4.rest_2_ = bf16[160,128]{1,0:T(8,128)(2,1)S(1)} collective-permute-done((bf16[160,128]{1,0:T(8,128)(2,1)S(1)}, bf16[160,128]{1,0:T(8,128)(2,1)S(1)}, u32[]{:S(2)}, u32[]{:S(2)}) %collective-permute-start.4) | collective-permute-done | bytes 40992 | tf_op jit(solution)/shard_map/ppermute | solution.py:522
  14.6 0.2 %early.1 = (f32[64,128]{1,0:T(8,128)S(1)}, f32[64,256]{1,0:T(8,128)S(1)}) custom-call(bf16[64,128]{1,0:T(8,128)(2,1)S(1)} %get-tuple-element.29.height_ref, bf16[640,256]{1,0:T(8,128)(2,1)S(1)} %get-tuple-element.31.velocity_map_ref, bf16[640,384]{1,0:T(8,128)(2,1)S(1)} %get-tuple-element.32.rim_map_ref, f32[8,256]{1,0:T(8,128)S(1)} %get-tuple-element.33.chosen_ref, ...), custom_call_target="tpu_custom_call" | custom-call | tf_op jit(solution)/shard_map/early/pallas_call | solution.py:525
  14.9 0.3 %collective-permute-done.5.rest_0_ = bf16[160,128]{1,0:T(8,128)(2,1)S(1)} collective-permute-done((bf16[160,128]{1,0:T(8,128)(2,1)S(1)}, bf16[160,128]{1,0:T(8,128)(2,1)S(1)}, u32[]{:S(2)}, u32[]{:S(2)}) %collective-permute-start.5) | collective-permute-done | bytes 40992 | tf_op jit(solution)/shard_map/ppermute | solution.py:522
  15.2 0.0 collective-permute-done.6.rest_1_
  15.2 2.0 %density.1 = f32[4096,128]{1,0:T(8,128)} custom-call(f32[64,128]{1,0:T(8,128)S(1)} %get-tuple-element.37.height_ref, f32[64,256]{1,0:T(8,128)S(1)} %get-tuple-element.38.velocity_ref, bf16[640,256]{1,0:T(8,128)(2,1)S(1)} %get-tuple-element.31.velocity_map_ref, bf16[640,384]{1,0:T(8,128)(2,1)S(1)} %get-tuple-element.32.rim_map_ref, ...), custom_call_target="tpu_custom_call" | custom-call | tf_op jit(solution)/shard_map/density/pallas_call | solution.py:536
Async XLA Ops:
  1.5 4.0 %collective-permute-start = (bf16[80,128]{1,0:T(8,128)(2,1)S(1)}, bf16[80,128]{1,0:T(8,128)(2,1)S(1)}, u32[]{:S(2)}, u32[]{:S(2)}) collective-permute-start(bf16[80,128]{1,0:T(8,128)(2,1)S(1)} %get-tuple-element.26), channel_id=1, source_target_pairs={{0,3},{1,2},{2,1},{3,0},{4,7},{5,6},{6,5},{7,4},{8,11},{9,10},{10,... | collective-permute-start | bytes 61448 | tf_op jit(solution)/shard_map/ppermute | solution.py:476
  4.0 3.8 %collective-permute-start.1 = (bf16[80,128]{1,0:T(8,128)(2,1)S(1)}, bf16[80,128]{1,0:T(8,128)(2,1)S(1)}, u32[]{:S(2)}, u32[]{:S(2)}) collective-permute-start(bf16[80,128]{1,0:T(8,128)(2,1)S(1)} %get-tuple-element.27), channel_id=1, source_target_pairs={{0,2},{1,3},{2,0},{3,1},{4,6},{5,7},{6,4},{7,5},{8,10},{9,11},{10,... | collective-permute-start | bytes 61448 | tf_op jit(solution)/shard_map/ppermute | solution.py:476
  4.6 3.1 %collective-permute-start.2 = (bf16[80,128]{1,0:T(8,128)(2,1)S(1)}, bf16[80,128]{1,0:T(8,128)(2,1)S(1)}, u32[]{:S(2)}, u32[]{:S(2)}) collective-permute-start(bf16[80,128]{1,0:T(8,128)(2,1)S(1)} %get-tuple-element.28), channel_id=1, source_target_pairs={{0,1},{1,0},{2,3},{3,2},{4,5},{5,4},{6,7},{7,6},{8,9},{9,8},{10,11... | collective-permute-start | bytes 61448 | tf_op jit(solution)/shard_map/ppermute | solution.py:476
  8.0 6.3 %collective-permute-start.3 = (bf16[160,128]{1,0:T(8,128)(2,1)S(1)}, bf16[160,128]{1,0:T(8,128)(2,1)S(1)}, u32[]{:S(2)}, u32[]{:S(2)}) collective-permute-start(bf16[160,128]{1,0:T(8,128)(2,1)S(1)} %get-tuple-element.35), channel_id=1, source_target_pairs={{0,4},{1,5},{4,12},{5,13},{8,9},{9,8},{12,0},{13,1},{2,6},{3,7},{6... | collective-permute-start | bytes 122888 | tf_op jit(solution)/shard_map/ppermute | solution.py:522
  9.6 5.0 %collective-permute-start.4 = (bf16[160,128]{1,0:T(8,128)(2,1)S(1)}, bf16[160,128]{1,0:T(8,128)(2,1)S(1)}, u32[]{:S(2)}, u32[]{:S(2)}) collective-permute-start(bf16[160,128]{1,0:T(8,128)(2,1)S(1)} %get-tuple-element.36), channel_id=1, source_target_pairs={{0,8},{1,9},{4,5},{5,4},{8,0},{9,1},{12,13},{13,12},{2,10},{3,11},... | collective-permute-start | bytes 122888 | tf_op jit(solution)/shard_map/ppermute | solution.py:522
  10.7 4.5 %collective-permute-start.5 = (bf16[160,128]{1,0:T(8,128)(2,1)S(1)}, bf16[160,128]{1,0:T(8,128)(2,1)S(1)}, u32[]{:S(2)}, u32[]{:S(2)}) collective-permute-start(bf16[160,128]{1,0:T(8,128)(2,1)S(1)} %get-tuple-element.39), channel_id=1, source_target_pairs={{0,12},{1,13},{4,0},{5,1},{8,4},{9,5},{12,8},{13,9},{2,14},{3,15},... | collective-permute-start | bytes 122888 | tf_op jit(solution)/shard_map/ppermute | solution.py:522
  11.9 3.3 %collective-permute-start.6 = (bf16[160,128]{1,0:T(8,128)(2,1)S(1)}, bf16[160,128]{1,0:T(8,128)(2,1)S(1)}, u32[]{:S(2)}, u32[]{:S(2)}) collective-permute-start(bf16[160,128]{1,0:T(8,128)(2,1)S(1)} %get-tuple-element.40), channel_id=1, source_target_pairs={{0,1},{1,0},{4,8},{5,9},{8,12},{9,13},{12,4},{13,5},{2,3},{3,2},{6... | collective-permute-start | bytes 122888 | tf_op jit(solution)/shard_map/ppermute | solution.py:522
